TPU v7x, 1024 devices: a whole 4x8x16 slice. The times are simulated.
1024 devices in a mesh: section: 4 (over z_hi), expert: 64 (over x, y, core), dp: 4 (over z_lo).
Axes of the slice: x: 4, y: 8, z: 16 (z_hi: 4, z_lo: 4; z = z_hi * 4 + z_lo), core: 2. Of those that a mesh axis runs over, the one named last changes fastest.
Arguments:
- fwd_act: bfloat16 [4, 1024, 7168], P('section', 'expert', 'dp'), may hold values from -6 to 6
- fwd_routes: int32 [4, 1024, 8], P('section', 'expert'), may hold values from 0 to 63, all different within a row; in each aligned block of 16 rows (0 to 15, 16 to 31, ..., all dimensions but the last counted through in order) at most 4 rows name the same one
- fwd_probs: float32 [4, 1024, 8], P('section', 'expert'), may hold values from 0.02 to 0.5
- bwd_grad: bfloat16 [4, 1024, 7168], P('section', 'expert', 'dp'), may hold values from -6 to 6
- bwd_routes: int32 [4, 1024, 8], P('section', 'expert'), may hold values from 0 to 63, all different within a row; in each aligned block of 16 rows (0 to 15, 16 to 31, ..., all dimensions but the last counted through in order) at most 4 rows name the same one
- bwd_probs: float32 [4, 1024, 8], P('section', 'expert'), may hold values from 0.02 to 0.5
- w_up: bfloat16 [64, 7168, 1024], P('expert', 'dp'), may hold values from -0.0625 to 0.0625
- w_down: bfloat16 [64, 1024, 7168], P('expert', None, 'dp'), may hold values from -0.1875 to 0.1875
- act_stash: bfloat16 [4, 64, 256, 1024], P('section', 'expert'), may hold values from -6 to 6
Outputs:
- fwd_out: bfloat16 [4, 1024, 7168], P('section', 'expert', 'dp')
- bwd_out: bfloat16 [4, 1024, 7168], P('section', 'expert', 'dp')
Inputs may be any that keep to these rules, and one draw needn't show every extreme that they name: `fwd_routes`: each row names 8 different experts. Among the 16 rows of one expert group of one section no expert is named more than 4 times, a bound that some block reaches. `bwd_routes`: each row names 8 different experts. Among the 16 rows of one expert group of one section no expert is named more than 4 times, a bound that some block reaches.
All inputs are finite; a program needn't handle non-finite values.
Results may differ from a plain program's by a relative error of at most 0.0064.
Values may be sent and summed in bfloat16 or wider, within the bound.
No kernel may reach another device: no remote copies, remote signals or barrier semaphores. Data moves between devices by JAX's collectives and lax.ppermute only.
A program may use at most 32 MiB of HBM per device.

v0:
```python
import jax
import jax.numpy as jnp
from jax import lax
from jax.sharding import PartitionSpec as P


def passed_along(block, axis, distance):
    devices = range(lax.axis_size(axis))
    route = [((i - distance) % len(devices), i) for i in devices]
    return lax.ppermute(block, axis, route)


def slot_table(route_rows, experts, capacity):
    flat_routes = route_rows.reshape(-1)
    matches = (flat_routes[:, None] == jnp.arange(experts, dtype=jnp.int32)[None, :]).astype(
        jnp.int32
    )
    before = jnp.cumsum(matches, axis=0) - matches
    slot_rank = jnp.sum(before * matches, axis=1)
    targets = flat_routes * capacity + slot_rank
    slot_ids = jnp.arange(experts * capacity, dtype=jnp.int32)
    return (targets[None, :] == slot_ids[:, None]).astype(jnp.bfloat16)


def silu_slope(pre_act):
    squash = jax.nn.sigmoid(pre_act)
    return squash * (1.0 + pre_act * (1.0 - squash))


def contract_last(left_rows, right_matrix):
    return lax.dot_general(
        left_rows, right_matrix, (((1,), (1,)), ((), ())), preferred_element_type=jnp.float32
    )


def shards(
    fwd_act, fwd_routes, fwd_probs, bwd_grad, bwd_routes, bwd_probs, w_up, w_down, act_stash
):
    experts = lax.axis_size("expert")
    capacity = act_stash.shape[2] // experts
    top_count = fwd_routes.shape[2]
    arriving = passed_along(fwd_act[0], "section", 1)
    incoming = passed_along(bwd_grad[0], "section", -1)
    tokens_here = arriving.shape[0]
    width_part = arriving.shape[1]
    table_fwd = slot_table(fwd_routes[0], experts, capacity)
    table_bwd = slot_table(bwd_routes[0], experts, capacity)
    rows_fwd = jnp.repeat(arriving, top_count, axis=0)
    weighted = (bwd_probs[0][:, :, None] * incoming[:, None, :].astype(jnp.float32)).astype(
        jnp.bfloat16
    )
    weighted = weighted.reshape(tokens_here * top_count, width_part)
    sent_fwd = jnp.dot(table_fwd, rows_fwd, preferred_element_type=jnp.float32).astype(jnp.bfloat16)
    sent_bwd = jnp.dot(table_bwd, weighted, preferred_element_type=jnp.float32).astype(jnp.bfloat16)
    sent_fwd = sent_fwd.reshape(experts, capacity, width_part)
    sent_bwd = sent_bwd.reshape(experts, capacity, width_part)
    recv_fwd, recv_bwd = (
        lax.all_to_all(sent_fwd, "expert", split_axis=0, concat_axis=0, tiled=True),
        lax.all_to_all(sent_bwd, "expert", split_axis=0, concat_axis=0, tiled=True),
    )
    recv_fwd = recv_fwd.reshape(experts * capacity, width_part)
    recv_bwd = recv_bwd.reshape(experts * capacity, width_part)
    up_weight = w_up[0]
    down_weight = w_down[0]
    pre_part = jnp.dot(recv_fwd, up_weight, preferred_element_type=jnp.float32)
    back_part = contract_last(recv_bwd, down_weight)
    stash_rows = act_stash[0, 0]
    pre_full, back_full = lax.psum((pre_part, back_part), "dp")
    hidden_fwd = jax.nn.silu(pre_full).astype(jnp.bfloat16)
    grad_pre = (back_full * silu_slope(stash_rows.astype(jnp.float32))).astype(jnp.bfloat16)
    out_rows = jnp.dot(hidden_fwd, down_weight, preferred_element_type=jnp.float32).astype(
        jnp.bfloat16
    )
    grad_rows = contract_last(grad_pre, up_weight).astype(jnp.bfloat16)
    out_rows = out_rows.reshape(experts, capacity, width_part)
    grad_rows = grad_rows.reshape(experts, capacity, width_part)
    back_fwd, back_bwd = (
        lax.all_to_all(out_rows, "expert", split_axis=0, concat_axis=0, tiled=True),
        lax.all_to_all(grad_rows, "expert", split_axis=0, concat_axis=0, tiled=True),
    )
    back_fwd = back_fwd.reshape(experts * capacity, width_part)
    back_bwd = back_bwd.reshape(experts * capacity, width_part)
    picked_fwd = lax.dot_general(
        table_fwd, back_fwd, (((0,), (0,)), ((), ())), preferred_element_type=jnp.float32
    )
    picked_bwd = lax.dot_general(
        table_bwd, back_bwd, (((0,), (0,)), ((), ())), preferred_element_type=jnp.float32
    )
    picked_fwd = picked_fwd.reshape(tokens_here, top_count, width_part)
    picked_bwd = picked_bwd.reshape(tokens_here, top_count, width_part)
    fwd_out = jnp.sum(fwd_probs[0][:, :, None] * picked_fwd, axis=1).astype(jnp.bfloat16)
    bwd_out = jnp.sum(picked_bwd, axis=1).astype(jnp.bfloat16)
    return (fwd_out[None], bwd_out[None])


def solution(mesh):
    return jax.shard_map(
        shards,
        mesh=mesh,
        in_specs=(
            P("section", "expert", "dp"),
            P("section", "expert", None),
            P("section", "expert", None),
            P("section", "expert", "dp"),
            P("section", "expert", None),
            P("section", "expert", None),
            P("expert", "dp", None),
            P("expert", None, "dp"),
            P("section", "expert", None, None),
        ),
        out_specs=(P("section", "expert", "dp"), P("section", "expert", "dp")),
        check_vma=False,
    )
```

profile of v0, /device:TPU:1, one launch (start us, length us, event | category | flops | bytes accessed | tf_op | source)
XLA Modules:
  0.0 295.0 jit_solution(11684028134820433701)
XLA Ops:
  7.2 18.9 %collective-permute-start.1 = (bf16[16,1792]{1,0:T(8,128)(2,1)}, bf16[16,1792]{1,0:T(8,128)(2,1)S(1)}, u32[]{:S(2)}, u32[]{:S(2)}) collective-permute-start(bf16[16,1792]{1,0:T(8,128)(2,1)} %bitcast.53), channel_id=1, source_target_pairs={{256,0},{512,256},{768,512},{0,768},{257,1},{513,257},{769,513},{1... | collective-permute-start | bytes 172040 | tf_op jit(solution)/shard_map/ppermute | solution.py:10
  26.1 0.8 copy.23
  26.8 0.1 reshape_squeeze.7
  26.9 0.1 fusion.38
  27.0 0.2 reduce_window_sum.18
  27.2 0.2 select_reduce_fusion
  27.4 0.8 copy.26
  28.1 0.1 mul.85
  28.2 0.5 convolution_convert_fusion
  28.7 1.2 reshape.124
  29.9 14.4 %all-to-all-start.2 = ((bf16[64,4,1792]{2,1,0:T(4,128)(2,1)}), bf16[64,4,1792]{2,1,0:T(4,128)(2,1)S(1)}, u32[]{:S(2)}, u32[]{:S(2)}) async-start(bf16[64,4,1792]{2,1,0:T(4,128)(2,1)} %reshape.124), calls=%async_computation.2 | async-start | bytes 1835008 | tf_op jit(solution)/shard_map/all_to_all | solution.py:59
  44.3 3.9 %collective-permute-start = (bf16[16,1792]{1,0:T(8,128)(2,1)S(1)}, bf16[16,1792]{1,0:T(8,128)(2,1)S(1)}, u32[]{:S(2)}, u32[]{:S(2)}) collective-permute-start(bf16[16,1792]{1,0:T(8,128)(2,1)S(1)} %bitcast.54), channel_id=1, source_target_pairs={{768,0},{0,256},{256,512},{512,768},{769,1},{1,257},{257,513},{513... | collective-permute-start | bytes 172040 | tf_op jit(solution)/shard_map/ppermute | solution.py:10
  48.2 0.1 copy.20
  48.3 0.1 reshape_squeeze.6
  48.4 0.1 fusion.41
  48.5 0.2 reduce_window_sum.17
  48.7 0.2 select_reduce_fusion.1
  48.9 5.2 %collective-permute-done = bf16[16,1792]{1,0:T(8,128)(2,1)S(1)} collective-permute-done((bf16[16,1792]{1,0:T(8,128)(2,1)S(1)}, bf16[16,1792]{1,0:T(8,128)(2,1)S(1)}, u32[]{:S(2)}, u32[]{:S(2)}) %collective-permute-start) | collective-permute-done | bytes 57376 | tf_op jit(solution)/shard_map/ppermute | solution.py:10
  54.0 0.4 convolution_convert_fusion.1
  54.4 1.1 reshape.120
  55.6 14.5 %all-to-all-done.2 = bf16[64,4,1792]{2,1,0:T(4,128)(2,1)S(1)} async-done(((bf16[64,4,1792]{2,1,0:T(4,128)(2,1)}), bf16[64,4,1792]{2,1,0:T(4,128)(2,1)S(1)}, u32[]{:S(2)}, u32[]{:S(2)}) %all-to-all-start.2) | async-done | bytes 917536 | tf_op jit(solution)/shard_map/all_to_all | solution.py:59
  70.0 6.2 %all-to-all-start = ((bf16[64,4,1792]{2,1,0:T(4,128)(2,1)}), bf16[64,4,1792]{2,1,0:T(4,128)(2,1)S(1)}, u32[]{:S(2)}, u32[]{:S(2)}) async-start(bf16[64,4,1792]{2,1,0:T(4,128)(2,1)} %reshape.120), calls=%async_computation | async-start | bytes 1835008 | tf_op jit(solution)/shard_map/all_to_all | solution.py:58
  76.3 0.0 all-reduce.3.cloned.1.call-start
  76.3 0.2 reshape.125
  76.5 4.2 %fusion = f32[256,1024]{1,0:T(8,128)} fusion(bf16[256,1792]{1,0:T(8,128)(2,1)S(1)} %reshape.125, bf16[1,1024,1792]{2,1,0:T(8,128)(2,1)} %param.16), kind=kOutput, calls=%fused_computation | convolution fusion | flops 939524096 | bytes 5636096 | tf_op jit(solution)/shard_map/dot_general | solution.py:31
  80.7 21.3 %all-to-all-done = bf16[64,4,1792]{2,1,0:T(4,128)(2,1)S(1)} async-done(((bf16[64,4,1792]{2,1,0:T(4,128)(2,1)}), bf16[64,4,1792]{2,1,0:T(4,128)(2,1)S(1)}, u32[]{:S(2)}, u32[]{:S(2)}) %all-to-all-start) | async-done | bytes 917536 | tf_op jit(solution)/shard_map/all_to_all | solution.py:58
  102.0 0.2 reshape.121
  102.2 4.2 %fusion.6 = f32[256,1024]{1,0:T(8,128)} fusion(bf16[256,1792]{1,0:T(8,128)(2,1)S(1)} %reshape.121, bf16[1,1792,1024]{2,1,0:T(8,128)(2,1)} %param.15), kind=kOutput, calls=%fused_computation.6 | convolution fusion | flops 939524096 | bytes 5636096 | tf_op jit(solution)/shard_map/dot_general | solution.py:65
  106.5 107.0 %all-reduce.3.cloned.1.call-done = (f32[256,1024]{1,0:T(8,128)}, f32[256,1024]{1,0:T(8,128)}) async-done(((f32[256,1024]{1,0:T(8,128)}, f32[256,1024]{1,0:T(8,128)}), (f32[256,1024]{1,0:T(8,128)}, f32[256,1024]{1,0:T(8,128)})) %all-reduce.3.cloned.1.call-update) | async-done | bytes 2097168 | tf_op jit(solution)/shard_map/psum | solution.py:68
  213.5 3.8 %fusion.8 = bf16[256,1792]{1,0:T(8,128)(2,1)S(1)} fusion(bf16[1,1792,1024]{2,1,0:T(8,128)(2,1)} %param.15, f32[256,1024]{1,0:T(8,128)} %get-tuple-element.3, bf16[1,1,256,1024]{3,2,1,0:T(8,128)(2,1)S(1)} %copy-done.4), kind=kOutput, calls=%fused_computation.10 | convolution fusion | flops 942604288 | bytes 6160384 | tf_op jit(solution)/shard_map/dot_general | solution.py:31
  217.3 1.2 reshape.126
  218.5 10.6 %all-to-all-start.3 = ((bf16[64,4,1792]{2,1,0:T(4,128)(2,1)}), bf16[64,4,1792]{2,1,0:T(4,128)(2,1)S(1)}, u32[]{:S(2)}, u32[]{:S(2)}) async-start(bf16[64,4,1792]{2,1,0:T(4,128)(2,1)} %reshape.126), calls=%async_computation.3 | async-start | bytes 1835008 | tf_op jit(solution)/shard_map/all_to_all | solution.py:79
  229.2 3.3 %fusion.11 = bf16[256,1792]{1,0:T(8,128)(2,1)S(1)} fusion(bf16[1,1024,1792]{2,1,0:T(8,128)(2,1)} %param.16, f32[256,1024]{1,0:T(8,128)S(1)} %copy-done.3), kind=kOutput, calls=%fused_computation.11 | convolution fusion | flops 941293568 | bytes 5636096 | tf_op jit(solution)/shard_map/dot_general | solution.py:71
  232.5 1.1 reshape.122
  233.6 21.3 %all-to-all-done.3 = bf16[64,4,1792]{2,1,0:T(4,128)(2,1)S(1)} async-done(((bf16[64,4,1792]{2,1,0:T(4,128)(2,1)}), bf16[64,4,1792]{2,1,0:T(4,128)(2,1)S(1)}, u32[]{:S(2)}, u32[]{:S(2)}) %all-to-all-start.3) | async-done | bytes 917536 | tf_op jit(solution)/shard_map/all_to_all | solution.py:79
  254.9 6.2 %all-to-all-start.1 = ((bf16[64,4,1792]{2,1,0:T(4,128)(2,1)}), bf16[64,4,1792]{2,1,0:T(4,128)(2,1)S(1)}, u32[]{:S(2)}, u32[]{:S(2)}) async-start(bf16[64,4,1792]{2,1,0:T(4,128)(2,1)} %reshape.122), calls=%async_computation.1 | async-start | bytes 1835008 | tf_op jit(solution)/shard_map/all_to_all | solution.py:78
  261.1 0.1 reduce_sum.44
  261.2 0.1 reduce_sum.41
  261.3 0.1 copy.24
  261.4 0.1 copy.25
  261.4 0.1 copy.21
  261.5 0.1 copy.22
  261.6 0.1 copy.19
  261.7 0.2 reshape.130
  261.9 1.1 convolution_reduce_fusion
  263.0 23.9 %all-to-all-done.1 = bf16[64,4,1792]{2,1,0:T(4,128)(2,1)S(1)} async-done(((bf16[64,4,1792]{2,1,0:T(4,128)(2,1)}), bf16[64,4,1792]{2,1,0:T(4,128)(2,1)S(1)}, u32[]{:S(2)}, u32[]{:S(2)}) %all-to-all-start.1) | async-done | bytes 917536 | tf_op jit(solution)/shard_map/all_to_all | solution.py:78
  286.9 0.2 reshape.129
  287.1 1.1 fusion.14
  (19 shorter events, 0.1 us)
Async XLA Ops:
  7.2 37.1 %copy-start.5 = (bf16[1,16,1792]{2,1,0:T(8,128)(2,1)S(1)}, bf16[1,16,1792]{2,1,0:T(8,128)(2,1)}, u32[]{:S(2)}) copy-start(bf16[1,16,1792]{2,1,0:T(8,128)(2,1)} %param.9) | copy-start | bytes 172036
  7.2 41.0 %copy-start.1 = (s32[1,16,8]{1,2,0:T(8,128)S(1)}, s32[1,16,8]{1,2,0:T(8,128)}, u32[]{:S(2)}) copy-start(s32[1,16,8]{1,2,0:T(8,128)} %param.10) | copy-start | bytes 1540
  7.2 21.0 %collective-permute-start.1 = (bf16[16,1792]{1,0:T(8,128)(2,1)}, bf16[16,1792]{1,0:T(8,128)(2,1)S(1)}, u32[]{:S(2)}, u32[]{:S(2)}) collective-permute-start(bf16[16,1792]{1,0:T(8,128)(2,1)} %bitcast.53), channel_id=1, source_target_pairs={{256,0},{512,256},{768,512},{0,768},{257,1},{513,257},{769,513},{1... | collective-permute-start | bytes 172040 | tf_op jit(solution)/shard_map/ppermute | solution.py:10
  29.9 40.1 %all-to-all-start.2 = ((bf16[64,4,1792]{2,1,0:T(4,128)(2,1)}), bf16[64,4,1792]{2,1,0:T(4,128)(2,1)S(1)}, u32[]{:S(2)}, u32[]{:S(2)}) async-start(bf16[64,4,1792]{2,1,0:T(4,128)(2,1)} %reshape.124), calls=%async_computation.2 | async-start | bytes 1835008 | tf_op jit(solution)/shard_map/all_to_all | solution.py:59
  44.3 9.7 %collective-permute-start = (bf16[16,1792]{1,0:T(8,128)(2,1)S(1)}, bf16[16,1792]{1,0:T(8,128)(2,1)S(1)}, u32[]{:S(2)}, u32[]{:S(2)}) collective-permute-start(bf16[16,1792]{1,0:T(8,128)(2,1)S(1)} %bitcast.54), channel_id=1, source_target_pairs={{768,0},{0,256},{256,512},{512,768},{769,1},{1,257},{257,513},{513... | collective-permute-start | bytes 172040 | tf_op jit(solution)/shard_map/ppermute | solution.py:10
  70.0 32.0 %all-to-all-start = ((bf16[64,4,1792]{2,1,0:T(4,128)(2,1)}), bf16[64,4,1792]{2,1,0:T(4,128)(2,1)S(1)}, u32[]{:S(2)}, u32[]{:S(2)}) async-start(bf16[64,4,1792]{2,1,0:T(4,128)(2,1)} %reshape.120), calls=%async_computation | async-start | bytes 1835008 | tf_op jit(solution)/shard_map/all_to_all | solution.py:58
  76.3 137.3 %all-reduce.3.cloned.1.call-start = ((), (), s32[]{:S(2)}) async-start(), calls=%async_computation.4 | async-start | bytes 4194304 | tf_op jit(solution)/shard_map/psum | solution.py:68
  102.2 111.3 %copy-start.4 = (bf16[1,1,256,1024]{3,2,1,0:T(8,128)(2,1)S(1)}, bf16[1,1,256,1024]{3,2,1,0:T(8,128)(2,1)}, u32[]{:S(2)}) copy-start(bf16[1,1,256,1024]{3,2,1,0:T(8,128)(2,1)} %param.17) | copy-start | bytes 1572868
  217.3 11.8 %copy-start.3 = (f32[256,1024]{1,0:T(8,128)S(1)}, f32[256,1024]{1,0:T(8,128)}, u32[]{:S(2)}) copy-start(f32[256,1024]{1,0:T(8,128)} %get-tuple-element.2) | copy-start | bytes 3145732
  218.5 36.4 %all-to-all-start.3 = ((bf16[64,4,1792]{2,1,0:T(4,128)(2,1)}), bf16[64,4,1792]{2,1,0:T(4,128)(2,1)S(1)}, u32[]{:S(2)}, u32[]{:S(2)}) async-start(bf16[64,4,1792]{2,1,0:T(4,128)(2,1)} %reshape.126), calls=%async_computation.3 | async-start | bytes 1835008 | tf_op jit(solution)/shard_map/all_to_all | solution.py:79
  232.5 28.9 %copy-start = (s32[1,16,8]{1,2,0:T(8,128)S(1)}, s32[1,16,8]{1,2,0:T(8,128)}, u32[]{:S(2)}) copy-start(s32[1,16,8]{1,2,0:T(8,128)} %param.13) | copy-start | bytes 1540
  232.5 29.1 %copy-start.2 = (f32[1,16,8]{1,2,0:T(8,128)S(1)}, f32[1,16,8]{1,2,0:T(8,128)}, u32[]{:S(2)}) copy-start(f32[1,16,8]{1,2,0:T(8,128)} %param.11) | copy-start | bytes 1540
  254.9 32.0 %all-to-all-start.1 = ((bf16[64,4,1792]{2,1,0:T(4,128)(2,1)}), bf16[64,4,1792]{2,1,0:T(4,128)(2,1)S(1)}, u32[]{:S(2)}, u32[]{:S(2)}) async-start(bf16[64,4,1792]{2,1,0:T(4,128)(2,1)} %reshape.122), calls=%async_computation.1 | async-start | bytes 1835008 | tf_op jit(solution)/shard_map/all_to_all | solution.py:78
Sparse Core Ops, SparseCore 0:
  106.6 106.8 all-reduce.2
where the time goes:
time: 296 us; the launch traced here: 295 us
  waiting for transfers between devices  193 us (65%)
  starting transfers between devices  60.3 us (20%)
  matrix products  18.5 us (6%)
  between operations  14.3 us (5%)
  local copies, waits for them, and re-layouts  7.89 us (3%)
    psum x1, waiting for transfers between devices, shards(): pre_full, back_full = lax.psum((pre_part, back_part), 'dp')  107 us
    all_to_all x1, waiting for transfers between devices, shards(): lax.all_to_all(out_rows, 'expert', split_axis=0, concat_axis=0, tiled=True)  23.9 us
    ppermute x2, starting transfers between devices, passed_along(): return lax.ppermute(block, axis, route)  22.8 us
    all_to_all x1, waiting for transfers between devices, shards(): lax.all_to_all(sent_fwd, 'expert', split_axis=0, concat_axis=0, tiled=True)  21.3 us
    all_to_all x1, waiting for transfers between devices, shards(): lax.all_to_all(grad_rows, 'expert', split_axis=0, concat_axis=0, tiled=True)  21.3 us
    all_to_all x1, waiting for transfers between devices, shards(): lax.all_to_all(sent_bwd, 'expert', split_axis=0, concat_axis=0, tiled=True)  14.5 us
    all_to_all x1, starting transfers between devices, shards(): lax.all_to_all(sent_bwd, 'expert', split_axis=0, concat_axis=0, tiled=True)  14.4 us
    all_to_all x1, starting transfers between devices, shards(): lax.all_to_all(grad_rows, 'expert', split_axis=0, concat_axis=0, tiled=True)  10.6 us
  transfers between devices with their start and end apart: 7, of which 6 were waited for; matrix products, arithmetic and copies ran while one was open for 5% of the time, Pallas kernels for 0%

commit v1 on v0

--- a/solution.py
+++ b/solution.py
@@ -33,6 +33,32 @@
     )
 
 
+def matmul(left_rows, right_matrix):
+    return jnp.dot(left_rows, right_matrix, preferred_element_type=jnp.float32)
+
+
+def turned_parts(array, dim):
+    parts = lax.axis_size("dp")
+    own = lax.axis_index("dp")
+    size = array.shape[dim] // parts
+    return [
+        lax.dynamic_slice_in_dim(array, lax.rem(own + j, parts) * size, size, axis=dim)
+        for j in range(parts)
+    ]
+
+
+def summed_own(partials):
+    total = partials[0]
+    for j in range(1, len(partials)):
+        total = total + passed_along(partials[j].astype(jnp.bfloat16), "dp", j).astype(jnp.float32)
+    return total
+
+
+def spread_own(block):
+    others = [passed_along(block, "dp", -j) for j in range(1, lax.axis_size("dp"))]
+    return jnp.concatenate([block] + others, axis=1)
+
+
 def shards(
     fwd_act, fwd_routes, fwd_probs, bwd_grad, bwd_routes, bwd_probs, w_up, w_down, act_stash
 ):
@@ -60,18 +86,16 @@
     )
     recv_fwd = recv_fwd.reshape(experts * capacity, width_part)
     recv_bwd = recv_bwd.reshape(experts * capacity, width_part)
-    up_weight = w_up[0]
-    down_weight = w_down[0]
-    pre_part = jnp.dot(recv_fwd, up_weight, preferred_element_type=jnp.float32)
-    back_part = contract_last(recv_bwd, down_weight)
-    stash_rows = act_stash[0, 0]
-    pre_full, back_full = lax.psum((pre_part, back_part), "dp")
-    hidden_fwd = jax.nn.silu(pre_full).astype(jnp.bfloat16)
-    grad_pre = (back_full * silu_slope(stash_rows.astype(jnp.float32))).astype(jnp.bfloat16)
-    out_rows = jnp.dot(hidden_fwd, down_weight, preferred_element_type=jnp.float32).astype(
-        jnp.bfloat16
-    )
-    grad_rows = contract_last(grad_pre, up_weight).astype(jnp.bfloat16)
+    up_parts = turned_parts(w_up[0], 1)
+    down_parts = turned_parts(w_down[0], 0)
+    stash_own = turned_parts(act_stash[0, 0], 1)[0]
+    slope_own = silu_slope(stash_own.astype(jnp.float32))
+    pre_own = summed_own([matmul(recv_fwd, part) for part in up_parts])
+    hidden_fwd = spread_own(jax.nn.silu(pre_own).astype(jnp.bfloat16))
+    out_rows = matmul(hidden_fwd, jnp.concatenate(down_parts, axis=0)).astype(jnp.bfloat16)
+    back_own = summed_own([contract_last(recv_bwd, part) for part in down_parts])
+    grad_pre = spread_own((back_own * slope_own).astype(jnp.bfloat16))
+    grad_rows = contract_last(grad_pre, jnp.concatenate(up_parts, axis=1)).astype(jnp.bfloat16)
     out_rows = out_rows.reshape(experts, capacity, width_part)
     grad_rows = grad_rows.reshape(experts, capacity, width_part)
     back_fwd, back_bwd = (

time: 296 us -> 209 us (0.71)
  waiting for transfers between devices: 193 us -> 74.6 us
  starting transfers between devices: 60.3 us -> 97.7 us
  between operations: 14.3 us -> 1.18 us
  local copies, waits for them, and re-layouts: 7.89 us -> 15.2 us
    psum x1 -> x0, waiting for transfers between devices: 107 us -> none  [shards(): pre_full, back_full = lax.psum((pre_part, back_part), 'dp')]
    ppermute x2 -> x14, starting transfers between devices: 22.8 us -> 56.1 us  [passed_along(): return lax.ppermute(block, axis, route)]
    ppermute x2 -> x14, waiting for transfers between devices: 5.18 us -> 36.2 us  [passed_along(): return lax.ppermute(block, axis, route)]
    all_to_all x1, waiting for transfers between devices: 21.3 us -> 0.01 us  [shards(): lax.all_to_all(sent_fwd, 'expert', split_axis=0, concat_axis=0, tiled=True)]
    all_to_all x1, waiting for transfers between devices: 21.3 us -> 0.01 us  [shards(): lax.all_to_all(grad_rows, 'expert', split_axis=0, concat_axis=0, tiled=True)]
    dynamic_slice x0 -> x3, local copies, waits for them, and re-layouts: none -> 5.72 us  [turned_parts(): lax.dynamic_slice_in_dim(array, lax.rem(own + j, parts) * size, size, axi...]
    all_to_all x1, starting transfers between devices: 6.22 us -> 10.5 us  [shards(): lax.all_to_all(out_rows, 'expert', split_axis=0, concat_axis=0, tiled=True)]
    dot_general x2 -> x5, matrix products: 8.01 us -> 11.4 us  [contract_last(): lax.dot_general(left_rows, right_matrix, (((1,), (1,)), ((), ())), prefer...]
  transfers between devices with their start and end apart: 7 -> 18, of which waited for: 6 -> 9; matrix products, arithmetic and copies ran while one was open for 5% -> 12% of each run, Pallas kernels for 0% -> 0%
where the time goes in v1:
time: 209 us; the launch traced here: 208 us
  starting transfers between devices  97.7 us (47%)
  waiting for transfers between devices  74.6 us (36%)
  matrix products  18.9 us (9%)
  local copies, waits for them, and re-layouts  15.2 us (7%)
    ppermute x14, starting transfers between devices, passed_along(): return lax.ppermute(block, axis, route)  56.1 us
    ppermute x14, waiting for transfers between devices, passed_along(): return lax.ppermute(block, axis, route)  36.2 us
    all_to_all x1, waiting for transfers between devices, shards(): lax.all_to_all(out_rows, 'expert', split_axis=0, concat_axis=0, tiled=True)  23.9 us
    all_to_all x1, waiting for transfers between devices, shards(): lax.all_to_all(sent_bwd, 'expert', split_axis=0, concat_axis=0, tiled=True)  14.5 us
    all_to_all x1, starting transfers between devices, shards(): lax.all_to_all(sent_bwd, 'expert', split_axis=0, concat_axis=0, tiled=True)  14.4 us
    dot_general x5, matrix products, contract_last(): lax.dot_general(left_rows, right_matrix, (((1,), (1,)), ((), ())), prefer...  11.4 us
    all_to_all x1, starting transfers between devices, shards(): lax.all_to_all(out_rows, 'expert', split_axis=0, concat_axis=0, tiled=True)  10.5 us
    all_to_all x1, starting transfers between devices, shards(): lax.all_to_all(grad_rows, 'expert', split_axis=0, concat_axis=0, tiled=True)  10.5 us
  transfers between devices with their start and end apart: 18, of which 9 were waited for; matrix products, arithmetic and copies ran while one was open for 12% of the time, Pallas kernels for 0%

profile of v1, /device:TPU:1, one launch (start us, length us, event | category | flops | bytes accessed | tf_op | source)
XLA Modules:
  0.0 208.4 jit_solution(16733653651092163783)
XLA Ops:
  0.7 18.9 %collective-permute-start.7 = (bf16[16,1792]{1,0:T(8,128)(2,1)}, bf16[16,1792]{1,0:T(8,128)(2,1)S(1)}, u32[]{:S(2)}, u32[]{:S(2)}) collective-permute-start(bf16[16,1792]{1,0:T(8,128)(2,1)} %bitcast.66), channel_id=1, source_target_pairs={{256,0},{512,256},{768,512},{0,768},{257,1},{513,257},{769,513},{1... | collective-permute-start | bytes 172040 | tf_op jit(solution)/shard_map/ppermute | solution.py:10
  19.5 0.8 copy.33
  20.9 0.8 copy.36
  21.7 0.5 convolution_convert_fusion
  22.2 1.2 reshape.133
  23.4 14.4 %all-to-all-start.2 = ((bf16[64,4,1792]{2,1,0:T(4,128)(2,1)}), bf16[64,4,1792]{2,1,0:T(4,128)(2,1)S(1)}, u32[]{:S(2)}, u32[]{:S(2)}) async-start(bf16[64,4,1792]{2,1,0:T(4,128)(2,1)} %reshape.133), calls=%async_computation.2 | async-start | bytes 1835008 | tf_op jit(solution)/shard_map/all_to_all | solution.py:85
  37.8 3.9 %collective-permute-start = (bf16[16,1792]{1,0:T(8,128)(2,1)S(1)}, bf16[16,1792]{1,0:T(8,128)(2,1)S(1)}, u32[]{:S(2)}, u32[]{:S(2)}) collective-permute-start(bf16[16,1792]{1,0:T(8,128)(2,1)S(1)} %bitcast.67), channel_id=1, source_target_pairs={{768,0},{0,256},{256,512},{512,768},{769,1},{1,257},{257,513},{513... | collective-permute-start | bytes 172040 | tf_op jit(solution)/shard_map/ppermute | solution.py:10
  42.3 5.2 %collective-permute-done = bf16[16,1792]{1,0:T(8,128)(2,1)S(1)} collective-permute-done((bf16[16,1792]{1,0:T(8,128)(2,1)S(1)}, bf16[16,1792]{1,0:T(8,128)(2,1)S(1)}, u32[]{:S(2)}, u32[]{:S(2)}) %collective-permute-start) | collective-permute-done | bytes 57376 | tf_op jit(solution)/shard_map/ppermute | solution.py:10
  47.5 0.4 convolution_convert_fusion.1
  47.9 1.1 reshape.129
  49.0 14.5 %all-to-all-done.2 = bf16[64,4,1792]{2,1,0:T(4,128)(2,1)S(1)} async-done(((bf16[64,4,1792]{2,1,0:T(4,128)(2,1)}), bf16[64,4,1792]{2,1,0:T(4,128)(2,1)S(1)}, u32[]{:S(2)}, u32[]{:S(2)}) %all-to-all-start.2) | async-done | bytes 917536 | tf_op jit(solution)/shard_map/all_to_all | solution.py:85
  63.5 6.2 %all-to-all-start = ((bf16[64,4,1792]{2,1,0:T(4,128)(2,1)}), bf16[64,4,1792]{2,1,0:T(4,128)(2,1)S(1)}, u32[]{:S(2)}, u32[]{:S(2)}) async-start(bf16[64,4,1792]{2,1,0:T(4,128)(2,1)} %reshape.129), calls=%async_computation | async-start | bytes 1835008 | tf_op jit(solution)/shard_map/all_to_all | solution.py:84
  69.7 3.9 %dynamic-slice_bitcast_fusion.3 = (bf16[256,1792]{1,0:T(8,128)(2,1)}, bf16[256,1792]{1,0:T(8,128)(2,1)}, bf16[256,1792]{1,0:T(8,128)(2,1)}, bf16[256,1792]{1,0:T(8,128)(2,1)}) fusion(bf16[1,1024,1792]{2,1,0:T(8,128)(2,1)} %param.16, s32[]{:T(128)S(6)} %select_n.8, s32[]{:T(128)S(6)} %select_n.18, s32[]{:T(128)S(6)} %select_n.20, s32[]{:T(128)S(6)} %select_n.19), kind=kLoop, calls=%fused_computation.34 | loop fusion | bytes 7340048 | tf_op jit(solution)/shard_map/dynamic_slice | solution.py:45
  73.9 2.4 %convolution_convert_fusion.2 = bf16[256,256]{0,1:T(8,128)(2,1)} fusion(bf16[256,1792]{1,0:T(8,128)(2,1)S(1)} %reshape.134, bf16[256,1792]{1,0:T(8,128)(2,1)} %get-tuple-element.8), kind=kOutput, calls=%fused_computation.23 | convolution fusion | flops 234946560 | bytes 1966080 | tf_op jit(solution)/shard_map/dot_general | solution.py:31
  76.3 1.9 collective-permute-start.10
  78.2 2.3 %convolution_convert_fusion.4 = bf16[256,256]{0,1:T(8,128)(2,1)} fusion(bf16[256,1792]{1,0:T(8,128)(2,1)S(1)} %reshape.134, bf16[256,1792]{1,0:T(8,128)(2,1)} %get-tuple-element.7), kind=kOutput, calls=%fused_computation.25 | convolution fusion | flops 234946560 | bytes 1966080 | tf_op jit(solution)/shard_map/dot_general | solution.py:31
  80.5 3.4 %collective-permute-start.8 = (bf16[256,256]{0,1:T(8,128)(2,1)}, bf16[256,256]{0,1:T(8,128)(2,1)}, u32[]{:S(2)}, u32[]{:S(2)}) collective-permute-start(bf16[256,256]{0,1:T(8,128)(2,1)} %convolution_convert_fusion.4), channel_id=1, source_target_pairs={{3,0},{0,1},{1,2},{2,3},{7,4},{4,5},{5,6},{6,7},{11,8},{8,9},{9,10... | collective-permute-start | bytes 393224 | tf_op jit(solution)/shard_map/ppermute | solution.py:10
  83.9 1.1 convolution_convert_fusion.3
  85.0 1.9 collective-permute-start.9
  87.1 2.0 collective-permute-done.8
  89.1 6.9 %collective-permute-done.9 = bf16[256,256]{0,1:T(8,128)(2,1)} collective-permute-done((bf16[256,256]{0,1:T(8,128)(2,1)}, bf16[256,256]{0,1:T(8,128)(2,1)}, u32[]{:S(2)}, u32[]{:S(2)}) %collective-permute-start.9) | collective-permute-done | bytes 131104 | tf_op jit(solution)/shard_map/ppermute | solution.py:10
  96.1 1.5 fusion.48
  97.6 3.1 %collective-permute-start.11 = (bf16[256,256]{0,1:T(8,128)(2,1)S(1)}, bf16[256,256]{0,1:T(8,128)(2,1)S(1)}, u32[]{:S(2)}, u32[]{:S(2)}) collective-permute-start(bf16[256,256]{0,1:T(8,128)(2,1)S(1)} %fusion.48), channel_id=1, source_target_pairs={{1,0},{2,1},{3,2},{0,3},{5,4},{6,5},{7,6},{4,7},{9,8},{10,9},{11,1... | collective-permute-start | bytes 393224 | tf_op jit(solution)/shard_map/ppermute | solution.py:10
  100.7 1.9 collective-permute-start.12
  102.6 2.2 %collective-permute-start.13 = (bf16[256,256]{0,1:T(8,128)(2,1)S(1)}, bf16[256,256]{0,1:T(8,128)(2,1)}, u32[]{:S(2)}, u32[]{:S(2)}) collective-permute-start(bf16[256,256]{0,1:T(8,128)(2,1)S(1)} %fusion.48), channel_id=1, source_target_pairs={{3,0},{0,1},{1,2},{2,3},{7,4},{4,5},{5,6},{6,7},{11,8},{8,9},{9,10... | collective-permute-start | bytes 393224 | tf_op jit(solution)/shard_map/ppermute | solution.py:10
  104.8 1.8 dynamic-slice_bitcast_fusion.6
  106.8 7.8 %collective-permute-done.12 = bf16[256,256]{0,1:T(8,128)(2,1)} collective-permute-done((bf16[256,256]{0,1:T(8,128)(2,1)S(1)}, bf16[256,256]{0,1:T(8,128)(2,1)}, u32[]{:S(2)}, u32[]{:S(2)}) %collective-permute-start.12) | collective-permute-done | bytes 131104 | tf_op jit(solution)/shard_map/ppermute | solution.py:10
  114.6 4.1 %fusion.16 = bf16[256,1792]{1,0:T(8,128)(2,1)} fusion(bf16[1792,256]{1,0:T(8,128)(2,1)S(1)} %get-tuple-element.4, bf16[1792,256]{1,0:T(8,128)(2,1)} %get-tuple-element.5, bf16[1792,256]{1,0:T(8,128)(2,1)} %get-tuple-element.2, bf16[1792,256]{1,0:T(8,128)(2,1)} %get-tuple-element.3, bf16[256,256]{0,1:T(8,128)(2,1)} %collective-permute-done.13, ...), kind=kOutput, calls=%fused_computation.16 | convolution fusion | flops 956760064 | bytes 5111808 | tf_op jit(solution)/shard_map/dot_general | solution.py:31
  118.7 2.6 %reshape.135 = bf16[64,4,1792]{2,1,0:T(4,128)(2,1)} reshape(bf16[256,1792]{1,0:T(8,128)(2,1)} %fusion.16) | data formatting | bytes 1835008 | tf_op jit(solution)/shard_map/reshape | solution.py:100
  121.3 10.5 %all-to-all-start.3 = ((bf16[64,4,1792]{2,1,0:T(4,128)(2,1)}), bf16[64,4,1792]{2,1,0:T(4,128)(2,1)S(1)}, u32[]{:S(2)}, u32[]{:S(2)}) async-start(bf16[64,4,1792]{2,1,0:T(4,128)(2,1)} %reshape.135), calls=%async_computation.3 | async-start | bytes 1835008 | tf_op jit(solution)/shard_map/all_to_all | solution.py:103
  131.8 0.5 convolution_convert_fusion.7
  132.3 1.8 convolution_convert_fusion.6
  134.2 0.5 convolution_convert_fusion.5
  134.7 1.9 collective-permute-start.1
  136.6 2.8 %collective-permute-start.2 = (bf16[256,256]{0,1:T(8,128)(2,1)S(1)}, bf16[256,256]{0,1:T(8,128)(2,1)S(1)}, u32[]{:S(2)}, u32[]{:S(2)}) collective-permute-start(bf16[256,256]{0,1:T(8,128)(2,1)S(1)} %convolution_convert_fusion.6), channel_id=1, source_target_pairs={{2,0},{3,1},{0,2},{1,3},{6,4},{7,5},{4,6},{5,7},{10,8},{11,9},{8,1... | collective-permute-start | bytes 393224 | tf_op jit(solution)/shard_map/ppermute | solution.py:10
  139.4 4.4 %collective-permute-start.3 = (bf16[256,256]{0,1:T(8,128)(2,1)S(1)}, bf16[256,256]{0,1:T(8,128)(2,1)S(1)}, u32[]{:S(2)}, u32[]{:S(2)}) collective-permute-start(bf16[256,256]{0,1:T(8,128)(2,1)S(1)} %convolution_convert_fusion.5), channel_id=1, source_target_pairs={{1,0},{2,1},{3,2},{0,3},{5,4},{6,5},{7,6},{4,7},{9,8},{10,9},{11,1... | collective-permute-start | bytes 393224 | tf_op jit(solution)/shard_map/ppermute | solution.py:10
  143.9 5.5 %collective-permute-done.2 = bf16[256,256]{0,1:T(8,128)(2,1)S(1)} collective-permute-done((bf16[256,256]{0,1:T(8,128)(2,1)S(1)}, bf16[256,256]{0,1:T(8,128)(2,1)S(1)}, u32[]{:S(2)}, u32[]{:S(2)}) %collective-permute-start.2) | collective-permute-done | bytes 131104 | tf_op jit(solution)/shard_map/ppermute | solution.py:10
  149.7 0.5 multiply_convert_fusion
  150.2 4.5 %collective-permute-start.4 = (bf16[256,256]{0,1:T(8,128)(2,1)S(1)}, bf16[256,256]{0,1:T(8,128)(2,1)S(1)}, u32[]{:S(2)}, u32[]{:S(2)}) collective-permute-start(bf16[256,256]{0,1:T(8,128)(2,1)S(1)} %multiply_convert_fusion), channel_id=1, source_target_pairs={{1,0},{2,1},{3,2},{0,3},{5,4},{6,5},{7,6},{4,7},{9,8},{10,9},{11,1... | collective-permute-start | bytes 393224 | tf_op jit(solution)/shard_map/ppermute | solution.py:10
  154.7 3.4 %collective-permute-start.5 = (bf16[256,256]{0,1:T(8,128)(2,1)S(1)}, bf16[256,256]{0,1:T(8,128)(2,1)S(1)}, u32[]{:S(2)}, u32[]{:S(2)}) collective-permute-start(bf16[256,256]{0,1:T(8,128)(2,1)S(1)} %multiply_convert_fusion), channel_id=1, source_target_pairs={{2,0},{3,1},{0,2},{1,3},{6,4},{7,5},{4,6},{5,7},{10,8},{11,9},{8,1... | collective-permute-start | bytes 393224 | tf_op jit(solution)/shard_map/ppermute | solution.py:10
  158.1 1.9 collective-permute-start.6
  160.0 8.5 %collective-permute-done.5 = bf16[256,256]{0,1:T(8,128)(2,1)S(1)} collective-permute-done((bf16[256,256]{0,1:T(8,128)(2,1)S(1)}, bf16[256,256]{0,1:T(8,128)(2,1)S(1)}, u32[]{:S(2)}, u32[]{:S(2)}) %collective-permute-start.5) | collective-permute-done | bytes 131104 | tf_op jit(solution)/shard_map/ppermute | solution.py:10
  168.5 1.1 fusion.19
  169.7 1.2 reshape.131
  170.9 10.5 %all-to-all-start.1 = ((bf16[64,4,1792]{2,1,0:T(4,128)(2,1)}), bf16[64,4,1792]{2,1,0:T(4,128)(2,1)S(1)}, u32[]{:S(2)}, u32[]{:S(2)}) async-start(bf16[64,4,1792]{2,1,0:T(4,128)(2,1)} %reshape.131), calls=%async_computation.1 | async-start | bytes 1835008 | tf_op jit(solution)/shard_map/all_to_all | solution.py:102
  182.1 1.1 convolution_reduce_fusion
  183.2 23.9 %all-to-all-done.1 = bf16[64,4,1792]{2,1,0:T(4,128)(2,1)S(1)} async-done(((bf16[64,4,1792]{2,1,0:T(4,128)(2,1)}), bf16[64,4,1792]{2,1,0:T(4,128)(2,1)S(1)}, u32[]{:S(2)}, u32[]{:S(2)}) %all-to-all-start.1) | async-done | bytes 917536 | tf_op jit(solution)/shard_map/all_to_all | solution.py:102
  207.3 1.1 fusion.22
  (70 shorter events, 3.1 us)
Async XLA Ops:
  0.6 86.3 %copy-start = (bf16[1,1,256,1024]{3,2,1,0:T(8,128)(2,1)S(1)}, bf16[1,1,256,1024]{3,2,1,0:T(8,128)(2,1)}, u32[]{:S(2)}) copy-start(bf16[1,1,256,1024]{3,2,1,0:T(8,128)(2,1)} %param.17) | copy-start | bytes 1572868
  0.6 37.1 %copy-start.15 = (bf16[1,16,1792]{2,1,0:T(8,128)(2,1)S(1)}, bf16[1,16,1792]{2,1,0:T(8,128)(2,1)}, u32[]{:S(2)}) copy-start(bf16[1,16,1792]{2,1,0:T(8,128)(2,1)} %param.9) | copy-start | bytes 172036
  0.7 41.0 %copy-start.13 = (s32[1,16,8]{1,2,0:T(8,128)S(1)}, s32[1,16,8]{1,2,0:T(8,128)}, u32[]{:S(2)}) copy-start(s32[1,16,8]{1,2,0:T(8,128)} %param.10) | copy-start | bytes 1540
  0.7 21.0 %collective-permute-start.7 = (bf16[16,1792]{1,0:T(8,128)(2,1)}, bf16[16,1792]{1,0:T(8,128)(2,1)S(1)}, u32[]{:S(2)}, u32[]{:S(2)}) collective-permute-start(bf16[16,1792]{1,0:T(8,128)(2,1)} %bitcast.66), channel_id=1, source_target_pairs={{256,0},{512,256},{768,512},{0,768},{257,1},{513,257},{769,513},{1... | collective-permute-start | bytes 172040 | tf_op jit(solution)/shard_map/ppermute | solution.py:10
  23.4 40.1 %all-to-all-start.2 = ((bf16[64,4,1792]{2,1,0:T(4,128)(2,1)}), bf16[64,4,1792]{2,1,0:T(4,128)(2,1)S(1)}, u32[]{:S(2)}, u32[]{:S(2)}) async-start(bf16[64,4,1792]{2,1,0:T(4,128)(2,1)} %reshape.133), calls=%async_computation.2 | async-start | bytes 1835008 | tf_op jit(solution)/shard_map/all_to_all | solution.py:85
  37.8 9.7 %collective-permute-start = (bf16[16,1792]{1,0:T(8,128)(2,1)S(1)}, bf16[16,1792]{1,0:T(8,128)(2,1)S(1)}, u32[]{:S(2)}, u32[]{:S(2)}) collective-permute-start(bf16[16,1792]{1,0:T(8,128)(2,1)S(1)} %bitcast.67), channel_id=1, source_target_pairs={{768,0},{0,256},{256,512},{512,768},{769,1},{1,257},{257,513},{513... | collective-permute-start | bytes 172040 | tf_op jit(solution)/shard_map/ppermute | solution.py:10
  63.5 43.1 %all-to-all-start = ((bf16[64,4,1792]{2,1,0:T(4,128)(2,1)}), bf16[64,4,1792]{2,1,0:T(4,128)(2,1)S(1)}, u32[]{:S(2)}, u32[]{:S(2)}) async-start(bf16[64,4,1792]{2,1,0:T(4,128)(2,1)} %reshape.129), calls=%async_computation | async-start | bytes 1835008 | tf_op jit(solution)/shard_map/all_to_all | solution.py:84
  73.9 10.0 %copy-start.4 = (bf16[256,1792]{1,0:T(8,128)(2,1)S(1)}, bf16[256,1792]{1,0:T(8,128)(2,1)}, u32[]{:S(2)}) copy-start(bf16[256,1792]{1,0:T(8,128)(2,1)} %get-tuple-element.9) | copy-start | bytes 2752516
  73.9 22.2 %copy-start.9 = (bf16[256,1792]{1,0:T(8,128)(2,1)S(1)}, bf16[256,1792]{1,0:T(8,128)(2,1)}, u32[]{:S(2)}) copy-start(bf16[256,1792]{1,0:T(8,128)(2,1)} %get-tuple-element.6) | copy-start | bytes 2752516
  76.3 10.8 %collective-permute-start.10 = (bf16[256,256]{0,1:T(8,128)(2,1)}, bf16[256,256]{0,1:T(8,128)(2,1)}, u32[]{:S(2)}, u32[]{:S(2)}) collective-permute-start(bf16[256,256]{0,1:T(8,128)(2,1)} %convolution_convert_fusion.2), channel_id=1, source_target_pairs={{1,0},{2,1},{3,2},{0,3},{5,4},{6,5},{7,6},{4,7},{9,8},{10,9},{11,1... | collective-permute-start | bytes 393224 | tf_op jit(solution)/shard_map/ppermute | solution.py:10
  80.5 8.6 %collective-permute-start.8 = (bf16[256,256]{0,1:T(8,128)(2,1)}, bf16[256,256]{0,1:T(8,128)(2,1)}, u32[]{:S(2)}, u32[]{:S(2)}) collective-permute-start(bf16[256,256]{0,1:T(8,128)(2,1)} %convolution_convert_fusion.4), channel_id=1, source_target_pairs={{3,0},{0,1},{1,2},{2,3},{7,4},{4,5},{5,6},{6,7},{11,8},{8,9},{9,10... | collective-permute-start | bytes 393224 | tf_op jit(solution)/shard_map/ppermute | solution.py:10
  85.0 11.1 %collective-permute-start.9 = (bf16[256,256]{0,1:T(8,128)(2,1)}, bf16[256,256]{0,1:T(8,128)(2,1)}, u32[]{:S(2)}, u32[]{:S(2)}) collective-permute-start(bf16[256,256]{0,1:T(8,128)(2,1)} %convolution_convert_fusion.3), channel_id=1, source_target_pairs={{2,0},{3,1},{0,2},{1,3},{6,4},{7,5},{4,6},{5,7},{10,8},{11,9},{8,1... | collective-permute-start | bytes 393224 | tf_op jit(solution)/shard_map/ppermute | solution.py:10
  87.1 17.8 %copy-start.1 = (bf16[1,1792,1024]{2,1,0:T(8,128)(2,1)S(1)}, bf16[1,1792,1024]{2,1,0:T(8,128)(2,1)}, u32[]{:S(2)}) copy-start(bf16[1,1792,1024]{2,1,0:T(8,128)(2,1)} %param.15) | copy-start | bytes 11010052
  97.6 9.2 %collective-permute-start.11 = (bf16[256,256]{0,1:T(8,128)(2,1)S(1)}, bf16[256,256]{0,1:T(8,128)(2,1)S(1)}, u32[]{:S(2)}, u32[]{:S(2)}) collective-permute-start(bf16[256,256]{0,1:T(8,128)(2,1)S(1)} %fusion.48), channel_id=1, source_target_pairs={{1,0},{2,1},{3,2},{0,3},{5,4},{6,5},{7,6},{4,7},{9,8},{10,9},{11,1... | collective-permute-start | bytes 393224 | tf_op jit(solution)/shard_map/ppermute | solution.py:10
  100.7 13.9 %collective-permute-start.12 = (bf16[256,256]{0,1:T(8,128)(2,1)S(1)}, bf16[256,256]{0,1:T(8,128)(2,1)}, u32[]{:S(2)}, u32[]{:S(2)}) collective-permute-start(bf16[256,256]{0,1:T(8,128)(2,1)S(1)} %fusion.48), channel_id=1, source_target_pairs={{2,0},{3,1},{0,2},{1,3},{6,4},{7,5},{4,6},{5,7},{10,8},{11,9},{8,1... | collective-permute-start | bytes 393224 | tf_op jit(solution)/shard_map/ppermute | solution.py:10
  102.6 12.0 %collective-permute-start.13 = (bf16[256,256]{0,1:T(8,128)(2,1)S(1)}, bf16[256,256]{0,1:T(8,128)(2,1)}, u32[]{:S(2)}, u32[]{:S(2)}) collective-permute-start(bf16[256,256]{0,1:T(8,128)(2,1)S(1)} %fusion.48), channel_id=1, source_target_pairs={{3,0},{0,1},{1,2},{2,3},{7,4},{4,5},{5,6},{6,7},{11,8},{8,9},{9,10... | collective-permute-start | bytes 393224 | tf_op jit(solution)/shard_map/ppermute | solution.py:10
  106.6 12.1 %copy-start.6 = (bf16[1792,256]{1,0:T(8,128)(2,1)}, bf16[1792,256]{1,0:T(8,128)(2,1)S(1)}, u32[]{:S(2)}) copy-start(bf16[1792,256]{1,0:T(8,128)(2,1)S(1)} %get-tuple-element.4) | copy-start | bytes 2752516
  118.7 13.1 %copy-start.8 = (bf16[1792,256]{1,0:T(8,128)(2,1)S(1)}, bf16[1792,256]{1,0:T(8,128)(2,1)}, u32[]{:S(2)}) copy-start(bf16[1792,256]{1,0:T(8,128)(2,1)} %get-tuple-element.2) | copy-start | bytes 2752516
  121.3 49.6 %all-to-all-start.3 = ((bf16[64,4,1792]{2,1,0:T(4,128)(2,1)}), bf16[64,4,1792]{2,1,0:T(4,128)(2,1)S(1)}, u32[]{:S(2)}, u32[]{:S(2)}) async-start(bf16[64,4,1792]{2,1,0:T(4,128)(2,1)} %reshape.135), calls=%async_computation.3 | async-start | bytes 1835008 | tf_op jit(solution)/shard_map/all_to_all | solution.py:103
  131.8 2.4 %copy-start.7 = (bf16[1792,256]{1,0:T(8,128)(2,1)S(1)}, bf16[1792,256]{1,0:T(8,128)(2,1)}, u32[]{:S(2)}) copy-start(bf16[1792,256]{1,0:T(8,128)(2,1)} %copy-done.6) | copy-start | bytes 2752516
  131.8 17.9 %copy-start.11 = (bf16[1792,256]{1,0:T(8,128)(2,1)S(1)}, bf16[1792,256]{1,0:T(8,128)(2,1)}, u32[]{:S(2)}) copy-start(bf16[1792,256]{1,0:T(8,128)(2,1)} %get-tuple-element.3) | copy-start | bytes 2752516
  132.3 36.2 %copy-start.2 = (bf16[256,1792]{1,0:T(8,128)(2,1)S(1)}, bf16[256,1792]{1,0:T(8,128)(2,1)}, u32[]{:S(2)}) copy-start(bf16[256,1792]{1,0:T(8,128)(2,1)} %get-tuple-element.7) | copy-start | bytes 2752516
  132.3 36.2 %copy-start.3 = (bf16[256,1792]{1,0:T(8,128)(2,1)S(1)}, bf16[256,1792]{1,0:T(8,128)(2,1)}, u32[]{:S(2)}) copy-start(bf16[256,1792]{1,0:T(8,128)(2,1)} %get-tuple-element.8) | copy-start | bytes 2752516
  132.3 36.2 %copy-start.5 = (bf16[256,1792]{1,0:T(8,128)(2,1)S(1)}, bf16[256,1792]{1,0:T(8,128)(2,1)}, u32[]{:S(2)}) copy-start(bf16[256,1792]{1,0:T(8,128)(2,1)} %get-tuple-element.9) | copy-start | bytes 2752516
  132.3 36.2 %copy-start.10 = (bf16[256,1792]{1,0:T(8,128)(2,1)S(1)}, bf16[256,1792]{1,0:T(8,128)(2,1)}, u32[]{:S(2)}) copy-start(bf16[256,1792]{1,0:T(8,128)(2,1)} %get-tuple-element.6) | copy-start | bytes 2752516
  134.7 9.2 %collective-permute-start.1 = (bf16[256,256]{0,1:T(8,128)(2,1)S(1)}, bf16[256,256]{0,1:T(8,128)(2,1)S(1)}, u32[]{:S(2)}, u32[]{:S(2)}) collective-permute-start(bf16[256,256]{0,1:T(8,128)(2,1)S(1)} %convolution_convert_fusion.7), channel_id=1, source_target_pairs={{3,0},{0,1},{1,2},{2,3},{7,4},{4,5},{5,6},{6,7},{11,8},{8,9},{9,10... | collective-permute-start | bytes 393224 | tf_op jit(solution)/shard_map/ppermute | solution.py:10
  136.6 12.9 %collective-permute-start.2 = (bf16[256,256]{0,1:T(8,128)(2,1)S(1)}, bf16[256,256]{0,1:T(8,128)(2,1)S(1)}, u32[]{:S(2)}, u32[]{:S(2)}) collective-permute-start(bf16[256,256]{0,1:T(8,128)(2,1)S(1)} %convolution_convert_fusion.6), channel_id=1, source_target_pairs={{2,0},{3,1},{0,2},{1,3},{6,4},{7,5},{4,6},{5,7},{10,8},{11,9},{8,1... | collective-permute-start | bytes 393224 | tf_op jit(solution)/shard_map/ppermute | solution.py:10
  139.4 10.2 %collective-permute-start.3 = (bf16[256,256]{0,1:T(8,128)(2,1)S(1)}, bf16[256,256]{0,1:T(8,128)(2,1)S(1)}, u32[]{:S(2)}, u32[]{:S(2)}) collective-permute-start(bf16[256,256]{0,1:T(8,128)(2,1)S(1)} %convolution_convert_fusion.5), channel_id=1, source_target_pairs={{1,0},{2,1},{3,2},{0,3},{5,4},{6,5},{7,6},{4,7},{9,8},{10,9},{11,1... | collective-permute-start | bytes 393224 | tf_op jit(solution)/shard_map/ppermute | solution.py:10
  150.2 9.8 %collective-permute-start.4 = (bf16[256,256]{0,1:T(8,128)(2,1)S(1)}, bf16[256,256]{0,1:T(8,128)(2,1)S(1)}, u32[]{:S(2)}, u32[]{:S(2)}) collective-permute-start(bf16[256,256]{0,1:T(8,128)(2,1)S(1)} %multiply_convert_fusion), channel_id=1, source_target_pairs={{1,0},{2,1},{3,2},{0,3},{5,4},{6,5},{7,6},{4,7},{9,8},{10,9},{11,1... | collective-permute-start | bytes 393224 | tf_op jit(solution)/shard_map/ppermute | solution.py:10
  154.7 13.8 %collective-permute-start.5 = (bf16[256,256]{0,1:T(8,128)(2,1)S(1)}, bf16[256,256]{0,1:T(8,128)(2,1)S(1)}, u32[]{:S(2)}, u32[]{:S(2)}) collective-permute-start(bf16[256,256]{0,1:T(8,128)(2,1)S(1)} %multiply_convert_fusion), channel_id=1, source_target_pairs={{2,0},{3,1},{0,2},{1,3},{6,4},{7,5},{4,6},{5,7},{10,8},{11,9},{8,1... | collective-permute-start | bytes 393224 | tf_op jit(solution)/shard_map/ppermute | solution.py:10
  158.1 10.4 %collective-permute-start.6 = (bf16[256,256]{0,1:T(8,128)(2,1)S(1)}, bf16[256,256]{0,1:T(8,128)(2,1)S(1)}, u32[]{:S(2)}, u32[]{:S(2)}) collective-permute-start(bf16[256,256]{0,1:T(8,128)(2,1)S(1)} %multiply_convert_fusion), channel_id=1, source_target_pairs={{3,0},{0,1},{1,2},{2,3},{7,4},{4,5},{5,6},{6,7},{11,8},{8,9},{9,10... | collective-permute-start | bytes 393224 | tf_op jit(solution)/shard_map/ppermute | solution.py:10
  169.7 11.9 %copy-start.12 = (s32[1,16,8]{1,2,0:T(8,128)S(1)}, s32[1,16,8]{1,2,0:T(8,128)}, u32[]{:S(2)}) copy-start(s32[1,16,8]{1,2,0:T(8,128)} %param.13) | copy-start | bytes 1540
  169.7 12.1 %copy-start.14 = (f32[1,16,8]{1,2,0:T(8,128)S(1)}, f32[1,16,8]{1,2,0:T(8,128)}, u32[]{:S(2)}) copy-start(f32[1,16,8]{1,2,0:T(8,128)} %param.11) | copy-start | bytes 1540
  170.9 36.2 %all-to-all-start.1 = ((bf16[64,4,1792]{2,1,0:T(4,128)(2,1)}), bf16[64,4,1792]{2,1,0:T(4,128)(2,1)S(1)}, u32[]{:S(2)}, u32[]{:S(2)}) async-start(bf16[64,4,1792]{2,1,0:T(4,128)(2,1)} %reshape.131), calls=%async_computation.1 | async-start | bytes 1835008 | tf_op jit(solution)/shard_map/all_to_all | solution.py:102

commit v2 on v1

v2 whole, which is shorter than its diff:
```python
import jax
import jax.numpy as jnp
from jax import lax
from jax.sharding import Mesh, PartitionSpec as P

ROWS = 4
CORES = 2
LANES = 128


def passed_along(block, axis, distance):
    devices = range(lax.axis_size(axis))
    route = [((i - distance) % len(devices), i) for i in devices]
    return lax.ppermute(block, axis, route)


def slot_targets(route_rows, experts, capacity):
    flat_routes = route_rows.reshape(-1)
    matches = (flat_routes[:, None] == jnp.arange(experts, dtype=jnp.int32)[None, :]).astype(
        jnp.int32
    )
    before = jnp.cumsum(matches, axis=0) - matches
    slot_rank = jnp.sum(before * matches, axis=1)
    return (flat_routes * capacity + slot_rank).reshape(route_rows.shape)


def silu_slope(pre_act):
    squash = jax.nn.sigmoid(pre_act)
    return squash * (1.0 + pre_act * (1.0 - squash))


def contract_last(left_rows, right_matrix):
    return lax.dot_general(
        left_rows, right_matrix, (((1,), (1,)), ((), ())), preferred_element_type=jnp.float32
    )


def contract_first(left_rows, right_rows):
    return lax.dot_general(
        left_rows, right_rows, (((0,), (0,)), ((), ())), preferred_element_type=jnp.float32
    )


def matmul(left_rows, right_matrix):
    return jnp.dot(left_rows, right_matrix, preferred_element_type=jnp.float32)


def bf16_pieces(values, count):
    pieces = []
    for _ in range(count):
        piece = lax.reduce_precision(values, 8, 7)
        pieces.append(piece.astype(jnp.bfloat16))
        values = values - piece
    return pieces


def turned_parts(array, dim):
    parts = lax.axis_size("dp")
    own = lax.axis_index("dp")
    size = array.shape[dim] // parts
    return [
        lax.dynamic_slice_in_dim(array, lax.rem(own + j, parts) * size, size, axis=dim)
        for j in range(parts)
    ]


def to_others(partials):
    return [
        passed_along(partials[j].astype(jnp.bfloat16), "dp", j) for j in range(1, len(partials))
    ]


def from_others(block):
    return [passed_along(block, "dp", -j) for j in range(1, lax.axis_size("dp"))]


def added(parts):
    total = parts[0].astype(jnp.float32)
    for part in parts[1:]:
        total = total + part.astype(jnp.float32)
    return total


def exchanged(rows, axes):
    size = lax.axis_size(axes)
    blocks = rows.reshape(size, rows.shape[0] // size, rows.shape[1])
    blocks = lax.all_to_all(blocks, axes, split_axis=0, concat_axis=0, tiled=True)
    return blocks.reshape(rows.shape)


def labels(targets, probs, pieces):
    fields = [targets.astype(jnp.bfloat16)] + bf16_pieces(probs, pieces)
    fields = jnp.concatenate(fields, axis=1)
    return jnp.pad(fields, ((0, 0), (0, LANES - fields.shape[1])))


def column_tokens(rows, label):
    message = jnp.concatenate([rows, label], axis=1)
    count = lax.axis_size("y")
    copies = jnp.broadcast_to(message[None], (count,) + message.shape)
    taken = lax.all_to_all(copies, "y", split_axis=0, concat_axis=0, tiled=True)
    taken = taken.reshape(count * message.shape[0], message.shape[1])
    return taken[:, : rows.shape[1]], taken[:, rows.shape[1] :].astype(jnp.float32)


def tables(label, top_count, capacity, pieces):
    columns, cores = lax.axis_size("y"), lax.axis_size("core")
    experts = lax.axis_size("x") * columns * cores
    tokens = label.shape[0] // columns
    slot = jnp.arange(experts * capacity, dtype=jnp.int32)
    place = slot % capacity
    group = (slot // capacity) % columns
    core = (slot // (capacity * columns)) % cores
    row = slot // (capacity * columns * cores)
    expert = (row * columns + lax.axis_index("y")) * cores + core
    wanted = expert * capacity + place + group * (experts * capacity)
    start = (jnp.arange(label.shape[0], dtype=jnp.int32) // tokens) * (experts * capacity)
    filled = jnp.zeros((label.shape[0], slot.shape[0]), jnp.bool_)
    probs = jnp.zeros(filled.shape, jnp.float32)
    for k in range(top_count):
        target = label[:, k].astype(jnp.int32) + start
        match = target[:, None] == wanted[None, :]
        filled = filled | match
        prob = label[:, top_count + k]
        for piece in range(1, pieces):
            prob = prob + label[:, (piece + 1) * top_count + k]
        probs = jnp.where(match, prob[:, None], probs)
    return filled.astype(jnp.bfloat16), probs


def shards(
    fwd_act, fwd_routes, fwd_probs, bwd_grad, bwd_routes, bwd_probs, w_up, w_down, act_stash
):
    columns = lax.axis_size("y")
    experts = lax.axis_size(("x", "y", "core"))
    capacity = act_stash.shape[2] // experts
    top_count = fwd_routes.shape[2]
    row_axes = ("x", "core")

    label_fwd = labels(slot_targets(fwd_routes[0], experts, capacity), fwd_probs[0], 2)
    arriving = passed_along(fwd_act[0], "section", 1)
    tokens_fwd, label_fwd = column_tokens(arriving, label_fwd)
    table_fwd, probs_fwd = tables(label_fwd, top_count, capacity, 2)
    sent_fwd = contract_first(table_fwd, tokens_fwd).astype(jnp.bfloat16)
    recv_fwd = exchanged(sent_fwd, row_axes)
    pick_fwd = jnp.concatenate(bf16_pieces(probs_fwd, 2), axis=0)

    grad_in, bwd_routes, arriving = lax.optimization_barrier((bwd_grad[0], bwd_routes, arriving))
    label_bwd = labels(slot_targets(bwd_routes[0], experts, capacity), bwd_probs[0], 3)
    incoming = passed_along(grad_in, "section", -1)
    up_parts = turned_parts(w_up[0], 1)
    down_parts = turned_parts(w_down[0], 0)
    stash = turned_parts(act_stash[0, 0], 1)[0]
    stash = stash.reshape(lax.axis_size("x"), columns, lax.axis_size("core"), capacity, -1)
    stash = stash.transpose(0, 2, 1, 3, 4).reshape(experts * capacity, -1)
    slope_own = silu_slope(stash.astype(jnp.float32))
    incoming, label_bwd, up_parts, down_parts, slope_own, recv_fwd = lax.optimization_barrier(
        (incoming, label_bwd, up_parts, down_parts, slope_own, recv_fwd)
    )
    tokens_bwd, label_bwd = column_tokens(incoming, label_bwd)
    table_bwd, probs_bwd = tables(label_bwd, top_count, capacity, 3)
    slot_prob = jnp.sum(probs_bwd, axis=0)
    sent_bwd = (slot_prob[:, None] * contract_first(table_bwd, tokens_bwd)).astype(jnp.bfloat16)
    recv_bwd = exchanged(sent_bwd, row_axes)

    pre_parts = [matmul(recv_fwd, part) for part in up_parts]
    pre_own = added([pre_parts[0]] + to_others(pre_parts))
    hidden_own = jax.nn.silu(pre_own).astype(jnp.bfloat16)
    hidden_fwd = jnp.concatenate([hidden_own] + from_others(hidden_own), axis=1)
    out_rows = matmul(hidden_fwd, jnp.concatenate(down_parts, axis=0)).astype(jnp.bfloat16)
    out_rows, recv_bwd = lax.optimization_barrier((out_rows, recv_bwd))
    back_fwd = exchanged(out_rows, row_axes)
    both = matmul(pick_fwd, back_fwd)
    half = both.shape[0] // 2
    part_fwd = (both[:half] + both[half:]).astype(jnp.bfloat16)

    def to_tokens(parts):
        parts = exchanged(parts, "y")
        size = parts.shape[0] // columns
        return added([parts[i * size : i * size + size] for i in range(columns)]).astype(
            jnp.bfloat16
        )

    fwd_out = to_tokens(part_fwd)

    back_parts = [contract_last(recv_bwd, part) for part in down_parts]
    back_own = added([back_parts[0]] + to_others(back_parts))
    grad_own = (back_own * slope_own).astype(jnp.bfloat16)
    grad_pre = jnp.concatenate([grad_own] + from_others(grad_own), axis=1)
    grad_rows = contract_last(grad_pre, jnp.concatenate(up_parts, axis=1)).astype(jnp.bfloat16)
    fwd_out, grad_rows = lax.optimization_barrier((fwd_out, grad_rows))
    back_bwd = exchanged(grad_rows, row_axes)
    part_bwd = matmul(table_bwd, back_bwd).astype(jnp.bfloat16)

    return (fwd_out[None], to_tokens(part_bwd)[None])


def solution(mesh):
    sections, experts, parts = mesh.devices.shape
    split = (sections, ROWS, experts // (ROWS * CORES), CORES, parts)
    mesh = Mesh(mesh.devices.reshape(split), ("section", "x", "y", "core", "dp"))
    expert = ("x", "y", "core")
    tokens = P("section", expert, "dp")
    routes = P("section", expert, None)
    return jax.shard_map(
        shards,
        mesh=mesh,
        in_specs=(
            tokens,
            routes,
            routes,
            tokens,
            routes,
            routes,
            P(expert, "dp", None),
            P(expert, None, "dp"),
            P("section", expert, None, None),
        ),
        out_specs=(tokens, tokens),
        check_vma=False,
    )
```

time: 209 us -> 214 us (1.024)
  blocking collectives: 0 us -> 38.1 us
  waiting for transfers between devices: 74.6 us -> 37 us
  other arithmetic: 0.9 us -> 9.06 us
  local copies, waits for them, and re-layouts: 15.2 us -> 8.97 us
  matrix products: 18.9 us -> 24.6 us
  starting transfers between devices: 97.7 us -> 93.4 us
    all_to_all x0 -> x2, blocking collectives: none -> 38.1 us  [exchanged(): lax.all_to_all(blocks, axes, split_axis=0, concat_axis=0, tiled=True)]
    all_to_all x4 -> x6, waiting for transfers between devices: 38.4 us -> 13.2 us  [the longest x2 9.58 us: column_tokens(): taken = lax.all_to_all(copies, 'y', split_axis=0, concat_axis=0, tiled=True)]
    ppermute x14, waiting for transfers between devices: 36.2 us -> 23.9 us  [passed_along(): return lax.ppermute(block, axis, route)]
    all_to_all x4 -> x6, starting transfers between devices: 41.5 us -> 31.4 us  [the longest x4 20.4 us: exchanged(): lax.all_to_all(blocks, axes, split_axis=0, concat_axis=0, tiled=True)]
    reshape x8 -> x0, local copies, waits for them, and re-layouts: 6.91 us -> none  [the longest x1 2.61 us: shards(): grad_rows = grad_rows.reshape(experts, capacity, width_part)]
    ppermute x14, starting transfers between devices: 56.1 us -> 62 us  [passed_along(): return lax.ppermute(block, axis, route)]
    dot_general x5 -> x7, matrix products: 4.45 us -> 10.3 us  [matmul(): return jnp.dot(left_rows, right_matrix, preferred_element_type=jnp.float32)]
    convert_element_type x3 -> x13, other arithmetic: 0.19 us -> 5.86 us  [the longest x2 1.37 us: to_tokens(): added([parts[i * size:i * size + size] for i in range(columns)])]
  transfers between devices with their start and end apart: 18 -> 20, of which waited for: 9 -> 6; matrix products, arithmetic and copies ran while one was open for 12% -> 17% of each run, Pallas kernels for 0% -> 0%
where the time goes in v2:
time: 214 us; the launch traced here: 212 us
  starting transfers between devices  93.4 us (44%)
  blocking collectives  38.1 us (18%)
  waiting for transfers between devices  37 us (17%)
  matrix products  24.6 us (11%)
  other arithmetic  9.06 us (4%)
  local copies, waits for them, and re-layouts  8.97 us (4%)
    ppermute x14, starting transfers between devices, passed_along(): return lax.ppermute(block, axis, route)  62 us
    all_to_all x2, blocking collectives, exchanged(): lax.all_to_all(blocks, axes, split_axis=0, concat_axis=0, tiled=True)  38.1 us
    ppermute x14, waiting for transfers between devices, passed_along(): return lax.ppermute(block, axis, route)  23.9 us
    all_to_all x4, starting transfers between devices, exchanged(): lax.all_to_all(blocks, axes, split_axis=0, concat_axis=0, tiled=True)  20.4 us
    all_to_all x2, starting transfers between devices, column_tokens(): taken = lax.all_to_all(copies, 'y', split_axis=0, concat_axis=0, tiled=True)  10.9 us
    dot_general x7, matrix products, matmul(): return jnp.dot(left_rows, right_matrix, preferred_element_type=jnp.float32)  10.3 us
    dot_general x5, matrix products, contract_last(): lax.dot_general(left_rows, right_matrix, (((1,), (1,)), ((), ())), prefer...  10.1 us
    all_to_all x2, waiting for transfers between devices, column_tokens(): taken = lax.all_to_all(copies, 'y', split_axis=0, concat_axis=0, tiled=True)  9.58 us
  transfers between devices with their start and end apart: 20, of which 6 were waited for; matrix products, arithmetic and copies ran while one was open for 17% of the time, Pallas kernels for 0%

profile of v2, /device:TPU:1, one launch (start us, length us, event | category | flops | bytes accessed | tf_op | source)
XLA Modules:
  0.0 212.2 jit_solution(3170754789478036805)
XLA Ops:
  0.6 11.5 %collective-permute-start = (bf16[16,1792]{1,0:T(8,128)(2,1)}, bf16[16,1792]{1,0:T(8,128)(2,1)S(1)}, u32[]{:S(2)}, u32[]{:S(2)}) collective-permute-start(bf16[16,1792]{1,0:T(8,128)(2,1)} %bitcast.93), channel_id=1, source_target_pairs={{768,0},{0,256},{256,512},{512,768},{769,1},{1,257},{257,513},{513... | collective-permute-start | bytes 172040 | tf_op jit(solution)/shard_map/ppermute | solution.py:14
  12.1 0.9 dynamic-slice_convert_fusion
  13.4 0.8 copy.56
  14.9 0.7 fusion.131
  16.4 5.0 %collective-permute-done = bf16[16,1792]{1,0:T(8,128)(2,1)S(1)} collective-permute-done((bf16[16,1792]{1,0:T(8,128)(2,1)}, bf16[16,1792]{1,0:T(8,128)(2,1)S(1)}, u32[]{:S(2)}, u32[]{:S(2)}) %collective-permute-start) | collective-permute-done | bytes 57376 | tf_op jit(solution)/shard_map/ppermute | solution.py:14
  21.4 0.8 broadcast_in_dim.182
  22.2 6.8 %all-to-all-start = ((bf16[8,16,1920]{2,1,0:T(8,128)(2,1)}), bf16[8,16,1920]{2,1,0:T(8,128)(2,1)S(1)}, u32[]{:S(2)}, u32[]{:S(2)}) async-start(bf16[8,16,1920]{2,1,0:T(8,128)(2,1)} %broadcast_in_dim.182), calls=%async_computation | async-start | bytes 983040 | tf_op jit(solution)/shard_map/all_to_all | solution.py:101
  29.1 3.8 %dynamic-slice_bitcast_fusion = (bf16[256,1792]{1,0:T(8,128)(2,1)}, bf16[256,1792]{1,0:T(8,128)(2,1)}, bf16[256,1792]{1,0:T(8,128)(2,1)S(1)}, bf16[256,1792]{1,0:T(8,128)(2,1)}) fusion(bf16[1,1024,1792]{2,1,0:T(8,128)(2,1)} %param.16, s32[]{:T(128)S(6)} %select_n.201, s32[]{:T(128)S(6)} %select_n.199, s32[]{:T(128)S(6)} %select_n.198, s32[]{:T(128)S(6)} %select_n.200), kind=kLoop, calls=%fused_computation.38 | loop fusion | bytes 7340048 | tf_op jit(solution)/shard_map/dynamic_slice | solution.py:62
  32.9 1.7 dynamic-slice_bitcast_fusion.4
  34.6 9.6 %all-to-all-done = bf16[8,16,1920]{2,1,0:T(8,128)(2,1)S(1)} async-done(((bf16[8,16,1920]{2,1,0:T(8,128)(2,1)}), bf16[8,16,1920]{2,1,0:T(8,128)(2,1)S(1)}, u32[]{:S(2)}, u32[]{:S(2)}) %all-to-all-start) | async-done | bytes 491552 | tf_op jit(solution)/shard_map/all_to_all | solution.py:101
  44.6 1.6 convolution_convert_fusion
  46.2 6.8 %all-to-all-start.1 = ((bf16[8,32,1792]{2,1,0:T(8,128)(2,1)}), bf16[8,32,1792]{2,1,0:T(8,128)(2,1)S(1)}, u32[]{:S(2)}, u32[]{:S(2)}) async-start(bf16[8,32,1792]{2,1,0:T(8,128)(2,1)} %bitcast.16), calls=%async_computation.1 | async-start | bytes 1835008 | tf_op jit(solution)/shard_map/all_to_all | solution.py:87
  53.8 7.3 %collective-permute-start.1 = (bf16[16,1792]{1,0:T(8,128)(2,1)S(1)}, bf16[16,1792]{1,0:T(8,128)(2,1)S(1)}, u32[]{:S(2)}, u32[]{:S(2)}) collective-permute-start(bf16[16,1792]{1,0:T(8,128)(2,1)S(1)} %bitcast.94), channel_id=1, source_target_pairs={{256,0},{512,256},{768,512},{0,768},{257,1},{513,257},{769,513},{1... | collective-permute-start | bytes 172040 | tf_op jit(solution)/shard_map/ppermute | solution.py:14
  61.1 2.0 collective-permute-done.1
  63.2 3.6 %all-to-all-done.1 = bf16[8,32,1792]{2,1,0:T(8,128)(2,1)S(1)} async-done(((bf16[8,32,1792]{2,1,0:T(8,128)(2,1)}), bf16[8,32,1792]{2,1,0:T(8,128)(2,1)S(1)}, u32[]{:S(2)}, u32[]{:S(2)}) %all-to-all-start.1) | async-done | bytes 917536 | tf_op jit(solution)/shard_map/all_to_all | solution.py:87
  66.8 0.8 broadcast_in_dim.199
  67.6 4.1 %all-to-all-start.2 = ((bf16[8,16,1920]{2,1,0:T(8,128)(2,1)}), bf16[8,16,1920]{2,1,0:T(8,128)(2,1)}, u32[]{:S(2)}, u32[]{:S(2)}) async-start(bf16[8,16,1920]{2,1,0:T(8,128)(2,1)} %broadcast_in_dim.199), calls=%async_computation.2 | async-start | bytes 983040 | tf_op jit(solution)/shard_map/all_to_all | solution.py:101
  72.3 1.7 convolution_convert_fusion.7
  74.0 4.8 %collective-permute-start.2 = (bf16[256,256]{0,1:T(8,128)(2,1)S(1)}, bf16[256,256]{0,1:T(8,128)(2,1)}, u32[]{:S(2)}, u32[]{:S(2)}) collective-permute-start(bf16[256,256]{0,1:T(8,128)(2,1)S(1)} %convolution_convert_fusion.7), channel_id=1, source_target_pairs={{3,0},{0,1},{1,2},{2,3},{7,4},{4,5},{5,6},{6,7},{11,8},{8,9},{9,10... | collective-permute-start | bytes 393224 | tf_op jit(solution)/shard_map/ppermute | solution.py:14
  78.8 1.7 convolution_convert_fusion.6
  80.5 6.6 %collective-permute-start.3 = (bf16[256,256]{0,1:T(8,128)(2,1)S(1)}, bf16[256,256]{0,1:T(8,128)(2,1)}, u32[]{:S(2)}, u32[]{:S(2)}) collective-permute-start(bf16[256,256]{0,1:T(8,128)(2,1)S(1)} %convolution_convert_fusion.6), channel_id=1, source_target_pairs={{2,0},{3,1},{0,2},{1,3},{6,4},{7,5},{4,6},{5,7},{10,8},{11,9},{8,1... | collective-permute-start | bytes 393224 | tf_op jit(solution)/shard_map/ppermute | solution.py:14
  87.5 1.9 collective-permute-start.4
  89.5 0.8 slice_convert_fusion.16
  91.7 2.6 %fusion.16 = bf16[256,1792]{1,0:T(8,128)(2,1)} fusion(f32[256]{0:T(256)S(1)} %fusion.46, bf16[128,1920]{1,0:T(8,128)(2,1)} %bitcast.18, s32[256]{0:T(256)S(1)} %fusion.135, s32[128]{0:T(128)S(1)} %get-tuple-element.50, s32[128]{0:T(128)S(1)} %get-tuple-element.52, s32[128]{0:T(128)S(1)} %get-tuple-element.48, s32[128]{0:T(128)S(1)} %get-tuple-element.53, ...), kind=kOutput, calls=%fused_computation.17 | convolution fusion | flops 118849536 | bytes 1382400 | tf_op jit(solution)/shard_map/dot_general | solution.py:39
  94.3 5.2 %all-to-all-start.3 = ((bf16[8,32,1792]{2,1,0:T(8,128)(2,1)}), bf16[8,32,1792]{2,1,0:T(8,128)(2,1)S(1)}, u32[]{:S(2)}, u32[]{:S(2)}) async-start(bf16[8,32,1792]{2,1,0:T(8,128)(2,1)} %bitcast.89), calls=%async_computation.3 | async-start | bytes 1835008 | tf_op jit(solution)/shard_map/all_to_all | solution.py:87
  99.5 1.8 multiply_convert_fusion
  101.3 7.5 %collective-permute-start.5 = (bf16[256,256]{0,1:T(8,128)(2,1)S(1)}, bf16[256,256]{0,1:T(8,128)(2,1)S(1)}, u32[]{:S(2)}, u32[]{:S(2)}) collective-permute-start(bf16[256,256]{0,1:T(8,128)(2,1)S(1)} %multiply_convert_fusion), channel_id=1, source_target_pairs={{1,0},{2,1},{3,2},{0,3},{5,4},{6,5},{7,6},{4,7},{9,8},{10,9},{11,1... | collective-permute-start | bytes 393224 | tf_op jit(solution)/shard_map/ppermute | solution.py:14
  108.8 1.9 collective-permute-start.6
  110.8 2.2 %collective-permute-start.7 = (bf16[256,256]{0,1:T(8,128)(2,1)S(1)}, bf16[256,256]{0,1:T(8,128)(2,1)S(1)}, u32[]{:S(2)}, u32[]{:S(2)}) collective-permute-start(bf16[256,256]{0,1:T(8,128)(2,1)S(1)} %multiply_convert_fusion), channel_id=1, source_target_pairs={{3,0},{0,1},{1,2},{2,3},{7,4},{4,5},{5,6},{6,7},{11,8},{8,9},{9,10... | collective-permute-start | bytes 393224 | tf_op jit(solution)/shard_map/ppermute | solution.py:14
  113.3 7.9 %collective-permute-done.6 = bf16[256,256]{0,1:T(8,128)(2,1)S(1)} collective-permute-done((bf16[256,256]{0,1:T(8,128)(2,1)S(1)}, bf16[256,256]{0,1:T(8,128)(2,1)S(1)}, u32[]{:S(2)}, u32[]{:S(2)}) %collective-permute-start.6) | collective-permute-done | bytes 131104 | tf_op jit(solution)/shard_map/ppermute | solution.py:14
  121.2 3.8 %fusion.20 = bf16[256,1792]{1,0:T(8,128)(2,1)} fusion(bf16[256,1792]{1,0:T(8,128)(2,1)} %get-tuple-element.30, bf16[256,1792]{1,0:T(8,128)(2,1)} %get-tuple-element.29, bf16[256,1792]{1,0:T(8,128)(2,1)} %get-tuple-element.28, bf16[256,1792]{1,0:T(8,128)(2,1)S(1)} %get-tuple-element.27, bf16[256,256]{0,1:T(8,128)(2,1)S(1)} %collective-permute-done.7, ...), kind=kOutput, calls=%fused_computation.19 | convolution fusion | flops 956760064 | bytes 5111808 | tf_op jit(solution)/shard_map/dot_general | solution.py:45
  125.0 4.9 %all-to-all-start.4 = ((bf16[8,32,1792]{2,1,0:T(8,128)(2,1)}), bf16[8,32,1792]{2,1,0:T(8,128)(2,1)S(1)}, u32[]{:S(2)}, u32[]{:S(2)}) async-start(bf16[8,32,1792]{2,1,0:T(8,128)(2,1)} %bitcast.90), calls=%async_computation.4 | async-start | bytes 1835008 | tf_op jit(solution)/shard_map/all_to_all | solution.py:87
  130.0 2.3 %convolution_convert_fusion.4 = bf16[256,256]{0,1:T(8,128)(2,1)} fusion(bf16[256,1792]{1,0:T(8,128)(2,1)S(1)} %bitcast.74, bf16[256,1792]{1,0:T(8,128)(2,1)} %get-tuple-element.28), kind=kOutput, calls=%fused_computation.32 | convolution fusion | flops 234946560 | bytes 1966080 | tf_op jit(solution)/shard_map/dot_general | solution.py:33
  132.3 2.4 %collective-permute-start.8 = (bf16[256,256]{0,1:T(8,128)(2,1)}, bf16[256,256]{0,1:T(8,128)(2,1)}, u32[]{:S(2)}, u32[]{:S(2)}) collective-permute-start(bf16[256,256]{0,1:T(8,128)(2,1)} %convolution_convert_fusion.4), channel_id=1, source_target_pairs={{3,0},{0,1},{1,2},{2,3},{7,4},{4,5},{5,6},{6,7},{11,8},{8,9},{9,10... | collective-permute-start | bytes 393224 | tf_op jit(solution)/shard_map/ppermute | solution.py:14
  134.7 2.3 %convolution_convert_fusion.3 = bf16[256,256]{0,1:T(8,128)(2,1)} fusion(bf16[256,1792]{1,0:T(8,128)(2,1)S(1)} %bitcast.75, bf16[256,1792]{1,0:T(8,128)(2,1)} %get-tuple-element.29), kind=kOutput, calls=%fused_computation.31 | convolution fusion | flops 234946560 | bytes 1966080 | tf_op jit(solution)/shard_map/dot_general | solution.py:33
  137.0 3.8 %collective-permute-start.9 = (bf16[256,256]{0,1:T(8,128)(2,1)}, bf16[256,256]{0,1:T(8,128)(2,1)}, u32[]{:S(2)}, u32[]{:S(2)}) collective-permute-start(bf16[256,256]{0,1:T(8,128)(2,1)} %convolution_convert_fusion.3), channel_id=1, source_target_pairs={{2,0},{3,1},{0,2},{1,3},{6,4},{7,5},{4,6},{5,7},{10,8},{11,9},{8,1... | collective-permute-start | bytes 393224 | tf_op jit(solution)/shard_map/ppermute | solution.py:14
  140.8 1.1 convolution_convert_fusion.2
  141.9 4.2 %collective-permute-start.10 = (bf16[256,256]{0,1:T(8,128)(2,1)}, bf16[256,256]{0,1:T(8,128)(2,1)}, u32[]{:S(2)}, u32[]{:S(2)}) collective-permute-start(bf16[256,256]{0,1:T(8,128)(2,1)} %convolution_convert_fusion.2), channel_id=1, source_target_pairs={{1,0},{2,1},{3,2},{0,3},{5,4},{6,5},{7,6},{4,7},{9,8},{10,9},{11,1... | collective-permute-start | bytes 393224 | tf_op jit(solution)/shard_map/ppermute | solution.py:14
  146.6 0.9 fusion.29
  147.5 3.5 %all-to-all-start.5 = ((bf16[8,16,1792]{2,1,0:T(8,128)(2,1)}), bf16[8,16,1792]{2,1,0:T(8,128)(2,1)S(1)}, u32[]{:S(2)}, u32[]{:S(2)}) async-start(bf16[8,16,1792]{2,1,0:T(8,128)(2,1)} %bitcast.87), calls=%async_computation.5 | async-start | bytes 917504 | tf_op jit(solution)/shard_map/all_to_all | solution.py:87
  151.0 1.5 fusion.28
  152.5 3.8 %collective-permute-start.11 = (bf16[256,256]{0,1:T(8,128)(2,1)S(1)}, bf16[256,256]{0,1:T(8,128)(2,1)S(1)}, u32[]{:S(2)}, u32[]{:S(2)}) collective-permute-start(bf16[256,256]{0,1:T(8,128)(2,1)S(1)} %fusion.28), channel_id=1, source_target_pairs={{1,0},{2,1},{3,2},{0,3},{5,4},{6,5},{7,6},{4,7},{9,8},{10,9},{11,1... | collective-permute-start | bytes 393224 | tf_op jit(solution)/shard_map/ppermute | solution.py:14
  156.3 1.9 collective-permute-start.12
  158.2 2.2 %collective-permute-start.13 = (bf16[256,256]{0,1:T(8,128)(2,1)S(1)}, bf16[256,256]{0,1:T(8,128)(2,1)S(1)}, u32[]{:S(2)}, u32[]{:S(2)}) collective-permute-start(bf16[256,256]{0,1:T(8,128)(2,1)S(1)} %fusion.28), channel_id=1, source_target_pairs={{3,0},{0,1},{1,2},{2,3},{7,4},{4,5},{5,6},{6,7},{11,8},{8,9},{9,10... | collective-permute-start | bytes 393224 | tf_op jit(solution)/shard_map/ppermute | solution.py:14
  160.4 8.9 %collective-permute-done.12 = bf16[256,256]{0,1:T(8,128)(2,1)S(1)} collective-permute-done((bf16[256,256]{0,1:T(8,128)(2,1)S(1)}, bf16[256,256]{0,1:T(8,128)(2,1)S(1)}, u32[]{:S(2)}, u32[]{:S(2)}) %collective-permute-start.12) | collective-permute-done | bytes 131104 | tf_op jit(solution)/shard_map/ppermute | solution.py:14
  169.4 2.9 %fusion.17 = bf16[256,1792]{1,0:T(8,128)(2,1)S(1)} fusion(bf16[1792,256]{1,0:T(8,128)(2,1)S(1)} %copy-done.2, bf16[1792,256]{1,0:T(8,128)(2,1)} %get-tuple-element.25, bf16[1792,256]{1,0:T(8,128)(2,1)} %get-tuple-element.24, bf16[1792,256]{1,0:T(8,128)(2,1)} %get-tuple-element.23, bf16[256,256]{0,1:T(8,128)(2,1)S(1)} %collective-permute-done.13, ...), kind=kOutput, calls=%fused_computation.18 | convolution fusion | flops 956760064 | bytes 5111808 | tf_op jit(solution)/shard_map/dot_general | solution.py:33
  173.0 18.6 %all_to_all.40 = bf16[8,32,1792]{2,1,0:T(8,128)(2,1)S(1)} all-to-all(bf16[8,32,1792]{2,1,0:T(8,128)(2,1)S(1)} %bitcast.91), channel_id=1, replica_groups=mesh['section'=4,'x'=4,'y'=8,'core'=2,'dp'=4] {'x','core'}, dimensions={0} | all-to-all | bytes 1835008 | tf_op jit(solution)/shard_map/all_to_all | solution.py:87
  192.0 19.5 %all_to_all.41 = bf16[8,16,1792]{2,1,0:T(8,128)(2,1)S(1)} all-to-all(bf16[8,16,1792]{2,1,0:T(8,128)(2,1)S(1)} %bitcast.86), channel_id=1, replica_groups=mesh['section'=4,'x'=4,'y'=8,'core'=2,'dp'=4] {'y'}, dimensions={0} | all-to-all | bytes 917504 | tf_op jit(solution)/shard_map/all_to_all | solution.py:87
  (69 shorter events, 8.2 us)
Async XLA Ops:
  0.6 20.7 %collective-permute-start = (bf16[16,1792]{1,0:T(8,128)(2,1)}, bf16[16,1792]{1,0:T(8,128)(2,1)S(1)}, u32[]{:S(2)}, u32[]{:S(2)}) collective-permute-start(bf16[16,1792]{1,0:T(8,128)(2,1)} %bitcast.93), channel_id=1, source_target_pairs={{768,0},{0,256},{256,512},{512,768},{769,1},{1,257},{257,513},{513... | collective-permute-start | bytes 172040 | tf_op jit(solution)/shard_map/ppermute | solution.py:14
  22.2 22.0 %all-to-all-start = ((bf16[8,16,1920]{2,1,0:T(8,128)(2,1)}), bf16[8,16,1920]{2,1,0:T(8,128)(2,1)S(1)}, u32[]{:S(2)}, u32[]{:S(2)}) async-start(bf16[8,16,1920]{2,1,0:T(8,128)(2,1)} %broadcast_in_dim.182), calls=%async_computation | async-start | bytes 983040 | tf_op jit(solution)/shard_map/all_to_all | solution.py:101
  29.1 3.8 %copy-start = (bf16[1,1792,1024]{2,1,0:T(8,128)(2,1)S(1)}, bf16[1,1792,1024]{2,1,0:T(8,128)(2,1)}, u32[]{:S(2)}) copy-start(bf16[1,1792,1024]{2,1,0:T(8,128)(2,1)} %param.15) | copy-start | bytes 11010052
  34.6 52.4 %copy-start.1 = (bf16[1792,256]{1,0:T(8,128)(2,1)}, bf16[1792,256]{1,0:T(8,128)(2,1)S(1)}, u32[]{:S(2)}) copy-start(bf16[1792,256]{1,0:T(8,128)(2,1)S(1)} %get-tuple-element.26) | copy-start | bytes 2752516
  34.6 18.4 %copy-start.5 = (f32[1,16,8]{1,2,0:T(8,128)S(1)}, f32[1,16,8]{1,2,0:T(8,128)}, u32[]{:S(2)}) copy-start(f32[1,16,8]{1,2,0:T(8,128)} %param.14) | copy-start | bytes 1540
  34.6 18.4 %copy-start.4 = (s32[1,16,8]{1,2,0:T(8,128)S(1)}, s32[1,16,8]{1,2,0:T(8,128)}, u32[]{:S(2)}) copy-start(s32[1,16,8]{1,2,0:T(8,128)} %param.13) | copy-start | bytes 1540
  34.6 19.2 %copy-start.6 = (bf16[1,16,1792]{2,1,0:T(8,128)(2,1)S(1)}, bf16[1,16,1792]{2,1,0:T(8,128)(2,1)}, u32[]{:S(2)}) copy-start(bf16[1,16,1792]{2,1,0:T(8,128)(2,1)} %param.12) | copy-start | bytes 172036
  46.2 20.5 %all-to-all-start.1 = ((bf16[8,32,1792]{2,1,0:T(8,128)(2,1)}), bf16[8,32,1792]{2,1,0:T(8,128)(2,1)S(1)}, u32[]{:S(2)}, u32[]{:S(2)}) async-start(bf16[8,32,1792]{2,1,0:T(8,128)(2,1)} %bitcast.16), calls=%async_computation.1 | async-start | bytes 1835008 | tf_op jit(solution)/shard_map/all_to_all | solution.py:87
  53.8 9.3 %collective-permute-start.1 = (bf16[16,1792]{1,0:T(8,128)(2,1)S(1)}, bf16[16,1792]{1,0:T(8,128)(2,1)S(1)}, u32[]{:S(2)}, u32[]{:S(2)}) collective-permute-start(bf16[16,1792]{1,0:T(8,128)(2,1)S(1)} %bitcast.94), channel_id=1, source_target_pairs={{256,0},{512,256},{768,512},{0,768},{257,1},{513,257},{769,513},{1... | collective-permute-start | bytes 172040 | tf_op jit(solution)/shard_map/ppermute | solution.py:14
  67.6 21.8 %all-to-all-start.2 = ((bf16[8,16,1920]{2,1,0:T(8,128)(2,1)}), bf16[8,16,1920]{2,1,0:T(8,128)(2,1)}, u32[]{:S(2)}, u32[]{:S(2)}) async-start(bf16[8,16,1920]{2,1,0:T(8,128)(2,1)} %broadcast_in_dim.199), calls=%async_computation.2 | async-start | bytes 983040 | tf_op jit(solution)/shard_map/all_to_all | solution.py:101
  74.0 25.5 %collective-permute-start.2 = (bf16[256,256]{0,1:T(8,128)(2,1)S(1)}, bf16[256,256]{0,1:T(8,128)(2,1)}, u32[]{:S(2)}, u32[]{:S(2)}) collective-permute-start(bf16[256,256]{0,1:T(8,128)(2,1)S(1)} %convolution_convert_fusion.7), channel_id=1, source_target_pairs={{3,0},{0,1},{1,2},{2,3},{7,4},{4,5},{5,6},{6,7},{11,8},{8,9},{9,10... | collective-permute-start | bytes 393224 | tf_op jit(solution)/shard_map/ppermute | solution.py:14
  80.5 19.0 %collective-permute-start.3 = (bf16[256,256]{0,1:T(8,128)(2,1)S(1)}, bf16[256,256]{0,1:T(8,128)(2,1)}, u32[]{:S(2)}, u32[]{:S(2)}) collective-permute-start(bf16[256,256]{0,1:T(8,128)(2,1)S(1)} %convolution_convert_fusion.6), channel_id=1, source_target_pairs={{2,0},{3,1},{0,2},{1,3},{6,4},{7,5},{4,6},{5,7},{10,8},{11,9},{8,1... | collective-permute-start | bytes 393224 | tf_op jit(solution)/shard_map/ppermute | solution.py:14
  87.5 11.9 %collective-permute-start.4 = (bf16[256,256]{0,1:T(8,128)(2,1)S(1)}, bf16[256,256]{0,1:T(8,128)(2,1)}, u32[]{:S(2)}, u32[]{:S(2)}) collective-permute-start(bf16[256,256]{0,1:T(8,128)(2,1)S(1)} %convolution_convert_fusion.5), channel_id=1, source_target_pairs={{1,0},{2,1},{3,2},{0,3},{5,4},{6,5},{7,6},{4,7},{9,8},{10,9},{11,1... | collective-permute-start | bytes 393224 | tf_op jit(solution)/shard_map/ppermute | solution.py:14
  94.3 30.7 %all-to-all-start.3 = ((bf16[8,32,1792]{2,1,0:T(8,128)(2,1)}), bf16[8,32,1792]{2,1,0:T(8,128)(2,1)S(1)}, u32[]{:S(2)}, u32[]{:S(2)}) async-start(bf16[8,32,1792]{2,1,0:T(8,128)(2,1)} %bitcast.89), calls=%async_computation.3 | async-start | bytes 1835008 | tf_op jit(solution)/shard_map/all_to_all | solution.py:87
  101.3 12.0 %collective-permute-start.5 = (bf16[256,256]{0,1:T(8,128)(2,1)S(1)}, bf16[256,256]{0,1:T(8,128)(2,1)S(1)}, u32[]{:S(2)}, u32[]{:S(2)}) collective-permute-start(bf16[256,256]{0,1:T(8,128)(2,1)S(1)} %multiply_convert_fusion), channel_id=1, source_target_pairs={{1,0},{2,1},{3,2},{0,3},{5,4},{6,5},{7,6},{4,7},{9,8},{10,9},{11,1... | collective-permute-start | bytes 393224 | tf_op jit(solution)/shard_map/ppermute | solution.py:14
  108.8 12.4 %collective-permute-start.6 = (bf16[256,256]{0,1:T(8,128)(2,1)S(1)}, bf16[256,256]{0,1:T(8,128)(2,1)S(1)}, u32[]{:S(2)}, u32[]{:S(2)}) collective-permute-start(bf16[256,256]{0,1:T(8,128)(2,1)S(1)} %multiply_convert_fusion), channel_id=1, source_target_pairs={{2,0},{3,1},{0,2},{1,3},{6,4},{7,5},{4,6},{5,7},{10,8},{11,9},{8,1... | collective-permute-start | bytes 393224 | tf_op jit(solution)/shard_map/ppermute | solution.py:14
  110.8 10.5 %collective-permute-start.7 = (bf16[256,256]{0,1:T(8,128)(2,1)S(1)}, bf16[256,256]{0,1:T(8,128)(2,1)S(1)}, u32[]{:S(2)}, u32[]{:S(2)}) collective-permute-start(bf16[256,256]{0,1:T(8,128)(2,1)S(1)} %multiply_convert_fusion), channel_id=1, source_target_pairs={{3,0},{0,1},{1,2},{2,3},{7,4},{4,5},{5,6},{6,7},{11,8},{8,9},{9,10... | collective-permute-start | bytes 393224 | tf_op jit(solution)/shard_map/ppermute | solution.py:14
  125.0 21.2 %all-to-all-start.4 = ((bf16[8,32,1792]{2,1,0:T(8,128)(2,1)}), bf16[8,32,1792]{2,1,0:T(8,128)(2,1)S(1)}, u32[]{:S(2)}, u32[]{:S(2)}) async-start(bf16[8,32,1792]{2,1,0:T(8,128)(2,1)} %bitcast.90), calls=%async_computation.4 | async-start | bytes 1835008 | tf_op jit(solution)/shard_map/all_to_all | solution.py:87
  130.0 10.8 %copy-start.3 = (bf16[256,1792]{1,0:T(8,128)(2,1)S(1)}, bf16[256,1792]{1,0:T(8,128)(2,1)}, u32[]{:S(2)}) copy-start(bf16[256,1792]{1,0:T(8,128)(2,1)} %get-tuple-element.30) | copy-start | bytes 2752516
  132.3 18.6 %collective-permute-start.8 = (bf16[256,256]{0,1:T(8,128)(2,1)}, bf16[256,256]{0,1:T(8,128)(2,1)}, u32[]{:S(2)}, u32[]{:S(2)}) collective-permute-start(bf16[256,256]{0,1:T(8,128)(2,1)} %convolution_convert_fusion.4), channel_id=1, source_target_pairs={{3,0},{0,1},{1,2},{2,3},{7,4},{4,5},{5,6},{6,7},{11,8},{8,9},{9,10... | collective-permute-start | bytes 393224 | tf_op jit(solution)/shard_map/ppermute | solution.py:14
  137.0 14.0 %collective-permute-start.9 = (bf16[256,256]{0,1:T(8,128)(2,1)}, bf16[256,256]{0,1:T(8,128)(2,1)}, u32[]{:S(2)}, u32[]{:S(2)}) collective-permute-start(bf16[256,256]{0,1:T(8,128)(2,1)} %convolution_convert_fusion.3), channel_id=1, source_target_pairs={{2,0},{3,1},{0,2},{1,3},{6,4},{7,5},{4,6},{5,7},{10,8},{11,9},{8,1... | collective-permute-start | bytes 393224 | tf_op jit(solution)/shard_map/ppermute | solution.py:14
  141.9 9.1 %collective-permute-start.10 = (bf16[256,256]{0,1:T(8,128)(2,1)}, bf16[256,256]{0,1:T(8,128)(2,1)}, u32[]{:S(2)}, u32[]{:S(2)}) collective-permute-start(bf16[256,256]{0,1:T(8,128)(2,1)} %convolution_convert_fusion.2), channel_id=1, source_target_pairs={{1,0},{2,1},{3,2},{0,3},{5,4},{6,5},{7,6},{4,7},{9,8},{10,9},{11,1... | collective-permute-start | bytes 393224 | tf_op jit(solution)/shard_map/ppermute | solution.py:14
  146.6 22.7 %copy-start.2 = (bf16[1792,256]{1,0:T(8,128)(2,1)S(1)}, bf16[1792,256]{1,0:T(8,128)(2,1)}, u32[]{:S(2)}) copy-start(bf16[1792,256]{1,0:T(8,128)(2,1)} %copy-done.1) | copy-start | bytes 2752516
  147.5 24.8 %all-to-all-start.5 = ((bf16[8,16,1792]{2,1,0:T(8,128)(2,1)}), bf16[8,16,1792]{2,1,0:T(8,128)(2,1)S(1)}, u32[]{:S(2)}, u32[]{:S(2)}) async-start(bf16[8,16,1792]{2,1,0:T(8,128)(2,1)} %bitcast.87), calls=%async_computation.5 | async-start | bytes 917504 | tf_op jit(solution)/shard_map/all_to_all | solution.py:87
  152.5 7.9 %collective-permute-start.11 = (bf16[256,256]{0,1:T(8,128)(2,1)S(1)}, bf16[256,256]{0,1:T(8,128)(2,1)S(1)}, u32[]{:S(2)}, u32[]{:S(2)}) collective-permute-start(bf16[256,256]{0,1:T(8,128)(2,1)S(1)} %fusion.28), channel_id=1, source_target_pairs={{1,0},{2,1},{3,2},{0,3},{5,4},{6,5},{7,6},{4,7},{9,8},{10,9},{11,1... | collective-permute-start | bytes 393224 | tf_op jit(solution)/shard_map/ppermute | solution.py:14
  156.3 13.1 %collective-permute-start.12 = (bf16[256,256]{0,1:T(8,128)(2,1)S(1)}, bf16[256,256]{0,1:T(8,128)(2,1)S(1)}, u32[]{:S(2)}, u32[]{:S(2)}) collective-permute-start(bf16[256,256]{0,1:T(8,128)(2,1)S(1)} %fusion.28), channel_id=1, source_target_pairs={{2,0},{3,1},{0,2},{1,3},{6,4},{7,5},{4,6},{5,7},{10,8},{11,9},{8,1... | collective-permute-start | bytes 393224 | tf_op jit(solution)/shard_map/ppermute | solution.py:14
  158.2 11.1 %collective-permute-start.13 = (bf16[256,256]{0,1:T(8,128)(2,1)S(1)}, bf16[256,256]{0,1:T(8,128)(2,1)S(1)}, u32[]{:S(2)}, u32[]{:S(2)}) collective-permute-start(bf16[256,256]{0,1:T(8,128)(2,1)S(1)} %fusion.28), channel_id=1, source_target_pairs={{3,0},{0,1},{1,2},{2,3},{7,4},{4,5},{5,6},{6,7},{11,8},{8,9},{9,10... | collective-permute-start | bytes 393224 | tf_op jit(solution)/shard_map/ppermute | solution.py:14

commit v3 on v1

v3 whole, which is shorter than its diff:
```python
import jax
import jax.numpy as jnp
from jax import lax
from jax.experimental import pallas as pl
from jax.experimental.pallas import tpu as pltpu
from jax.sharding import Mesh, PartitionSpec as P

CORES = 2
VMEM_LIMIT = 48 * 1024 * 1024


def passed_along(block, axis, distance):
    devices = range(lax.axis_size(axis))
    route = [((i - distance) % len(devices), i) for i in devices]
    return lax.ppermute(block, axis, route)


def slot_targets(route_rows, experts, capacity):
    flat_routes = route_rows.reshape(-1)
    matches = (flat_routes[:, None] == jnp.arange(experts, dtype=jnp.int32)[None, :]).astype(
        jnp.int32
    )
    before = jnp.cumsum(matches, axis=0) - matches
    slot_rank = jnp.sum(before * matches, axis=1)
    return (flat_routes * capacity + slot_rank).reshape(route_rows.shape)


def chip_tables(targets, probs, rows, capacity):
    tokens, top_count = targets.shape
    core = lax.axis_index("core")
    other = jnp.arange(tokens, dtype=jnp.int32) // (tokens // CORES)
    group_core = jnp.where(other == 0, core, 1 - core)
    expert, place = targets // capacity, targets % capacity
    here = expert % CORES == core
    row = ((expert // CORES) * CORES + group_core[:, None]) * capacity + place
    row = jnp.where(here, row, -1)
    slots = jnp.arange(rows, dtype=jnp.int32)[None, :]
    filled = jnp.zeros((tokens, rows), jnp.bool_)
    shares = jnp.zeros((tokens, rows), jnp.float32)
    for k in range(top_count):
        match = row[:, k : k + 1] == slots
        filled = filled | match
        shares = jnp.where(match, probs[:, k : k + 1], shares)
    return filled.astype(jnp.bfloat16), shares


def silu_slope(pre_act):
    squash = jax.nn.sigmoid(pre_act)
    return squash * (1.0 + pre_act * (1.0 - squash))


def contract_last(left_rows, right_matrix):
    return lax.dot_general(
        left_rows, right_matrix, (((1,), (1,)), ((), ())), preferred_element_type=jnp.float32
    )


def matmul(left_rows, right_matrix):
    return jnp.dot(left_rows, right_matrix, preferred_element_type=jnp.float32)


def turned_own(array):
    size = array.shape[1] // lax.axis_size("dp")
    return lax.dynamic_slice_in_dim(array, lax.axis_index("dp") * size, size, axis=1)


def block_spec(weight, dim, parts):
    shape = list(weight.shape)
    shape[dim] //= parts

    def place(j, own):
        turned = lax.rem(own[0] + j, parts)
        return (turned, 0) if dim == 0 else (0, turned)

    return pl.BlockSpec(tuple(shape), place)


def whole_spec(shape):
    return pl.BlockSpec(shape, lambda j, own: (0,) * len(shape))


def hidden_blocks(rows, weight, dim):
    parts = lax.axis_size("dp")
    size = weight.shape[dim] // parts
    block = (rows.shape[0], size)
    contract = (((1,), (1 - dim,)), ((), ()))

    def kernel(own, rows_ref, weight_ref, *out_refs):
        product = lax.dot_general(
            rows_ref[...], weight_ref[...], contract, preferred_element_type=jnp.float32
        )
        for k in range(parts):

            @pl.when(pl.program_id(0) == k)
            def _():
                out_refs[k][...] = product.astype(out_refs[k].dtype)

    kinds = [jnp.float32] + [jnp.bfloat16] * (parts - 1)
    results = pl.pallas_call(
        kernel,
        out_shape=[jax.ShapeDtypeStruct(block, kind) for kind in kinds],
        grid_spec=pltpu.PrefetchScalarGridSpec(
            num_scalar_prefetch=1,
            grid=(parts,),
            in_specs=[whole_spec(rows.shape), block_spec(weight, dim, parts)],
            out_specs=[whole_spec(block)] * parts,
        ),
        compiler_params=pltpu.CompilerParams(vmem_limit_bytes=VMEM_LIMIT),
    )(lax.axis_index("dp").reshape(1), rows, weight)
    return list(results)


def ranked_blocks(rows, weight):
    parts = lax.axis_size("dp")
    size = weight.shape[0] // parts
    block = (rows.shape[0], size)

    def kernel(own, rows_ref, weight_ref, own_ref, out_ref):
        product = contract_last(rows_ref[...], weight_ref[...])
        out_ref[0] = product.astype(out_ref.dtype)

        @pl.when(pl.program_id(0) == own[0])
        def _():
            own_ref[...] = product

    return pl.pallas_call(
        kernel,
        out_shape=[
            jax.ShapeDtypeStruct(block, jnp.float32),
            jax.ShapeDtypeStruct((parts,) + block, jnp.bfloat16),
        ],
        grid_spec=pltpu.PrefetchScalarGridSpec(
            num_scalar_prefetch=1,
            grid=(parts,),
            in_specs=[
                whole_spec(rows.shape),
                pl.BlockSpec((size, weight.shape[1]), lambda j, own: (j, 0)),
            ],
            out_specs=[whole_spec(block), pl.BlockSpec((1,) + block, lambda j, own: (j, 0, 0))],
        ),
        compiler_params=pltpu.CompilerParams(vmem_limit_bytes=VMEM_LIMIT),
    )(lax.axis_index("dp").reshape(1), rows, weight)


def model_rows(hidden_parts, weight, dim):
    parts = len(hidden_parts)
    out_shape = (hidden_parts[0].shape[0], weight.shape[1 - dim])
    contract = (((1,), (dim,)), ((), ()))

    def kernel(own, *refs):
        hidden_refs, (weight_ref, out_ref, total) = refs[:parts], refs[parts:]
        for k in range(parts):

            @pl.when(pl.program_id(0) == k)
            def _():
                product = lax.dot_general(
                    hidden_refs[k][...],
                    weight_ref[...],
                    contract,
                    preferred_element_type=jnp.float32,
                )
                if k == 0:
                    total[...] = product
                elif k < parts - 1:
                    total[...] += product
                else:
                    out_ref[...] = (total[...] + product).astype(out_ref.dtype)

    return pl.pallas_call(
        kernel,
        out_shape=jax.ShapeDtypeStruct(out_shape, jnp.bfloat16),
        grid_spec=pltpu.PrefetchScalarGridSpec(
            num_scalar_prefetch=1,
            grid=(parts,),
            in_specs=[whole_spec(part.shape) for part in hidden_parts]
            + [block_spec(weight, dim, parts)],
            out_specs=whole_spec(out_shape),
            scratch_shapes=[pltpu.VMEM(out_shape, jnp.float32)],
        ),
        compiler_params=pltpu.CompilerParams(vmem_limit_bytes=VMEM_LIMIT),
    )(lax.axis_index("dp").reshape(1), *hidden_parts, weight)


def summed_at_once(total, blocks):
    own = lax.axis_index("dp")
    blocks = lax.all_to_all(blocks, "dp", split_axis=0, concat_axis=0, tiled=True)
    for rank in range(blocks.shape[0]):
        total = total + jnp.where(own == rank, 0.0, blocks[rank].astype(jnp.float32))
    return total


def to_others(partials):
    return [
        passed_along(partials[j].astype(jnp.bfloat16), "dp", j) for j in range(1, len(partials))
    ]


def from_others(block):
    return [passed_along(block, "dp", -j) for j in range(1, lax.axis_size("dp"))]


def added(parts):
    total = parts[0]
    for part in parts[1:]:
        total = total + part.astype(jnp.float32)
    return total


def halves(values):
    coarse = lax.reduce_precision(values, 8, 7)
    return coarse.astype(jnp.bfloat16), (values - coarse).astype(jnp.bfloat16)


def contract_first(left_rows, right_rows):
    return lax.dot_general(
        left_rows, right_rows, (((0,), (0,)), ((), ())), preferred_element_type=jnp.float32
    )


def with_other_core(block):
    return jnp.concatenate([block, passed_along(block, "core", 1)], axis=0)


def shards(
    fwd_act, fwd_routes, fwd_probs, bwd_grad, bwd_routes, bwd_probs, w_up, w_down, act_stash
):
    chips = lax.axis_size("chip")
    experts = chips * lax.axis_size("core")
    tokens_here, width_part = fwd_act.shape[1:]
    rows = act_stash.shape[2]
    capacity = rows // experts

    def to_experts(block):
        block = block.reshape(chips, rows // chips, width_part)
        block = lax.all_to_all(block, "chip", split_axis=0, concat_axis=0, tiled=True)
        return block.reshape(rows, width_part)

    def to_tokens(part):
        other = passed_along(part[tokens_here:], "core", 1)
        return (part[:tokens_here] + other).astype(jnp.bfloat16)

    arriving = passed_along(fwd_act[0], "section", 1)
    targets = jnp.concatenate(
        [
            slot_targets(fwd_routes[0], experts, capacity),
            slot_targets(bwd_routes[0], experts, capacity),
        ],
        axis=1,
    )
    targets = with_other_core(targets)
    probs = with_other_core(jnp.concatenate([fwd_probs[0], bwd_probs[0]], axis=1))
    top_count = fwd_routes.shape[2]
    table_fwd, shares_fwd = chip_tables(
        targets[:, :top_count], probs[:, :top_count], rows, capacity
    )
    table_bwd, shares_bwd = chip_tables(
        targets[:, top_count:], probs[:, top_count:], rows, capacity
    )
    slot_probs = jnp.sum(shares_bwd, axis=0)[:, None]
    pick_fwd = jnp.concatenate(halves(shares_fwd), axis=0)

    sent_fwd = contract_first(table_fwd, with_other_core(arriving)).astype(jnp.bfloat16)
    sent_fwd, grad_in = lax.optimization_barrier((sent_fwd, bwd_grad[0]))
    recv_fwd = to_experts(sent_fwd)

    incoming = with_other_core(passed_along(grad_in, "section", -1))
    sent_bwd = (slot_probs * contract_first(table_bwd, incoming)).astype(jnp.bfloat16)
    stash_own = turned_own(act_stash[0, 0])
    slope_own = silu_slope(stash_own.astype(jnp.float32))
    sent_bwd, slope_own = lax.optimization_barrier((sent_bwd, slope_own))
    recv_bwd = to_experts(sent_bwd)

    up_weight, down_weight = w_up[0], w_down[0]
    pre_parts = hidden_blocks(recv_fwd, up_weight, 1)
    pre_own = added([pre_parts[0]] + to_others(pre_parts))
    hidden_own = jax.nn.silu(pre_own).astype(jnp.bfloat16)
    hidden_parts = [hidden_own] + from_others(hidden_own)
    hidden_parts[1], recv_bwd = lax.optimization_barrier((hidden_parts[1], recv_bwd))
    back_own = summed_at_once(*ranked_blocks(recv_bwd, down_weight))
    out_rows = model_rows(hidden_parts, down_weight, 0)
    out_rows, back_own = lax.optimization_barrier((out_rows, back_own))
    back_fwd = to_experts(out_rows)
    grad_own = (back_own * slope_own).astype(jnp.bfloat16)
    grad_rows = model_rows([grad_own] + from_others(grad_own), up_weight, 1)
    back_bwd = to_experts(grad_rows)

    both = matmul(pick_fwd, back_fwd)
    half = both.shape[0] // 2
    fwd_out = to_tokens(both[:half] + both[half:])
    bwd_out = to_tokens(matmul(table_bwd, back_bwd))
    return (fwd_out[None], bwd_out[None])


def solution(mesh):
    sections, experts, parts = mesh.devices.shape
    split = (sections, experts // CORES, CORES, parts)
    mesh = Mesh(mesh.devices.reshape(split), ("section", "chip", "core", "dp"))
    expert = ("chip", "core")
    tokens = P("section", expert, "dp")
    routes = P("section", expert, None)
    return jax.shard_map(
        shards,
        mesh=mesh,
        in_specs=(
            tokens,
            routes,
            routes,
            tokens,
            routes,
            routes,
            P(expert, "dp", None),
            P(expert, None, "dp"),
            P("section", expert, None, None),
        ),
        out_specs=(tokens, tokens),
        check_vma=False,
    )
```

time: 209 us -> 201 us (0.962)
  waiting for transfers between devices: 74.6 us -> 46.3 us
  starting transfers between devices: 97.7 us -> 123 us
  matrix products: 18.9 us -> 3.56 us
  Pallas kernels: 0 us -> 11 us
  local copies, waits for them, and re-layouts: 15.2 us -> 10.2 us
  other arithmetic: 0.9 us -> 4.63 us
    ppermute x14 -> x17, starting transfers between devices: 56.1 us -> 84.8 us  [passed_along(): return lax.ppermute(block, axis, route)]
    all_to_all x4 -> x5, waiting for transfers between devices: 38.4 us -> 15.4 us  [the longest x4 15.4 us: to_experts(): lax.all_to_all(block, 'chip', split_axis=0, concat_axis=0, tiled=True)]
    dot_general x9 -> x2, matrix products: 14.4 us -> 2.98 us  [contract_first(): lax.dot_general(left_rows, right_rows, (((0,), (0,)), ((), ())), preferre...]
    pallas_call x0 -> x4, Pallas kernels: none -> 11 us  [the longest x2 6.04 us: model_rows(): pl.pallas_call(kernel, out_shape=jax.ShapeDtypeStruct(out_shape, jnp.bflo...]
    unnamed x36 -> x16, local copies, waits for them, and re-layouts: 1.77 us -> 9.7 us
    reshape x8 -> x0, local copies, waits for them, and re-layouts: 6.91 us -> none  [the longest x1 2.61 us: shards(): grad_rows = grad_rows.reshape(experts, capacity, width_part)]
    dynamic_slice x3 -> x0, local copies, waits for them, and re-layouts: 5.72 us -> none  [turned_parts(): lax.dynamic_slice_in_dim(array, lax.rem(own + j, parts) * size, size, axi...]
    ppermute x14 -> x17, waiting for transfers between devices: 36.2 us -> 30.9 us  [passed_along(): return lax.ppermute(block, axis, route)]
  transfers between devices with their start and end apart: 18 -> 22, of which waited for: 9 -> 13; matrix products, arithmetic and copies ran while one was open for 12% -> 4% of each run, Pallas kernels for 0% -> 4%
where the time goes in v3:
time: 201 us; the launch traced here: 200 us
  starting transfers between devices  123 us (61%)
  waiting for transfers between devices  46.3 us (23%)
  Pallas kernels  11 us (5%)
  local copies, waits for them, and re-layouts  10.2 us (5%)
  other arithmetic  4.63 us (2%)
  matrix products  3.56 us (2%)
    ppermute x17, starting transfers between devices, passed_along(): return lax.ppermute(block, axis, route)  84.8 us
    all_to_all x4, starting transfers between devices, to_experts(): lax.all_to_all(block, 'chip', split_axis=0, concat_axis=0, tiled=True)  33.3 us
    ppermute x17, waiting for transfers between devices, passed_along(): return lax.ppermute(block, axis, route)  30.9 us
    all_to_all x4, waiting for transfers between devices, to_experts(): lax.all_to_all(block, 'chip', split_axis=0, concat_axis=0, tiled=True)  15.4 us
    unnamed x16, local copies, waits for them, and re-layouts  9.7 us
    pallas_call x2, Pallas kernels, model_rows(): pl.pallas_call(kernel, out_shape=jax.ShapeDtypeStruct(out_shape, jnp.bflo...  6.04 us
    all_to_all x1, starting transfers between devices, summed_at_once(): lax.all_to_all(blocks, 'dp', split_axis=0, concat_axis=0, tiled=True)  4.83 us
  transfers between devices with their start and end apart: 22, of which 13 were waited for; matrix products, arithmetic and copies ran while one was open for 4% of the time, Pallas kernels for 4%

profile of v3, /device:TPU:1, one launch (start us, length us, event | category | flops | bytes accessed | tf_op | source)
XLA Modules:
  0.0 199.8 jit_solution(15985976126668234054)
XLA Ops:
  0.6 11.6 %collective-permute-start.2 = (bf16[16,1792]{1,0:T(8,128)(2,1)}, bf16[16,1792]{1,0:T(8,128)(2,1)S(1)}, u32[]{:S(2)}, u32[]{:S(2)}) collective-permute-start(bf16[16,1792]{1,0:T(8,128)(2,1)} %bitcast.118), channel_id=1, source_target_pairs={{768,0},{0,256},{256,512},{512,768},{769,1},{1,257},{257,513},{513... | collective-permute-start | bytes 172040 | tf_op jit(solution)/shard_map/ppermute | solution.py:15
  12.3 0.8 copy.21
  13.7 0.8 copy.19
  15.2 0.7 bitcast_add_fusion.4
  15.9 6.5 %collective-permute-start = (s32[16,16]{0,1:T(8,128)S(1)}, s32[16,16]{0,1:T(8,128)S(1)}, u32[]{:S(2)}, u32[]{:S(2)}) collective-permute-start(s32[16,16]{0,1:T(8,128)S(1)} %pad_add_fusion), channel_id=1, source_target_pairs={{4,0},{0,4},{5,1},{1,5},{6,2},{2,6},{7,3},{3,7},{12,8},{8,12},{13,... | collective-permute-start | bytes 3080 | tf_op jit(solution)/shard_map/ppermute | solution.py:15
  22.4 0.8 collective-permute-done
  23.4 3.7 %collective-permute-start.3 = (bf16[16,1792]{1,0:T(8,128)(2,1)S(1)}, bf16[16,1792]{1,0:T(8,128)(2,1)S(1)}, u32[]{:S(2)}, u32[]{:S(2)}) collective-permute-start(bf16[16,1792]{1,0:T(8,128)(2,1)S(1)} %collective-permute-done.2), channel_id=1, source_target_pairs={{4,0},{0,4},{5,1},{1,5},{6,2},{2,6},{7,3},{3,7},{12,8},{8,12},{13,... | collective-permute-start | bytes 172040 | tf_op jit(solution)/shard_map/ppermute | solution.py:15
  27.1 0.9 collective-permute-done.3
  27.9 1.5 convolution_convert_fusion
  29.4 7.5 %all-to-all-start = ((bf16[32,8,1792]{2,1,0:T(8,128)(2,1)}), bf16[32,8,1792]{2,1,0:T(8,128)(2,1)S(1)}, u32[]{:S(2)}, u32[]{:S(2)}) async-start(bf16[32,8,1792]{2,1,0:T(8,128)(2,1)} %bitcast.23), calls=%async_computation | async-start | bytes 1835008 | tf_op jit(solution)/shard_map/all_to_all | solution.py:235
  37.0 2.5 %collective-permute-start.1 = (f32[16,16]{0,1:T(8,128)S(1)}, f32[16,16]{0,1:T(8,128)S(1)}, u32[]{:S(2)}, u32[]{:S(2)}) collective-permute-start(f32[16,16]{0,1:T(8,128)S(1)} %pad_maximum_fusion), channel_id=1, source_target_pairs={{4,0},{0,4},{5,1},{1,5},{6,2},{2,6},{7,3},{3,7},{12,8},{8,12},{13,... | collective-permute-start | bytes 3080 | tf_op jit(solution)/shard_map/ppermute | solution.py:15
  39.6 1.0 fusion.9
  40.7 9.0 %collective-permute-start.8 = (bf16[16,1792]{1,0:T(8,128)(2,1)S(1)}, bf16[16,1792]{1,0:T(8,128)(2,1)S(1)}, u32[]{:S(2)}, u32[]{:S(2)}) collective-permute-start(bf16[16,1792]{1,0:T(8,128)(2,1)S(1)} %bitcast.119), channel_id=1, source_target_pairs={{256,0},{512,256},{768,512},{0,768},{257,1},{513,257},{769,513},{1... | collective-permute-start | bytes 172040 | tf_op jit(solution)/shard_map/ppermute | solution.py:15
  49.7 1.2 collective-permute-done.8
  50.9 2.9 %collective-permute-start.9 = (bf16[16,1792]{1,0:T(8,128)(2,1)S(1)}, bf16[16,1792]{1,0:T(8,128)(2,1)S(1)}, u32[]{:S(2)}, u32[]{:S(2)}) collective-permute-start(bf16[16,1792]{1,0:T(8,128)(2,1)S(1)} %collective-permute-done.8), channel_id=1, source_target_pairs={{4,0},{0,4},{5,1},{1,5},{6,2},{2,6},{7,3},{3,7},{12,8},{8,12},{13,... | collective-permute-start | bytes 172040 | tf_op jit(solution)/shard_map/ppermute | solution.py:15
  54.0 0.7 collective-permute-done.9
  54.7 1.5 fusion
  56.2 3.1 %all-to-all-done = bf16[32,8,1792]{2,1,0:T(8,128)(2,1)S(1)} async-done(((bf16[32,8,1792]{2,1,0:T(8,128)(2,1)}), bf16[32,8,1792]{2,1,0:T(8,128)(2,1)S(1)}, u32[]{:S(2)}, u32[]{:S(2)}) %all-to-all-start) | async-done | bytes 917536 | tf_op jit(solution)/shard_map/all_to_all | solution.py:235
  59.2 8.2 %all-to-all-start.1 = ((bf16[32,8,1792]{2,1,0:T(8,128)(2,1)}), bf16[32,8,1792]{2,1,0:T(8,128)(2,1)S(1)}, u32[]{:S(2)}, u32[]{:S(2)}) async-start(bf16[32,8,1792]{2,1,0:T(8,128)(2,1)} %bitcast.44), calls=%async_computation.1 | async-start | bytes 1835008 | tf_op jit(solution)/shard_map/all_to_all | solution.py:235
  67.4 2.0 %copy-done.2 = bf16[1,1792,1024]{2,1,0:T(8,128)(2,1)S(1)} copy-done((bf16[1,1792,1024]{2,1,0:T(8,128)(2,1)S(1)}, bf16[1,1792,1024]{2,1,0:T(8,128)(2,1)}, u32[]{:S(2)}) %copy-start.2) | copy-done | bytes 3670040
  69.4 2.3 %shard_map.104 = (f32[256,256]{1,0:T(8,128)S(1)}, bf16[256,256]{1,0:T(8,128)(2,1)S(1)}, bf16[256,256]{1,0:T(8,128)(2,1)S(1)}, bf16[256,256]{1,0:T(8,128)(2,1)S(1)}) custom-call(s32[1]{0:T(128)} %bitcast.20.own, bf16[256,1792]{1,0:T(8,128)(2,1)S(1)} %bitcast.112, bf16[1792,1024]{1,0:T(8,128)(2,1)S(1)} %bitcast.110), custom_call_target="tpu_custom_call" | custom-call | tf_op jit(solution)/shard_map/pallas_call | solution.py:99
  71.8 8.1 %collective-permute-start.6 = (bf16[256,256]{1,0:T(8,128)(2,1)S(1)}, bf16[256,256]{1,0:T(8,128)(2,1)S(1)}, u32[]{:S(2)}, u32[]{:S(2)}) collective-permute-start(bf16[256,256]{1,0:T(8,128)(2,1)S(1)} %get-tuple-element.20), channel_id=1, source_target_pairs={{1,0},{2,1},{3,2},{0,3},{5,4},{6,5},{7,6},{4,7},{9,8},{10,9},{11,1... | collective-permute-start | bytes 393224 | tf_op jit(solution)/shard_map/ppermute | solution.py:15
  79.9 1.9 collective-permute-start.5
  81.8 2.2 %collective-permute-start.4 = (bf16[256,256]{1,0:T(8,128)(2,1)S(1)}, bf16[256,256]{1,0:T(8,128)(2,1)S(1)}, u32[]{:S(2)}, u32[]{:S(2)}) collective-permute-start(bf16[256,256]{1,0:T(8,128)(2,1)S(1)} %get-tuple-element.18), channel_id=1, source_target_pairs={{3,0},{0,1},{1,2},{2,3},{7,4},{4,5},{5,6},{6,7},{11,8},{8,9},{9,10... | collective-permute-start | bytes 393224 | tf_op jit(solution)/shard_map/ppermute | solution.py:15
  84.0 6.5 %collective-permute-done.5 = bf16[256,256]{1,0:T(8,128)(2,1)S(1)} collective-permute-done((bf16[256,256]{1,0:T(8,128)(2,1)S(1)}, bf16[256,256]{1,0:T(8,128)(2,1)S(1)}, u32[]{:S(2)}, u32[]{:S(2)}) %collective-permute-start.5) | collective-permute-done | bytes 131104 | tf_op jit(solution)/shard_map/ppermute | solution.py:15
  90.6 3.6 %collective-permute-start.7 = (bf16[256,256]{1,0:T(8,128)(2,1)S(1)}, bf16[256,256]{1,0:T(8,128)(2,1)S(1)}, u32[]{:S(2)}, u32[]{:S(2)}) collective-permute-start(bf16[256,256]{1,0:T(8,128)(2,1)S(1)} %multiply_convert_fusion.1.refs_0_), channel_id=1, source_target_pairs={{1,0},{2,1},{3,2},{0,3},{5,4},{6,5},{7,6},{4,7},{9,8},{10,9},{11,1... | collective-permute-start | bytes 393224 | tf_op jit(solution)/shard_map/ppermute | solution.py:15
  94.2 2.3 %collective-permute-done.7.refs_1_ = bf16[256,256]{1,0:T(8,128)(2,1)S(1)} collective-permute-done((bf16[256,256]{1,0:T(8,128)(2,1)S(1)}, bf16[256,256]{1,0:T(8,128)(2,1)S(1)}, u32[]{:S(2)}, u32[]{:S(2)}) %collective-permute-start.7) | collective-permute-done | bytes 131104 | tf_op jit(solution)/shard_map/ppermute | solution.py:15
  96.5 2.0 %copy-done = bf16[1,1024,1792]{2,1,0:T(8,128)(2,1)S(1)} copy-done((bf16[1,1024,1792]{2,1,0:T(8,128)(2,1)S(1)}, bf16[1,1024,1792]{2,1,0:T(8,128)(2,1)}, u32[]{:S(2)}) %copy-start) | copy-done | bytes 3670040
  98.6 2.7 %shard_map.106 = (f32[256,256]{1,0:T(8,128)S(1)}, bf16[4,256,256]{2,1,0:T(8,128)(2,1)}) custom-call(s32[1]{0:T(128)} %bitcast.20.own, bf16[256,1792]{1,0:T(8,128)(2,1)S(1)} %bitcast.113, bf16[1024,1792]{1,0:T(8,128)(2,1)S(1)} %bitcast.108), custom_call_target="tpu_custom_call" | custom-call | tf_op jit(solution)/shard_map/pallas_call | solution.py:126
  101.2 4.8 %all-to-all-start.2 = ((bf16[4,256,256]{2,1,0:T(8,128)(2,1)}), bf16[4,256,256]{2,1,0:T(8,128)(2,1)S(1)}, u32[]{:S(2)}, u32[]{:S(2)}) async-start(bf16[4,256,256]{2,1,0:T(8,128)(2,1)} %get-tuple-element.26), calls=%async_computation.2 | async-start | bytes 1048576 | tf_op jit(solution)/shard_map/all_to_all | solution.py:186
  106.1 4.3 %collective-permute-start.10 = (bf16[256,256]{1,0:T(8,128)(2,1)S(1)}, bf16[256,256]{1,0:T(8,128)(2,1)S(1)}, u32[]{:S(2)}, u32[]{:S(2)}) collective-permute-start(bf16[256,256]{1,0:T(8,128)(2,1)S(1)} %multiply_convert_fusion.1.refs_0_), channel_id=1, source_target_pairs={{2,0},{3,1},{0,2},{1,3},{6,4},{7,5},{4,6},{5,7},{10,8},{11,9},{8,1... | collective-permute-start | bytes 393224 | tf_op jit(solution)/shard_map/ppermute | solution.py:15
  110.3 3.1 %collective-permute-start.11 = (bf16[256,256]{1,0:T(8,128)(2,1)S(1)}, bf16[256,256]{1,0:T(8,128)(2,1)S(1)}, u32[]{:S(2)}, u32[]{:S(2)}) collective-permute-start(bf16[256,256]{1,0:T(8,128)(2,1)S(1)} %multiply_convert_fusion.1.refs_0_), channel_id=1, source_target_pairs={{3,0},{0,1},{1,2},{2,3},{7,4},{4,5},{5,6},{6,7},{11,8},{8,9},{9,10... | collective-permute-start | bytes 393224 | tf_op jit(solution)/shard_map/ppermute | solution.py:15
  113.4 13.7 %collective-permute-done.10.refs_2_ = bf16[256,256]{1,0:T(8,128)(2,1)S(1)} collective-permute-done((bf16[256,256]{1,0:T(8,128)(2,1)S(1)}, bf16[256,256]{1,0:T(8,128)(2,1)S(1)}, u32[]{:S(2)}, u32[]{:S(2)}) %collective-permute-start.10) | collective-permute-done | bytes 131104 | tf_op jit(solution)/shard_map/ppermute | solution.py:15
  127.2 2.0 %copy-done.1 = bf16[1,1024,1792]{2,1,0:T(8,128)(2,1)S(1)} copy-done((bf16[1,1024,1792]{2,1,0:T(8,128)(2,1)S(1)}, bf16[1,1024,1792]{2,1,0:T(8,128)(2,1)}, u32[]{:S(2)}) %copy-start.1) | copy-done | bytes 3670040
  129.2 2.7 %shard_map.105 = bf16[256,1792]{1,0:T(8,128)(2,1)} custom-call(s32[1]{0:T(128)} %bitcast.20.own, bf16[256,256]{1,0:T(8,128)(2,1)S(1)} %multiply_convert_fusion.1.refs_0_, bf16[256,256]{1,0:T(8,128)(2,1)S(1)} %collective-permute-done.7.refs_1_, bf16[256,256]{1,0:T(8,128)(2,1)S(1)} %collective-permute-done.10.refs_2_, ...), custom_call_target="tpu_custom_call" | custom-call | tf_op jit(solution)/shard_map/pallas_call | solution.py:169
  132.0 8.9 %all-to-all-start.3 = ((bf16[32,8,1792]{2,1,0:T(8,128)(2,1)}), bf16[32,8,1792]{2,1,0:T(8,128)(2,1)S(1)}, u32[]{:S(2)}, u32[]{:S(2)}) async-start(bf16[32,8,1792]{2,1,0:T(8,128)(2,1)} %bitcast.51), calls=%async_computation.3 | async-start | bytes 1835008 | tf_op jit(solution)/shard_map/all_to_all | solution.py:235
  141.0 1.9 collective-permute-start.13
  142.9 2.9 %collective-permute-start.14 = (bf16[256,256]{1,0:T(8,128)(2,1)S(1)}, bf16[256,256]{1,0:T(8,128)(2,1)S(1)}, u32[]{:S(2)}, u32[]{:S(2)}) collective-permute-start(bf16[256,256]{1,0:T(8,128)(2,1)S(1)} %multiply_convert_fusion.refs_0_), channel_id=1, source_target_pairs={{2,0},{3,1},{0,2},{1,3},{6,4},{7,5},{4,6},{5,7},{10,8},{11,9},{8,1... | collective-permute-start | bytes 393224 | tf_op jit(solution)/shard_map/ppermute | solution.py:15
  145.9 3.4 %collective-permute-start.15 = (bf16[256,256]{1,0:T(8,128)(2,1)S(1)}, bf16[256,256]{1,0:T(8,128)(2,1)S(1)}, u32[]{:S(2)}, u32[]{:S(2)}) collective-permute-start(bf16[256,256]{1,0:T(8,128)(2,1)S(1)} %multiply_convert_fusion.refs_0_), channel_id=1, source_target_pairs={{3,0},{0,1},{1,2},{2,3},{7,4},{4,5},{5,6},{6,7},{11,8},{8,9},{9,10... | collective-permute-start | bytes 393224 | tf_op jit(solution)/shard_map/ppermute | solution.py:15
  149.2 2.5 %collective-permute-done.14.refs_2_ = bf16[256,256]{1,0:T(8,128)(2,1)S(1)} collective-permute-done((bf16[256,256]{1,0:T(8,128)(2,1)S(1)}, bf16[256,256]{1,0:T(8,128)(2,1)S(1)}, u32[]{:S(2)}, u32[]{:S(2)}) %collective-permute-start.14) | collective-permute-done | bytes 131104 | tf_op jit(solution)/shard_map/ppermute | solution.py:15
  151.7 2.1 %collective-permute-done.15.refs_3_ = bf16[256,256]{1,0:T(8,128)(2,1)S(1)} collective-permute-done((bf16[256,256]{1,0:T(8,128)(2,1)S(1)}, bf16[256,256]{1,0:T(8,128)(2,1)S(1)}, u32[]{:S(2)}, u32[]{:S(2)}) %collective-permute-start.15) | collective-permute-done | bytes 131104 | tf_op jit(solution)/shard_map/ppermute | solution.py:15
  153.8 2.0 %copy-done.3 = bf16[1,1792,1024]{2,1,0:T(8,128)(2,1)S(1)} copy-done((bf16[1,1792,1024]{2,1,0:T(8,128)(2,1)S(1)}, bf16[1,1792,1024]{2,1,0:T(8,128)(2,1)}, u32[]{:S(2)}) %copy-start.3) | copy-done | bytes 3670040
  155.8 3.3 %shard_map.107 = bf16[256,1792]{1,0:T(8,128)(2,1)} custom-call(s32[1]{0:T(128)} %bitcast.20.own, bf16[256,256]{1,0:T(8,128)(2,1)S(1)} %multiply_convert_fusion.refs_0_, bf16[256,256]{1,0:T(8,128)(2,1)S(1)} %collective-permute-done.13.refs_1_, bf16[256,256]{1,0:T(8,128)(2,1)S(1)} %collective-permute-done.14.refs_2_, ...), custom_call_target="tpu_custom_call" | custom-call | tf_op jit(solution)/shard_map/pallas_call | solution.py:169
  159.1 1.2 all-to-all-done.3
  160.4 8.7 %all-to-all-start.4 = ((bf16[32,8,1792]{2,1,0:T(8,128)(2,1)}), bf16[32,8,1792]{2,1,0:T(8,128)(2,1)S(1)}, u32[]{:S(2)}, u32[]{:S(2)}) async-start(bf16[32,8,1792]{2,1,0:T(8,128)(2,1)} %bitcast.54), calls=%async_computation.4 | async-start | bytes 1835008 | tf_op jit(solution)/shard_map/all_to_all | solution.py:235
  169.5 6.1 %collective-permute-start.12 = (f32[16,1792]{1,0:T(8,128)S(1)}, f32[16,1792]{1,0:T(8,128)S(1)}, u32[]{:S(2)}, u32[]{:S(2)}) collective-permute-start(f32[16,1792]{1,0:T(8,128)S(1)} %slice.219), channel_id=1, source_target_pairs={{4,0},{0,4},{5,1},{1,5},{6,2},{2,6},{7,3},{3,7},{12,8},{8,12},{13,... | collective-permute-start | bytes 344072 | tf_op jit(solution)/shard_map/ppermute | solution.py:15
  175.7 11.1 %all-to-all-done.4 = bf16[32,8,1792]{2,1,0:T(8,128)(2,1)S(1)} async-done(((bf16[32,8,1792]{2,1,0:T(8,128)(2,1)}), bf16[32,8,1792]{2,1,0:T(8,128)(2,1)S(1)}, u32[]{:S(2)}, u32[]{:S(2)}) %all-to-all-start.4) | async-done | bytes 917536 | tf_op jit(solution)/shard_map/all_to_all | solution.py:235
  187.1 11.1 %collective-permute-start.16 = (f32[16,1792]{1,0:T(8,128)S(1)}, f32[16,1792]{1,0:T(8,128)S(1)}, u32[]{:S(2)}, u32[]{:S(2)}) collective-permute-start(f32[16,1792]{1,0:T(8,128)S(1)} %slice.221), channel_id=1, source_target_pairs={{4,0},{0,4},{5,1},{1,5},{6,2},{2,6},{7,3},{3,7},{12,8},{8,12},{13,... | collective-permute-start | bytes 344072 | tf_op jit(solution)/shard_map/ppermute | solution.py:15
  (53 shorter events, 4.4 us)
Async XLA Ops:
  0.6 36.3 %copy-start.4 = (f32[1,16,8]{1,2,0:T(8,128)S(1)}, f32[1,16,8]{1,2,0:T(8,128)}, u32[]{:S(2)}) copy-start(f32[1,16,8]{1,2,0:T(8,128)} %param.14) | copy-start | bytes 1540
  0.6 36.3 %copy-start.5 = (f32[1,16,8]{1,2,0:T(8,128)S(1)}, f32[1,16,8]{1,2,0:T(8,128)}, u32[]{:S(2)}) copy-start(f32[1,16,8]{1,2,0:T(8,128)} %param.11) | copy-start | bytes 1540
  0.6 22.7 %collective-permute-start.2 = (bf16[16,1792]{1,0:T(8,128)(2,1)}, bf16[16,1792]{1,0:T(8,128)(2,1)S(1)}, u32[]{:S(2)}, u32[]{:S(2)}) collective-permute-start(bf16[16,1792]{1,0:T(8,128)(2,1)} %bitcast.118), channel_id=1, source_target_pairs={{768,0},{0,256},{256,512},{512,768},{769,1},{1,257},{257,513},{513... | collective-permute-start | bytes 172040 | tf_op jit(solution)/shard_map/ppermute | solution.py:15
  14.7 26.0 %copy-start.6 = (bf16[1,16,1792]{2,1,0:T(8,128)(2,1)S(1)}, bf16[1,16,1792]{2,1,0:T(8,128)(2,1)}, u32[]{:S(2)}) copy-start(bf16[1,16,1792]{2,1,0:T(8,128)(2,1)} %param.12) | copy-start | bytes 172036
  15.9 7.3 %collective-permute-start = (s32[16,16]{0,1:T(8,128)S(1)}, s32[16,16]{0,1:T(8,128)S(1)}, u32[]{:S(2)}, u32[]{:S(2)}) collective-permute-start(s32[16,16]{0,1:T(8,128)S(1)} %pad_add_fusion), channel_id=1, source_target_pairs={{4,0},{0,4},{5,1},{1,5},{6,2},{2,6},{7,3},{3,7},{12,8},{8,12},{13,... | collective-permute-start | bytes 3080 | tf_op jit(solution)/shard_map/ppermute | solution.py:15
  23.4 4.6 %collective-permute-start.3 = (bf16[16,1792]{1,0:T(8,128)(2,1)S(1)}, bf16[16,1792]{1,0:T(8,128)(2,1)S(1)}, u32[]{:S(2)}, u32[]{:S(2)}) collective-permute-start(bf16[16,1792]{1,0:T(8,128)(2,1)S(1)} %collective-permute-done.2), channel_id=1, source_target_pairs={{4,0},{0,4},{5,1},{1,5},{6,2},{2,6},{7,3},{3,7},{12,8},{8,12},{13,... | collective-permute-start | bytes 172040 | tf_op jit(solution)/shard_map/ppermute | solution.py:15
  29.4 29.8 %all-to-all-start = ((bf16[32,8,1792]{2,1,0:T(8,128)(2,1)}), bf16[32,8,1792]{2,1,0:T(8,128)(2,1)S(1)}, u32[]{:S(2)}, u32[]{:S(2)}) async-start(bf16[32,8,1792]{2,1,0:T(8,128)(2,1)} %bitcast.23), calls=%async_computation | async-start | bytes 1835008 | tf_op jit(solution)/shard_map/all_to_all | solution.py:235
  37.0 3.6 %collective-permute-start.1 = (f32[16,16]{0,1:T(8,128)S(1)}, f32[16,16]{0,1:T(8,128)S(1)}, u32[]{:S(2)}, u32[]{:S(2)}) collective-permute-start(f32[16,16]{0,1:T(8,128)S(1)} %pad_maximum_fusion), channel_id=1, source_target_pairs={{4,0},{0,4},{5,1},{1,5},{6,2},{2,6},{7,3},{3,7},{12,8},{8,12},{13,... | collective-permute-start | bytes 3080 | tf_op jit(solution)/shard_map/ppermute | solution.py:15
  40.7 10.2 %collective-permute-start.8 = (bf16[16,1792]{1,0:T(8,128)(2,1)S(1)}, bf16[16,1792]{1,0:T(8,128)(2,1)S(1)}, u32[]{:S(2)}, u32[]{:S(2)}) collective-permute-start(bf16[16,1792]{1,0:T(8,128)(2,1)S(1)} %bitcast.119), channel_id=1, source_target_pairs={{256,0},{512,256},{768,512},{0,768},{257,1},{513,257},{769,513},{1... | collective-permute-start | bytes 172040 | tf_op jit(solution)/shard_map/ppermute | solution.py:15
  50.9 3.8 %collective-permute-start.9 = (bf16[16,1792]{1,0:T(8,128)(2,1)S(1)}, bf16[16,1792]{1,0:T(8,128)(2,1)S(1)}, u32[]{:S(2)}, u32[]{:S(2)}) collective-permute-start(bf16[16,1792]{1,0:T(8,128)(2,1)S(1)} %collective-permute-done.8), channel_id=1, source_target_pairs={{4,0},{0,4},{5,1},{1,5},{6,2},{2,6},{7,3},{3,7},{12,8},{8,12},{13,... | collective-permute-start | bytes 172040 | tf_op jit(solution)/shard_map/ppermute | solution.py:15
  59.2 35.0 %all-to-all-start.1 = ((bf16[32,8,1792]{2,1,0:T(8,128)(2,1)}), bf16[32,8,1792]{2,1,0:T(8,128)(2,1)S(1)}, u32[]{:S(2)}, u32[]{:S(2)}) async-start(bf16[32,8,1792]{2,1,0:T(8,128)(2,1)} %bitcast.44), calls=%async_computation.1 | async-start | bytes 1835008 | tf_op jit(solution)/shard_map/all_to_all | solution.py:235
  67.4 2.0 %copy-start.2 = (bf16[1,1792,1024]{2,1,0:T(8,128)(2,1)S(1)}, bf16[1,1792,1024]{2,1,0:T(8,128)(2,1)}, u32[]{:S(2)}) copy-start(bf16[1,1792,1024]{2,1,0:T(8,128)(2,1)} %param.15) | copy-start | bytes 11010052
  71.8 12.3 %collective-permute-start.6 = (bf16[256,256]{1,0:T(8,128)(2,1)S(1)}, bf16[256,256]{1,0:T(8,128)(2,1)S(1)}, u32[]{:S(2)}, u32[]{:S(2)}) collective-permute-start(bf16[256,256]{1,0:T(8,128)(2,1)S(1)} %get-tuple-element.20), channel_id=1, source_target_pairs={{1,0},{2,1},{3,2},{0,3},{5,4},{6,5},{7,6},{4,7},{9,8},{10,9},{11,1... | collective-permute-start | bytes 393224 | tf_op jit(solution)/shard_map/ppermute | solution.py:15
  79.9 10.6 %collective-permute-start.5 = (bf16[256,256]{1,0:T(8,128)(2,1)S(1)}, bf16[256,256]{1,0:T(8,128)(2,1)S(1)}, u32[]{:S(2)}, u32[]{:S(2)}) collective-permute-start(bf16[256,256]{1,0:T(8,128)(2,1)S(1)} %get-tuple-element.19), channel_id=1, source_target_pairs={{2,0},{3,1},{0,2},{1,3},{6,4},{7,5},{4,6},{5,7},{10,8},{11,9},{8,1... | collective-permute-start | bytes 393224 | tf_op jit(solution)/shard_map/ppermute | solution.py:15
  81.8 8.7 %collective-permute-start.4 = (bf16[256,256]{1,0:T(8,128)(2,1)S(1)}, bf16[256,256]{1,0:T(8,128)(2,1)S(1)}, u32[]{:S(2)}, u32[]{:S(2)}) collective-permute-start(bf16[256,256]{1,0:T(8,128)(2,1)S(1)} %get-tuple-element.18), channel_id=1, source_target_pairs={{3,0},{0,1},{1,2},{2,3},{7,4},{4,5},{5,6},{6,7},{11,8},{8,9},{9,10... | collective-permute-start | bytes 393224 | tf_op jit(solution)/shard_map/ppermute | solution.py:15
  90.6 5.9 %collective-permute-start.7 = (bf16[256,256]{1,0:T(8,128)(2,1)S(1)}, bf16[256,256]{1,0:T(8,128)(2,1)S(1)}, u32[]{:S(2)}, u32[]{:S(2)}) collective-permute-start(bf16[256,256]{1,0:T(8,128)(2,1)S(1)} %multiply_convert_fusion.1.refs_0_), channel_id=1, source_target_pairs={{1,0},{2,1},{3,2},{0,3},{5,4},{6,5},{7,6},{4,7},{9,8},{10,9},{11,1... | collective-permute-start | bytes 393224 | tf_op jit(solution)/shard_map/ppermute | solution.py:15
  96.5 2.0 %copy-start = (bf16[1,1024,1792]{2,1,0:T(8,128)(2,1)S(1)}, bf16[1,1024,1792]{2,1,0:T(8,128)(2,1)}, u32[]{:S(2)}) copy-start(bf16[1,1024,1792]{2,1,0:T(8,128)(2,1)} %param.16) | copy-start | bytes 11010052
  101.2 30.7 %all-to-all-start.2 = ((bf16[4,256,256]{2,1,0:T(8,128)(2,1)}), bf16[4,256,256]{2,1,0:T(8,128)(2,1)S(1)}, u32[]{:S(2)}, u32[]{:S(2)}) async-start(bf16[4,256,256]{2,1,0:T(8,128)(2,1)} %get-tuple-element.26), calls=%async_computation.2 | async-start | bytes 1048576 | tf_op jit(solution)/shard_map/all_to_all | solution.py:186
  106.1 21.1 %collective-permute-start.10 = (bf16[256,256]{1,0:T(8,128)(2,1)S(1)}, bf16[256,256]{1,0:T(8,128)(2,1)S(1)}, u32[]{:S(2)}, u32[]{:S(2)}) collective-permute-start(bf16[256,256]{1,0:T(8,128)(2,1)S(1)} %multiply_convert_fusion.1.refs_0_), channel_id=1, source_target_pairs={{2,0},{3,1},{0,2},{1,3},{6,4},{7,5},{4,6},{5,7},{10,8},{11,9},{8,1... | collective-permute-start | bytes 393224 | tf_op jit(solution)/shard_map/ppermute | solution.py:15
  110.3 16.9 %collective-permute-start.11 = (bf16[256,256]{1,0:T(8,128)(2,1)S(1)}, bf16[256,256]{1,0:T(8,128)(2,1)S(1)}, u32[]{:S(2)}, u32[]{:S(2)}) collective-permute-start(bf16[256,256]{1,0:T(8,128)(2,1)S(1)} %multiply_convert_fusion.1.refs_0_), channel_id=1, source_target_pairs={{3,0},{0,1},{1,2},{2,3},{7,4},{4,5},{5,6},{6,7},{11,8},{8,9},{9,10... | collective-permute-start | bytes 393224 | tf_op jit(solution)/shard_map/ppermute | solution.py:15
  127.2 2.0 %copy-start.1 = (bf16[1,1024,1792]{2,1,0:T(8,128)(2,1)S(1)}, bf16[1,1024,1792]{2,1,0:T(8,128)(2,1)}, u32[]{:S(2)}) copy-start(bf16[1,1024,1792]{2,1,0:T(8,128)(2,1)} %param.16) | copy-start | bytes 11010052
  132.0 28.4 %all-to-all-start.3 = ((bf16[32,8,1792]{2,1,0:T(8,128)(2,1)}), bf16[32,8,1792]{2,1,0:T(8,128)(2,1)S(1)}, u32[]{:S(2)}, u32[]{:S(2)}) async-start(bf16[32,8,1792]{2,1,0:T(8,128)(2,1)} %bitcast.51), calls=%async_computation.3 | async-start | bytes 1835008 | tf_op jit(solution)/shard_map/all_to_all | solution.py:235
  141.0 8.2 %collective-permute-start.13 = (bf16[256,256]{1,0:T(8,128)(2,1)S(1)}, bf16[256,256]{1,0:T(8,128)(2,1)S(1)}, u32[]{:S(2)}, u32[]{:S(2)}) collective-permute-start(bf16[256,256]{1,0:T(8,128)(2,1)S(1)} %multiply_convert_fusion.refs_0_), channel_id=1, source_target_pairs={{1,0},{2,1},{3,2},{0,3},{5,4},{6,5},{7,6},{4,7},{9,8},{10,9},{11,1... | collective-permute-start | bytes 393224 | tf_op jit(solution)/shard_map/ppermute | solution.py:15
  142.9 8.8 %collective-permute-start.14 = (bf16[256,256]{1,0:T(8,128)(2,1)S(1)}, bf16[256,256]{1,0:T(8,128)(2,1)S(1)}, u32[]{:S(2)}, u32[]{:S(2)}) collective-permute-start(bf16[256,256]{1,0:T(8,128)(2,1)S(1)} %multiply_convert_fusion.refs_0_), channel_id=1, source_target_pairs={{2,0},{3,1},{0,2},{1,3},{6,4},{7,5},{4,6},{5,7},{10,8},{11,9},{8,1... | collective-permute-start | bytes 393224 | tf_op jit(solution)/shard_map/ppermute | solution.py:15
  145.9 7.9 %collective-permute-start.15 = (bf16[256,256]{1,0:T(8,128)(2,1)S(1)}, bf16[256,256]{1,0:T(8,128)(2,1)S(1)}, u32[]{:S(2)}, u32[]{:S(2)}) collective-permute-start(bf16[256,256]{1,0:T(8,128)(2,1)S(1)} %multiply_convert_fusion.refs_0_), channel_id=1, source_target_pairs={{3,0},{0,1},{1,2},{2,3},{7,4},{4,5},{5,6},{6,7},{11,8},{8,9},{9,10... | collective-permute-start | bytes 393224 | tf_op jit(solution)/shard_map/ppermute | solution.py:15
  153.8 2.0 %copy-start.3 = (bf16[1,1792,1024]{2,1,0:T(8,128)(2,1)S(1)}, bf16[1,1792,1024]{2,1,0:T(8,128)(2,1)}, u32[]{:S(2)}) copy-start(bf16[1,1792,1024]{2,1,0:T(8,128)(2,1)} %param.15) | copy-start | bytes 11010052
  160.4 26.4 %all-to-all-start.4 = ((bf16[32,8,1792]{2,1,0:T(8,128)(2,1)}), bf16[32,8,1792]{2,1,0:T(8,128)(2,1)S(1)}, u32[]{:S(2)}, u32[]{:S(2)}) async-start(bf16[32,8,1792]{2,1,0:T(8,128)(2,1)} %bitcast.54), calls=%async_computation.4 | async-start | bytes 1835008 | tf_op jit(solution)/shard_map/all_to_all | solution.py:235
  169.5 28.7 %collective-permute-start.12 = (f32[16,1792]{1,0:T(8,128)S(1)}, f32[16,1792]{1,0:T(8,128)S(1)}, u32[]{:S(2)}, u32[]{:S(2)}) collective-permute-start(f32[16,1792]{1,0:T(8,128)S(1)} %slice.219), channel_id=1, source_target_pairs={{4,0},{0,4},{5,1},{1,5},{6,2},{2,6},{7,3},{3,7},{12,8},{8,12},{13,... | collective-permute-start | bytes 344072 | tf_op jit(solution)/shard_map/ppermute | solution.py:15
  187.1 12.1 %collective-permute-start.16 = (f32[16,1792]{1,0:T(8,128)S(1)}, f32[16,1792]{1,0:T(8,128)S(1)}, u32[]{:S(2)}, u32[]{:S(2)}) collective-permute-start(f32[16,1792]{1,0:T(8,128)S(1)} %slice.221), channel_id=1, source_target_pairs={{4,0},{0,4},{5,1},{1,5},{6,2},{2,6},{7,3},{3,7},{12,8},{8,12},{13,... | collective-permute-start | bytes 344072 | tf_op jit(solution)/shard_map/ppermute | solution.py:15

commit v4 on v3

--- a/solution.py
+++ b/solution.py
@@ -64,121 +64,100 @@
     return lax.dynamic_slice_in_dim(array, lax.axis_index("dp") * size, size, axis=1)
 
 
-def block_spec(weight, dim, parts):
-    shape = list(weight.shape)
-    shape[dim] //= parts
-
-    def place(j, own):
-        turned = lax.rem(own[0] + j, parts)
-        return (turned, 0) if dim == 0 else (0, turned)
-
-    return pl.BlockSpec(tuple(shape), place)
-
-
-def whole_spec(shape):
-    return pl.BlockSpec(shape, lambda j, own: (0,) * len(shape))
+def streamed(weight, dim, order, body, out_shape, inputs):
+    parts = lax.axis_size("dp")
+    size = weight.shape[dim] // parts
+    shape = (size, weight.shape[1]) if dim == 0 else (weight.shape[0], size)
+
+    def kernel(own, *refs):
+        in_refs, weight_ref = refs[: len(inputs)], refs[len(inputs)]
+        out_refs, blocks, arrived = refs[len(inputs) + 1 : -2], refs[-2], refs[-1]
+        copies = []
+        for j in range(parts):
+            start = pl.multiple_of(order(own[0], j) * size, size)
+            block = (
+                weight_ref.at[pl.ds(start, size), :]
+                if dim == 0
+                else weight_ref.at[:, pl.ds(start, size)]
+            )
+            copies.append(pltpu.make_async_copy(block, blocks.at[j], arrived.at[j]))
+            copies[j].start()
+        carried = None
+        for j in range(parts):
+            copies[j].wait()
+            carried = body(j, own[0], in_refs, blocks[j], out_refs, carried)
+
+    return pl.pallas_call(
+        kernel,
+        out_shape=out_shape,
+        in_specs=[pl.BlockSpec(memory_space=pltpu.SMEM)]
+        + [pl.BlockSpec(memory_space=pltpu.VMEM)] * len(inputs)
+        + [pl.BlockSpec(memory_space=pltpu.HBM)],
+        out_specs=jax.tree.map(lambda _: pl.BlockSpec(memory_space=pltpu.VMEM), out_shape),
+        scratch_shapes=[
+            pltpu.VMEM((parts,) + shape, weight.dtype),
+            pltpu.SemaphoreType.DMA((parts,)),
+        ],
+        compiler_params=pltpu.CompilerParams(vmem_limit_bytes=VMEM_LIMIT),
+    )(lax.axis_index("dp").reshape(1), *inputs, pltpu.with_memory_space_constraint(weight, pltpu.HBM))
+
+
+def turned(own, j):
+    return lax.rem(own + j, lax.axis_size("dp"))
+
+
+def product(left, right, dim):
+    return lax.dot_general(
+        left, right, (((1,), (dim,)), ((), ())), preferred_element_type=jnp.float32
+    )
 
 
 def hidden_blocks(rows, weight, dim):
     parts = lax.axis_size("dp")
-    size = weight.shape[dim] // parts
-    block = (rows.shape[0], size)
-    contract = (((1,), (1 - dim,)), ((), ()))
-
-    def kernel(own, rows_ref, weight_ref, *out_refs):
-        product = lax.dot_general(
-            rows_ref[...], weight_ref[...], contract, preferred_element_type=jnp.float32
+    block = (rows.shape[0], weight.shape[dim] // parts)
+
+    def body(j, own, in_refs, weight_block, out_refs, carried):
+        out_refs[j][...] = product(in_refs[0][...], weight_block, 1 - dim).astype(
+            out_refs[j].dtype
         )
-        for k in range(parts):
-
-            @pl.when(pl.program_id(0) == k)
-            def _():
-                out_refs[k][...] = product.astype(out_refs[k].dtype)
 
     kinds = [jnp.float32] + [jnp.bfloat16] * (parts - 1)
-    results = pl.pallas_call(
-        kernel,
-        out_shape=[jax.ShapeDtypeStruct(block, kind) for kind in kinds],
-        grid_spec=pltpu.PrefetchScalarGridSpec(
-            num_scalar_prefetch=1,
-            grid=(parts,),
-            in_specs=[whole_spec(rows.shape), block_spec(weight, dim, parts)],
-            out_specs=[whole_spec(block)] * parts,
-        ),
-        compiler_params=pltpu.CompilerParams(vmem_limit_bytes=VMEM_LIMIT),
-    )(lax.axis_index("dp").reshape(1), rows, weight)
-    return list(results)
+    out_shape = [jax.ShapeDtypeStruct(block, kind) for kind in kinds]
+    return list(streamed(weight, dim, turned, body, out_shape, [rows]))
 
 
 def ranked_blocks(rows, weight):
     parts = lax.axis_size("dp")
-    size = weight.shape[0] // parts
-    block = (rows.shape[0], size)
-
-    def kernel(own, rows_ref, weight_ref, own_ref, out_ref):
-        product = contract_last(rows_ref[...], weight_ref[...])
-        out_ref[0] = product.astype(out_ref.dtype)
-
-        @pl.when(pl.program_id(0) == own[0])
+    block = (rows.shape[0], weight.shape[0] // parts)
+
+    def body(j, own, in_refs, weight_block, out_refs, carried):
+        result = product(in_refs[0][...], weight_block, 1)
+        out_refs[1][j] = result.astype(jnp.bfloat16)
+
+        @pl.when(own == j)
         def _():
-            own_ref[...] = product
-
-    return pl.pallas_call(
-        kernel,
-        out_shape=[
-            jax.ShapeDtypeStruct(block, jnp.float32),
-            jax.ShapeDtypeStruct((parts,) + block, jnp.bfloat16),
-        ],
-        grid_spec=pltpu.PrefetchScalarGridSpec(
-            num_scalar_prefetch=1,
-            grid=(parts,),
-            in_specs=[
-                whole_spec(rows.shape),
-                pl.BlockSpec((size, weight.shape[1]), lambda j, own: (j, 0)),
-            ],
-            out_specs=[whole_spec(block), pl.BlockSpec((1,) + block, lambda j, own: (j, 0, 0))],
-        ),
-        compiler_params=pltpu.CompilerParams(vmem_limit_bytes=VMEM_LIMIT),
-    )(lax.axis_index("dp").reshape(1), rows, weight)
+            out_refs[0][...] = result
+
+    out_shape = [
+        jax.ShapeDtypeStruct(block, jnp.float32),
+        jax.ShapeDtypeStruct((parts,) + block, jnp.bfloat16),
+    ]
+    return streamed(weight, 0, lambda own, j: j, body, out_shape, [rows])
 
 
 def model_rows(hidden_parts, weight, dim):
     parts = len(hidden_parts)
     out_shape = (hidden_parts[0].shape[0], weight.shape[1 - dim])
-    contract = (((1,), (dim,)), ((), ()))
-
-    def kernel(own, *refs):
-        hidden_refs, (weight_ref, out_ref, total) = refs[:parts], refs[parts:]
-        for k in range(parts):
-
-            @pl.when(pl.program_id(0) == k)
-            def _():
-                product = lax.dot_general(
-                    hidden_refs[k][...],
-                    weight_ref[...],
-                    contract,
-                    preferred_element_type=jnp.float32,
-                )
-                if k == 0:
-                    total[...] = product
-                elif k < parts - 1:
-                    total[...] += product
-                else:
-                    out_ref[...] = (total[...] + product).astype(out_ref.dtype)
-
-    return pl.pallas_call(
-        kernel,
-        out_shape=jax.ShapeDtypeStruct(out_shape, jnp.bfloat16),
-        grid_spec=pltpu.PrefetchScalarGridSpec(
-            num_scalar_prefetch=1,
-            grid=(parts,),
-            in_specs=[whole_spec(part.shape) for part in hidden_parts]
-            + [block_spec(weight, dim, parts)],
-            out_specs=whole_spec(out_shape),
-            scratch_shapes=[pltpu.VMEM(out_shape, jnp.float32)],
-        ),
-        compiler_params=pltpu.CompilerParams(vmem_limit_bytes=VMEM_LIMIT),
-    )(lax.axis_index("dp").reshape(1), *hidden_parts, weight)
+
+    def body(j, own, in_refs, weight_block, out_refs, carried):
+        result = product(in_refs[j][...], weight_block, dim)
+        total = result if carried is None else carried + result
+        if j == parts - 1:
+            out_refs[0][...] = total.astype(jnp.bfloat16)
+        return total
+
+    out_shape = jax.ShapeDtypeStruct(out_shape, jnp.bfloat16)
+    return streamed(weight, dim, turned, body, out_shape, hidden_parts)
 
 
 def summed_at_once(total, blocks):
@@ -274,11 +253,13 @@
     pre_parts = hidden_blocks(recv_fwd, up_weight, 1)
     pre_own = added([pre_parts[0]] + to_others(pre_parts))
     hidden_own = jax.nn.silu(pre_own).astype(jnp.bfloat16)
+    hidden_own, recv_bwd = lax.optimization_barrier((hidden_own, recv_bwd))
     hidden_parts = [hidden_own] + from_others(hidden_own)
-    hidden_parts[1], recv_bwd = lax.optimization_barrier((hidden_parts[1], recv_bwd))
-    back_own = summed_at_once(*ranked_blocks(recv_bwd, down_weight))
+    back_parts = hidden_blocks(recv_bwd, down_weight, 0)
+    back_parts = [back_parts[0]] + to_others(back_parts)
     out_rows = model_rows(hidden_parts, down_weight, 0)
-    out_rows, back_own = lax.optimization_barrier((out_rows, back_own))
+    out_rows, back_parts = lax.optimization_barrier((out_rows, back_parts))
+    back_own = added(back_parts)
     back_fwd = to_experts(out_rows)
     grad_own = (back_own * slope_own).astype(jnp.bfloat16)
     grad_rows = model_rows([grad_own] + from_others(grad_own), up_weight, 1)

time: 201 us -> 198 us (0.985)
  local copies, waits for them, and re-layouts: 10.2 us -> 2.09 us
  Pallas kernels: 11 us -> 15.2 us
    unnamed x16 -> x8, local copies, waits for them, and re-layouts: 9.7 us -> 1.55 us
    all_to_all x4, waiting for transfers between devices: 15.4 us -> 22.8 us  [to_experts(): lax.all_to_all(block, 'chip', split_axis=0, concat_axis=0, tiled=True)]
    ppermute x17 -> x20, waiting for transfers between devices: 30.9 us -> 23.6 us  [passed_along(): return lax.ppermute(block, axis, route)]
    all_to_all x1 -> x0, starting transfers between devices: 4.83 us -> none  [summed_at_once(): lax.all_to_all(blocks, 'dp', split_axis=0, concat_axis=0, tiled=True)]
    pallas_call x4, Pallas kernels: 11 us -> 15.2 us  [streamed(): pl.pallas_call(kernel, out_shape=out_shape, in_specs=[pl.BlockSpec(memory...]
    ppermute x17 -> x20, starting transfers between devices: 84.8 us -> 87.7 us  [passed_along(): return lax.ppermute(block, axis, route)]
  transfers between devices with their start and end apart: 22 -> 24, of which waited for: 13 -> 11; matrix products, arithmetic and copies ran while one was open for 4% -> 2% of each run, Pallas kernels for 4% -> 8%
where the time goes in v4:
time: 198 us; the launch traced here: 195 us
  starting transfers between devices  122 us (62%)
  waiting for transfers between devices  46.4 us (23%)
  Pallas kernels  15.2 us (8%)
  other arithmetic  4.57 us (2%)
  matrix products  3.57 us (2%)
  local copies, waits for them, and re-layouts  2.09 us (1%)
    ppermute x20, starting transfers between devices, passed_along(): return lax.ppermute(block, axis, route)  87.7 us
    all_to_all x4, starting transfers between devices, to_experts(): lax.all_to_all(block, 'chip', split_axis=0, concat_axis=0, tiled=True)  34.5 us
    ppermute x20, waiting for transfers between devices, passed_along(): return lax.ppermute(block, axis, route)  23.6 us
    all_to_all x4, waiting for transfers between devices, to_experts(): lax.all_to_all(block, 'chip', split_axis=0, concat_axis=0, tiled=True)  22.8 us
    pallas_call x4, Pallas kernels, streamed(): pl.pallas_call(kernel, out_shape=out_shape, in_specs=[pl.BlockSpec(memory...  15.2 us
  transfers between devices with their start and end apart: 24, of which 11 were waited for; matrix products, arithmetic and copies ran while one was open for 2% of the time, Pallas kernels for 8%

profile of v4, /device:TPU:1, one launch (start us, length us, event | category | flops | bytes accessed | tf_op | source)
XLA Modules:
  0.0 195.3 jit_solution(11859806013744624245)
XLA Ops:
  0.6 0.8 copy.19
  1.5 0.8 copy.21
  3.6 0.7 bitcast_add_fusion
  4.3 16.1 %collective-permute-start = (s32[16,16]{0,1:T(8,128)S(1)}, s32[16,16]{0,1:T(8,128)S(1)}, u32[]{:S(2)}, u32[]{:S(2)}) collective-permute-start(s32[16,16]{0,1:T(8,128)S(1)} %pad_add_fusion), channel_id=1, source_target_pairs={{4,0},{0,4},{5,1},{1,5},{6,2},{2,6},{7,3},{3,7},{12,8},{8,12},{13,... | collective-permute-start | bytes 3080 | tf_op jit(solution)/shard_map/ppermute | solution.py:15
  20.4 1.9 collective-permute-start.2
  22.4 7.5 %collective-permute-done.2 = bf16[16,1792]{1,0:T(8,128)(2,1)S(1)} collective-permute-done((bf16[16,1792]{1,0:T(8,128)(2,1)}, bf16[16,1792]{1,0:T(8,128)(2,1)S(1)}, u32[]{:S(2)}, u32[]{:S(2)}) %collective-permute-start.2) | collective-permute-done | bytes 57376 | tf_op jit(solution)/shard_map/ppermute | solution.py:15
  29.9 2.9 %collective-permute-start.3 = (bf16[16,1792]{1,0:T(8,128)(2,1)S(1)}, bf16[16,1792]{1,0:T(8,128)(2,1)S(1)}, u32[]{:S(2)}, u32[]{:S(2)}) collective-permute-start(bf16[16,1792]{1,0:T(8,128)(2,1)S(1)} %collective-permute-done.2), channel_id=1, source_target_pairs={{4,0},{0,4},{5,1},{1,5},{6,2},{2,6},{7,3},{3,7},{12,8},{8,12},{13,... | collective-permute-start | bytes 172040 | tf_op jit(solution)/shard_map/ppermute | solution.py:15
  32.8 0.9 collective-permute-done.3
  33.7 1.5 convolution_convert_fusion
  35.1 7.8 %all-to-all-start = ((bf16[32,8,1792]{2,1,0:T(8,128)(2,1)}), bf16[32,8,1792]{2,1,0:T(8,128)(2,1)S(1)}, u32[]{:S(2)}, u32[]{:S(2)}) async-start(bf16[32,8,1792]{2,1,0:T(8,128)(2,1)} %bitcast.23), calls=%async_computation | async-start | bytes 1835008 | tf_op jit(solution)/shard_map/all_to_all | solution.py:214
  43.0 2.5 %collective-permute-start.1 = (f32[16,16]{0,1:T(8,128)S(1)}, f32[16,16]{0,1:T(8,128)S(1)}, u32[]{:S(2)}, u32[]{:S(2)}) collective-permute-start(f32[16,16]{0,1:T(8,128)S(1)} %pad_maximum_fusion), channel_id=1, source_target_pairs={{4,0},{0,4},{5,1},{1,5},{6,2},{2,6},{7,3},{3,7},{12,8},{8,12},{13,... | collective-permute-start | bytes 3080 | tf_op jit(solution)/shard_map/ppermute | solution.py:15
  45.5 1.0 fusion.9
  46.6 7.3 %collective-permute-start.7 = (bf16[16,1792]{1,0:T(8,128)(2,1)S(1)}, bf16[16,1792]{1,0:T(8,128)(2,1)S(1)}, u32[]{:S(2)}, u32[]{:S(2)}) collective-permute-start(bf16[16,1792]{1,0:T(8,128)(2,1)S(1)} %bitcast.105), channel_id=1, source_target_pairs={{256,0},{512,256},{768,512},{0,768},{257,1},{513,257},{769,513},{1... | collective-permute-start | bytes 172040 | tf_op jit(solution)/shard_map/ppermute | solution.py:15
  53.9 1.9 collective-permute-done.7
  55.8 2.8 %collective-permute-start.8 = (bf16[16,1792]{1,0:T(8,128)(2,1)S(1)}, bf16[16,1792]{1,0:T(8,128)(2,1)S(1)}, u32[]{:S(2)}, u32[]{:S(2)}) collective-permute-start(bf16[16,1792]{1,0:T(8,128)(2,1)S(1)} %collective-permute-done.7), channel_id=1, source_target_pairs={{4,0},{0,4},{5,1},{1,5},{6,2},{2,6},{7,3},{3,7},{12,8},{8,12},{13,... | collective-permute-start | bytes 172040 | tf_op jit(solution)/shard_map/ppermute | solution.py:15
  58.8 0.7 collective-permute-done.8
  59.6 1.5 fusion
  61.1 4.2 %all-to-all-done = bf16[32,8,1792]{2,1,0:T(8,128)(2,1)S(1)} async-done(((bf16[32,8,1792]{2,1,0:T(8,128)(2,1)}), bf16[32,8,1792]{2,1,0:T(8,128)(2,1)S(1)}, u32[]{:S(2)}, u32[]{:S(2)}) %all-to-all-start) | async-done | bytes 917536 | tf_op jit(solution)/shard_map/all_to_all | solution.py:214
  65.2 8.2 %all-to-all-start.1 = ((bf16[32,8,1792]{2,1,0:T(8,128)(2,1)}), bf16[32,8,1792]{2,1,0:T(8,128)(2,1)S(1)}, u32[]{:S(2)}, u32[]{:S(2)}) async-start(bf16[32,8,1792]{2,1,0:T(8,128)(2,1)} %bitcast.44), calls=%async_computation.1 | async-start | bytes 1835008 | tf_op jit(solution)/shard_map/all_to_all | solution.py:214
  73.4 3.7 %shard_map.104 = (f32[256,256]{1,0:T(8,128)S(1)}, bf16[256,256]{1,0:T(8,128)(2,1)S(1)}, bf16[256,256]{1,0:T(8,128)(2,1)S(1)}, bf16[256,256]{1,0:T(8,128)(2,1)S(1)}) custom-call(s32[1]{0:T(128)} %bitcast.20.own, bf16[256,1792]{1,0:T(8,128)(2,1)S(1)} %bitcast.94, bf16[1792,1024]{1,0:T(8,128)(2,1)} %bitcast.98), custom_call_target="tpu_custom_call" | custom-call | tf_op jit(solution)/shard_map/pallas_call | solution.py:90
  77.1 4.2 %collective-permute-start.4 = (bf16[256,256]{1,0:T(8,128)(2,1)S(1)}, bf16[256,256]{1,0:T(8,128)(2,1)S(1)}, u32[]{:S(2)}, u32[]{:S(2)}) collective-permute-start(bf16[256,256]{1,0:T(8,128)(2,1)S(1)} %get-tuple-element.23), channel_id=1, source_target_pairs={{3,0},{0,1},{1,2},{2,3},{7,4},{4,5},{5,6},{6,7},{11,8},{8,9},{9,10... | collective-permute-start | bytes 393224 | tf_op jit(solution)/shard_map/ppermute | solution.py:15
  81.3 6.2 %collective-permute-start.5 = (bf16[256,256]{1,0:T(8,128)(2,1)S(1)}, bf16[256,256]{1,0:T(8,128)(2,1)S(1)}, u32[]{:S(2)}, u32[]{:S(2)}) collective-permute-start(bf16[256,256]{1,0:T(8,128)(2,1)S(1)} %get-tuple-element.24), channel_id=1, source_target_pairs={{2,0},{3,1},{0,2},{1,3},{6,4},{7,5},{4,6},{5,7},{10,8},{11,9},{8,1... | collective-permute-start | bytes 393224 | tf_op jit(solution)/shard_map/ppermute | solution.py:15
  87.6 2.0 %collective-permute-start.6 = (bf16[256,256]{1,0:T(8,128)(2,1)S(1)}, bf16[256,256]{1,0:T(8,128)(2,1)S(1)}, u32[]{:S(2)}, u32[]{:S(2)}) collective-permute-start(bf16[256,256]{1,0:T(8,128)(2,1)S(1)} %get-tuple-element.25), channel_id=1, source_target_pairs={{1,0},{2,1},{3,2},{0,3},{5,4},{6,5},{7,6},{4,7},{9,8},{10,9},{11,1... | collective-permute-start | bytes 393224 | tf_op jit(solution)/shard_map/ppermute | solution.py:15
  89.6 5.6 %collective-permute-done.5 = bf16[256,256]{1,0:T(8,128)(2,1)S(1)} collective-permute-done((bf16[256,256]{1,0:T(8,128)(2,1)S(1)}, bf16[256,256]{1,0:T(8,128)(2,1)S(1)}, u32[]{:S(2)}, u32[]{:S(2)}) %collective-permute-start.5) | collective-permute-done | bytes 131104 | tf_op jit(solution)/shard_map/ppermute | solution.py:15
  95.2 1.8 collective-permute-done.6
  97.1 3.2 %collective-permute-start.11 = (bf16[256,256]{1,0:T(8,128)(2,1)S(1)}, bf16[256,256]{1,0:T(8,128)(2,1)S(1)}, u32[]{:S(2)}, u32[]{:S(2)}) collective-permute-start(bf16[256,256]{1,0:T(8,128)(2,1)S(1)} %multiply_convert_fusion.1.refs_0_), channel_id=1, source_target_pairs={{3,0},{0,1},{1,2},{2,3},{7,4},{4,5},{5,6},{6,7},{11,8},{8,9},{9,10... | collective-permute-start | bytes 393224 | tf_op jit(solution)/shard_map/ppermute | solution.py:15
  100.3 5.5 %collective-permute-start.10 = (bf16[256,256]{1,0:T(8,128)(2,1)S(1)}, bf16[256,256]{1,0:T(8,128)(2,1)S(1)}, u32[]{:S(2)}, u32[]{:S(2)}) collective-permute-start(bf16[256,256]{1,0:T(8,128)(2,1)S(1)} %multiply_convert_fusion.1.refs_0_), channel_id=1, source_target_pairs={{2,0},{3,1},{0,2},{1,3},{6,4},{7,5},{4,6},{5,7},{10,8},{11,9},{8,1... | collective-permute-start | bytes 393224 | tf_op jit(solution)/shard_map/ppermute | solution.py:15
  105.8 2.0 %collective-permute-start.9 = (bf16[256,256]{1,0:T(8,128)(2,1)S(1)}, bf16[256,256]{1,0:T(8,128)(2,1)S(1)}, u32[]{:S(2)}, u32[]{:S(2)}) collective-permute-start(bf16[256,256]{1,0:T(8,128)(2,1)S(1)} %multiply_convert_fusion.1.refs_0_), channel_id=1, source_target_pairs={{1,0},{2,1},{3,2},{0,3},{5,4},{6,5},{7,6},{4,7},{9,8},{10,9},{11,1... | collective-permute-start | bytes 393224 | tf_op jit(solution)/shard_map/ppermute | solution.py:15
  107.8 3.8 %shard_map.106 = (f32[256,256]{1,0:T(8,128)S(1)}, bf16[256,256]{1,0:T(8,128)(2,1)S(1)}, bf16[256,256]{1,0:T(8,128)(2,1)S(1)}, bf16[256,256]{1,0:T(8,128)(2,1)S(1)}) custom-call(s32[1]{0:T(128)} %bitcast.20.own, bf16[256,1792]{1,0:T(8,128)(2,1)S(1)} %bitcast.95, bf16[1024,1792]{1,0:T(8,128)(2,1)} %bitcast.96), custom_call_target="tpu_custom_call" | custom-call | tf_op jit(solution)/shard_map/pallas_call | solution.py:90
  111.6 3.3 %collective-permute-start.12 = (bf16[256,256]{1,0:T(8,128)(2,1)S(1)}, bf16[256,256]{1,0:T(8,128)(2,1)S(1)}, u32[]{:S(2)}, u32[]{:S(2)}) collective-permute-start(bf16[256,256]{1,0:T(8,128)(2,1)S(1)} %get-tuple-element.31), channel_id=1, source_target_pairs={{3,0},{0,1},{1,2},{2,3},{7,4},{4,5},{5,6},{6,7},{11,8},{8,9},{9,10... | collective-permute-start | bytes 393224 | tf_op jit(solution)/shard_map/ppermute | solution.py:15
  115.0 1.9 collective-permute-start.13
  116.9 4.0 %collective-permute-start.14 = (bf16[256,256]{1,0:T(8,128)(2,1)S(1)}, bf16[256,256]{1,0:T(8,128)(2,1)S(1)}, u32[]{:S(2)}, u32[]{:S(2)}) collective-permute-start(bf16[256,256]{1,0:T(8,128)(2,1)S(1)} %get-tuple-element.33), channel_id=1, source_target_pairs={{1,0},{2,1},{3,2},{0,3},{5,4},{6,5},{7,6},{4,7},{9,8},{10,9},{11,1... | collective-permute-start | bytes 393224 | tf_op jit(solution)/shard_map/ppermute | solution.py:15
  120.9 3.8 %shard_map.105 = bf16[256,1792]{1,0:T(8,128)(2,1)} custom-call(s32[1]{0:T(128)} %bitcast.20.own, bf16[256,256]{1,0:T(8,128)(2,1)S(1)} %multiply_convert_fusion.1.refs_0_, bf16[256,256]{1,0:T(8,128)(2,1)S(1)} %collective-permute-done.9.refs_1_, bf16[256,256]{1,0:T(8,128)(2,1)S(1)} %collective-permute-done.10.refs_2_, ...), custom_call_target="tpu_custom_call" | custom-call | tf_op jit(solution)/shard_map/pallas_call | solution.py:90
  124.7 10.5 %all-to-all-start.2 = ((bf16[32,8,1792]{2,1,0:T(8,128)(2,1)}), bf16[32,8,1792]{2,1,0:T(8,128)(2,1)S(1)}, u32[]{:S(2)}, u32[]{:S(2)}) async-start(bf16[32,8,1792]{2,1,0:T(8,128)(2,1)} %bitcast.47), calls=%async_computation.2 | async-start | bytes 1835008 | tf_op jit(solution)/shard_map/all_to_all | solution.py:214
  135.3 5.0 %collective-permute-start.18 = (bf16[256,256]{1,0:T(8,128)(2,1)S(1)}, bf16[256,256]{1,0:T(8,128)(2,1)S(1)}, u32[]{:S(2)}, u32[]{:S(2)}) collective-permute-start(bf16[256,256]{1,0:T(8,128)(2,1)S(1)} %multiply_convert_fusion.refs_0_), channel_id=1, source_target_pairs={{3,0},{0,1},{1,2},{2,3},{7,4},{4,5},{5,6},{6,7},{11,8},{8,9},{9,10... | collective-permute-start | bytes 393224 | tf_op jit(solution)/shard_map/ppermute | solution.py:15
  140.3 1.9 collective-permute-start.17
  142.3 4.0 %collective-permute-start.16 = (bf16[256,256]{1,0:T(8,128)(2,1)S(1)}, bf16[256,256]{1,0:T(8,128)(2,1)S(1)}, u32[]{:S(2)}, u32[]{:S(2)}) collective-permute-start(bf16[256,256]{1,0:T(8,128)(2,1)S(1)} %multiply_convert_fusion.refs_0_), channel_id=1, source_target_pairs={{1,0},{2,1},{3,2},{0,3},{5,4},{6,5},{7,6},{4,7},{9,8},{10,9},{11,1... | collective-permute-start | bytes 393224 | tf_op jit(solution)/shard_map/ppermute | solution.py:15
  146.3 4.9 %collective-permute-done.17.refs_2_ = bf16[256,256]{1,0:T(8,128)(2,1)S(1)} collective-permute-done((bf16[256,256]{1,0:T(8,128)(2,1)S(1)}, bf16[256,256]{1,0:T(8,128)(2,1)S(1)}, u32[]{:S(2)}, u32[]{:S(2)}) %collective-permute-start.17) | collective-permute-done | bytes 131104 | tf_op jit(solution)/shard_map/ppermute | solution.py:15
  151.1 3.9 %shard_map.107 = bf16[256,1792]{1,0:T(8,128)(2,1)} custom-call(s32[1]{0:T(128)} %bitcast.20.own, bf16[256,256]{1,0:T(8,128)(2,1)S(1)} %multiply_convert_fusion.refs_0_, bf16[256,256]{1,0:T(8,128)(2,1)S(1)} %collective-permute-done.16.refs_1_, bf16[256,256]{1,0:T(8,128)(2,1)S(1)} %collective-permute-done.17.refs_2_, ...), custom_call_target="tpu_custom_call" | custom-call | tf_op jit(solution)/shard_map/pallas_call | solution.py:90
  155.1 1.7 all-to-all-done.2
  156.8 8.1 %all-to-all-start.3 = ((bf16[32,8,1792]{2,1,0:T(8,128)(2,1)}), bf16[32,8,1792]{2,1,0:T(8,128)(2,1)S(1)}, u32[]{:S(2)}, u32[]{:S(2)}) async-start(bf16[32,8,1792]{2,1,0:T(8,128)(2,1)} %bitcast.50), calls=%async_computation.3 | async-start | bytes 1835008 | tf_op jit(solution)/shard_map/all_to_all | solution.py:214
  165.4 4.1 %collective-permute-start.15 = (f32[16,1792]{1,0:T(8,128)S(1)}, f32[16,1792]{1,0:T(8,128)S(1)}, u32[]{:S(2)}, u32[]{:S(2)}) collective-permute-start(f32[16,1792]{1,0:T(8,128)S(1)} %slice.199), channel_id=1, source_target_pairs={{4,0},{0,4},{5,1},{1,5},{6,2},{2,6},{7,3},{3,7},{12,8},{8,12},{13,... | collective-permute-start | bytes 344072 | tf_op jit(solution)/shard_map/ppermute | solution.py:15
  169.5 17.0 %all-to-all-done.3 = bf16[32,8,1792]{2,1,0:T(8,128)(2,1)S(1)} async-done(((bf16[32,8,1792]{2,1,0:T(8,128)(2,1)}), bf16[32,8,1792]{2,1,0:T(8,128)(2,1)S(1)}, u32[]{:S(2)}, u32[]{:S(2)}) %all-to-all-start.3) | async-done | bytes 917536 | tf_op jit(solution)/shard_map/all_to_all | solution.py:214
  186.5 0.3 fusion.1
  186.8 6.9 %collective-permute-start.19 = (f32[16,1792]{1,0:T(8,128)S(1)}, f32[16,1792]{1,0:T(8,128)S(1)}, u32[]{:S(2)}, u32[]{:S(2)}) collective-permute-start(f32[16,1792]{1,0:T(8,128)S(1)} %slice.201), channel_id=1, source_target_pairs={{4,0},{0,4},{5,1},{1,5},{6,2},{2,6},{7,3},{3,7},{12,8},{8,12},{13,... | collective-permute-start | bytes 344072 | tf_op jit(solution)/shard_map/ppermute | solution.py:15
  193.7 0.6 fusion.20
  194.3 0.3 collective-permute-done.19
  194.6 0.6 fusion.21
  (48 shorter events, 2.4 us)
Async XLA Ops:
  0.6 42.3 %copy-start = (f32[1,16,8]{1,2,0:T(8,128)S(1)}, f32[1,16,8]{1,2,0:T(8,128)}, u32[]{:S(2)}) copy-start(f32[1,16,8]{1,2,0:T(8,128)} %param.14) | copy-start | bytes 1540
  0.6 42.3 %copy-start.1 = (f32[1,16,8]{1,2,0:T(8,128)S(1)}, f32[1,16,8]{1,2,0:T(8,128)}, u32[]{:S(2)}) copy-start(f32[1,16,8]{1,2,0:T(8,128)} %param.11) | copy-start | bytes 1540
  3.1 43.6 %copy-start.2 = (bf16[1,16,1792]{2,1,0:T(8,128)(2,1)S(1)}, bf16[1,16,1792]{2,1,0:T(8,128)(2,1)}, u32[]{:S(2)}) copy-start(bf16[1,16,1792]{2,1,0:T(8,128)(2,1)} %param.12) | copy-start | bytes 172036
  4.3 18.0 %collective-permute-start = (s32[16,16]{0,1:T(8,128)S(1)}, s32[16,16]{0,1:T(8,128)S(1)}, u32[]{:S(2)}, u32[]{:S(2)}) collective-permute-start(s32[16,16]{0,1:T(8,128)S(1)} %pad_add_fusion), channel_id=1, source_target_pairs={{4,0},{0,4},{5,1},{1,5},{6,2},{2,6},{7,3},{3,7},{12,8},{8,12},{13,... | collective-permute-start | bytes 3080 | tf_op jit(solution)/shard_map/ppermute | solution.py:15
  20.4 9.6 %collective-permute-start.2 = (bf16[16,1792]{1,0:T(8,128)(2,1)}, bf16[16,1792]{1,0:T(8,128)(2,1)S(1)}, u32[]{:S(2)}, u32[]{:S(2)}) collective-permute-start(bf16[16,1792]{1,0:T(8,128)(2,1)} %bitcast.104), channel_id=1, source_target_pairs={{768,0},{0,256},{256,512},{512,768},{769,1},{1,257},{257,513},{513... | collective-permute-start | bytes 172040 | tf_op jit(solution)/shard_map/ppermute | solution.py:15
  29.9 3.7 %collective-permute-start.3 = (bf16[16,1792]{1,0:T(8,128)(2,1)S(1)}, bf16[16,1792]{1,0:T(8,128)(2,1)S(1)}, u32[]{:S(2)}, u32[]{:S(2)}) collective-permute-start(bf16[16,1792]{1,0:T(8,128)(2,1)S(1)} %collective-permute-done.2), channel_id=1, source_target_pairs={{4,0},{0,4},{5,1},{1,5},{6,2},{2,6},{7,3},{3,7},{12,8},{8,12},{13,... | collective-permute-start | bytes 172040 | tf_op jit(solution)/shard_map/ppermute | solution.py:15
  35.1 30.1 %all-to-all-start = ((bf16[32,8,1792]{2,1,0:T(8,128)(2,1)}), bf16[32,8,1792]{2,1,0:T(8,128)(2,1)S(1)}, u32[]{:S(2)}, u32[]{:S(2)}) async-start(bf16[32,8,1792]{2,1,0:T(8,128)(2,1)} %bitcast.23), calls=%async_computation | async-start | bytes 1835008 | tf_op jit(solution)/shard_map/all_to_all | solution.py:214
  43.0 3.6 %collective-permute-start.1 = (f32[16,16]{0,1:T(8,128)S(1)}, f32[16,16]{0,1:T(8,128)S(1)}, u32[]{:S(2)}, u32[]{:S(2)}) collective-permute-start(f32[16,16]{0,1:T(8,128)S(1)} %pad_maximum_fusion), channel_id=1, source_target_pairs={{4,0},{0,4},{5,1},{1,5},{6,2},{2,6},{7,3},{3,7},{12,8},{8,12},{13,... | collective-permute-start | bytes 3080 | tf_op jit(solution)/shard_map/ppermute | solution.py:15
  46.6 9.2 %collective-permute-start.7 = (bf16[16,1792]{1,0:T(8,128)(2,1)S(1)}, bf16[16,1792]{1,0:T(8,128)(2,1)S(1)}, u32[]{:S(2)}, u32[]{:S(2)}) collective-permute-start(bf16[16,1792]{1,0:T(8,128)(2,1)S(1)} %bitcast.105), channel_id=1, source_target_pairs={{256,0},{512,256},{768,512},{0,768},{257,1},{513,257},{769,513},{1... | collective-permute-start | bytes 172040 | tf_op jit(solution)/shard_map/ppermute | solution.py:15
  55.8 3.7 %collective-permute-start.8 = (bf16[16,1792]{1,0:T(8,128)(2,1)S(1)}, bf16[16,1792]{1,0:T(8,128)(2,1)S(1)}, u32[]{:S(2)}, u32[]{:S(2)}) collective-permute-start(bf16[16,1792]{1,0:T(8,128)(2,1)S(1)} %collective-permute-done.7), channel_id=1, source_target_pairs={{4,0},{0,4},{5,1},{1,5},{6,2},{2,6},{7,3},{3,7},{12,8},{8,12},{13,... | collective-permute-start | bytes 172040 | tf_op jit(solution)/shard_map/ppermute | solution.py:15
  65.2 31.9 %all-to-all-start.1 = ((bf16[32,8,1792]{2,1,0:T(8,128)(2,1)}), bf16[32,8,1792]{2,1,0:T(8,128)(2,1)S(1)}, u32[]{:S(2)}, u32[]{:S(2)}) async-start(bf16[32,8,1792]{2,1,0:T(8,128)(2,1)} %bitcast.44), calls=%async_computation.1 | async-start | bytes 1835008 | tf_op jit(solution)/shard_map/all_to_all | solution.py:214
  77.1 12.5 %collective-permute-start.4 = (bf16[256,256]{1,0:T(8,128)(2,1)S(1)}, bf16[256,256]{1,0:T(8,128)(2,1)S(1)}, u32[]{:S(2)}, u32[]{:S(2)}) collective-permute-start(bf16[256,256]{1,0:T(8,128)(2,1)S(1)} %get-tuple-element.23), channel_id=1, source_target_pairs={{3,0},{0,1},{1,2},{2,3},{7,4},{4,5},{5,6},{6,7},{11,8},{8,9},{9,10... | collective-permute-start | bytes 393224 | tf_op jit(solution)/shard_map/ppermute | solution.py:15
  81.3 13.9 %collective-permute-start.5 = (bf16[256,256]{1,0:T(8,128)(2,1)S(1)}, bf16[256,256]{1,0:T(8,128)(2,1)S(1)}, u32[]{:S(2)}, u32[]{:S(2)}) collective-permute-start(bf16[256,256]{1,0:T(8,128)(2,1)S(1)} %get-tuple-element.24), channel_id=1, source_target_pairs={{2,0},{3,1},{0,2},{1,3},{6,4},{7,5},{4,6},{5,7},{10,8},{11,9},{8,1... | collective-permute-start | bytes 393224 | tf_op jit(solution)/shard_map/ppermute | solution.py:15
  87.6 9.4 %collective-permute-start.6 = (bf16[256,256]{1,0:T(8,128)(2,1)S(1)}, bf16[256,256]{1,0:T(8,128)(2,1)S(1)}, u32[]{:S(2)}, u32[]{:S(2)}) collective-permute-start(bf16[256,256]{1,0:T(8,128)(2,1)S(1)} %get-tuple-element.25), channel_id=1, source_target_pairs={{1,0},{2,1},{3,2},{0,3},{5,4},{6,5},{7,6},{4,7},{9,8},{10,9},{11,1... | collective-permute-start | bytes 393224 | tf_op jit(solution)/shard_map/ppermute | solution.py:15
  97.1 19.8 %collective-permute-start.11 = (bf16[256,256]{1,0:T(8,128)(2,1)S(1)}, bf16[256,256]{1,0:T(8,128)(2,1)S(1)}, u32[]{:S(2)}, u32[]{:S(2)}) collective-permute-start(bf16[256,256]{1,0:T(8,128)(2,1)S(1)} %multiply_convert_fusion.1.refs_0_), channel_id=1, source_target_pairs={{3,0},{0,1},{1,2},{2,3},{7,4},{4,5},{5,6},{6,7},{11,8},{8,9},{9,10... | collective-permute-start | bytes 393224 | tf_op jit(solution)/shard_map/ppermute | solution.py:15
  100.3 20.6 %collective-permute-start.10 = (bf16[256,256]{1,0:T(8,128)(2,1)S(1)}, bf16[256,256]{1,0:T(8,128)(2,1)S(1)}, u32[]{:S(2)}, u32[]{:S(2)}) collective-permute-start(bf16[256,256]{1,0:T(8,128)(2,1)S(1)} %multiply_convert_fusion.1.refs_0_), channel_id=1, source_target_pairs={{2,0},{3,1},{0,2},{1,3},{6,4},{7,5},{4,6},{5,7},{10,8},{11,9},{8,1... | collective-permute-start | bytes 393224 | tf_op jit(solution)/shard_map/ppermute | solution.py:15
  105.8 15.1 %collective-permute-start.9 = (bf16[256,256]{1,0:T(8,128)(2,1)S(1)}, bf16[256,256]{1,0:T(8,128)(2,1)S(1)}, u32[]{:S(2)}, u32[]{:S(2)}) collective-permute-start(bf16[256,256]{1,0:T(8,128)(2,1)S(1)} %multiply_convert_fusion.1.refs_0_), channel_id=1, source_target_pairs={{1,0},{2,1},{3,2},{0,3},{5,4},{6,5},{7,6},{4,7},{9,8},{10,9},{11,1... | collective-permute-start | bytes 393224 | tf_op jit(solution)/shard_map/ppermute | solution.py:15
  111.6 13.1 %collective-permute-start.12 = (bf16[256,256]{1,0:T(8,128)(2,1)S(1)}, bf16[256,256]{1,0:T(8,128)(2,1)S(1)}, u32[]{:S(2)}, u32[]{:S(2)}) collective-permute-start(bf16[256,256]{1,0:T(8,128)(2,1)S(1)} %get-tuple-element.31), channel_id=1, source_target_pairs={{3,0},{0,1},{1,2},{2,3},{7,4},{4,5},{5,6},{6,7},{11,8},{8,9},{9,10... | collective-permute-start | bytes 393224 | tf_op jit(solution)/shard_map/ppermute | solution.py:15
  115.0 9.8 %collective-permute-start.13 = (bf16[256,256]{1,0:T(8,128)(2,1)S(1)}, bf16[256,256]{1,0:T(8,128)(2,1)S(1)}, u32[]{:S(2)}, u32[]{:S(2)}) collective-permute-start(bf16[256,256]{1,0:T(8,128)(2,1)S(1)} %get-tuple-element.32), channel_id=1, source_target_pairs={{2,0},{3,1},{0,2},{1,3},{6,4},{7,5},{4,6},{5,7},{10,8},{11,9},{8,1... | collective-permute-start | bytes 393224 | tf_op jit(solution)/shard_map/ppermute | solution.py:15
  116.9 7.8 %collective-permute-start.14 = (bf16[256,256]{1,0:T(8,128)(2,1)S(1)}, bf16[256,256]{1,0:T(8,128)(2,1)S(1)}, u32[]{:S(2)}, u32[]{:S(2)}) collective-permute-start(bf16[256,256]{1,0:T(8,128)(2,1)S(1)} %get-tuple-element.33), channel_id=1, source_target_pairs={{1,0},{2,1},{3,2},{0,3},{5,4},{6,5},{7,6},{4,7},{9,8},{10,9},{11,1... | collective-permute-start | bytes 393224 | tf_op jit(solution)/shard_map/ppermute | solution.py:15
  124.7 32.1 %all-to-all-start.2 = ((bf16[32,8,1792]{2,1,0:T(8,128)(2,1)}), bf16[32,8,1792]{2,1,0:T(8,128)(2,1)S(1)}, u32[]{:S(2)}, u32[]{:S(2)}) async-start(bf16[32,8,1792]{2,1,0:T(8,128)(2,1)} %bitcast.47), calls=%async_computation.2 | async-start | bytes 1835008 | tf_op jit(solution)/shard_map/all_to_all | solution.py:214
  135.3 10.9 %collective-permute-start.18 = (bf16[256,256]{1,0:T(8,128)(2,1)S(1)}, bf16[256,256]{1,0:T(8,128)(2,1)S(1)}, u32[]{:S(2)}, u32[]{:S(2)}) collective-permute-start(bf16[256,256]{1,0:T(8,128)(2,1)S(1)} %multiply_convert_fusion.refs_0_), channel_id=1, source_target_pairs={{3,0},{0,1},{1,2},{2,3},{7,4},{4,5},{5,6},{6,7},{11,8},{8,9},{9,10... | collective-permute-start | bytes 393224 | tf_op jit(solution)/shard_map/ppermute | solution.py:15
  140.3 10.8 %collective-permute-start.17 = (bf16[256,256]{1,0:T(8,128)(2,1)S(1)}, bf16[256,256]{1,0:T(8,128)(2,1)S(1)}, u32[]{:S(2)}, u32[]{:S(2)}) collective-permute-start(bf16[256,256]{1,0:T(8,128)(2,1)S(1)} %multiply_convert_fusion.refs_0_), channel_id=1, source_target_pairs={{2,0},{3,1},{0,2},{1,3},{6,4},{7,5},{4,6},{5,7},{10,8},{11,9},{8,1... | collective-permute-start | bytes 393224 | tf_op jit(solution)/shard_map/ppermute | solution.py:15
  142.3 8.9 %collective-permute-start.16 = (bf16[256,256]{1,0:T(8,128)(2,1)S(1)}, bf16[256,256]{1,0:T(8,128)(2,1)S(1)}, u32[]{:S(2)}, u32[]{:S(2)}) collective-permute-start(bf16[256,256]{1,0:T(8,128)(2,1)S(1)} %multiply_convert_fusion.refs_0_), channel_id=1, source_target_pairs={{1,0},{2,1},{3,2},{0,3},{5,4},{6,5},{7,6},{4,7},{9,8},{10,9},{11,1... | collective-permute-start | bytes 393224 | tf_op jit(solution)/shard_map/ppermute | solution.py:15
  156.8 29.7 %all-to-all-start.3 = ((bf16[32,8,1792]{2,1,0:T(8,128)(2,1)}), bf16[32,8,1792]{2,1,0:T(8,128)(2,1)S(1)}, u32[]{:S(2)}, u32[]{:S(2)}) async-start(bf16[32,8,1792]{2,1,0:T(8,128)(2,1)} %bitcast.50), calls=%async_computation.3 | async-start | bytes 1835008 | tf_op jit(solution)/shard_map/all_to_all | solution.py:214
  165.4 28.3 %collective-permute-start.15 = (f32[16,1792]{1,0:T(8,128)S(1)}, f32[16,1792]{1,0:T(8,128)S(1)}, u32[]{:S(2)}, u32[]{:S(2)}) collective-permute-start(f32[16,1792]{1,0:T(8,128)S(1)} %slice.199), channel_id=1, source_target_pairs={{4,0},{0,4},{5,1},{1,5},{6,2},{2,6},{7,3},{3,7},{12,8},{8,12},{13,... | collective-permute-start | bytes 344072 | tf_op jit(solution)/shard_map/ppermute | solution.py:15
  186.8 7.8 %collective-permute-start.19 = (f32[16,1792]{1,0:T(8,128)S(1)}, f32[16,1792]{1,0:T(8,128)S(1)}, u32[]{:S(2)}, u32[]{:S(2)}) collective-permute-start(f32[16,1792]{1,0:T(8,128)S(1)} %slice.201), channel_id=1, source_target_pairs={{4,0},{0,4},{5,1},{1,5},{6,2},{2,6},{7,3},{3,7},{12,8},{8,12},{13,... | collective-permute-start | bytes 344072 | tf_op jit(solution)/shard_map/ppermute | solution.py:15

commit v5 on v4

--- a/solution.py
+++ b/solution.py
@@ -6,6 +6,7 @@
 from jax.sharding import Mesh, PartitionSpec as P
 
 CORES = 2
+LANES = 128
 VMEM_LIMIT = 48 * 1024 * 1024
 
 
@@ -196,8 +197,27 @@
     )
 
 
-def with_other_core(block):
-    return jnp.concatenate([block, passed_along(block, "core", 1)], axis=0)
+def labels(targets, probs, pieces):
+    fields = [targets.astype(jnp.bfloat16)]
+    for _ in range(pieces):
+        piece = lax.reduce_precision(probs, 8, 7)
+        fields.append(piece.astype(jnp.bfloat16))
+        probs = probs - piece
+    fields = jnp.concatenate(fields, axis=1)
+    return jnp.pad(fields, ((0, 0), (0, LANES - fields.shape[1])))
+
+
+def with_other_core(rows, label, top_count, pieces):
+    message = jnp.concatenate([rows, label], axis=1)
+    other = passed_along(message, "core", 1)
+    width = rows.shape[1]
+    both = jnp.concatenate([rows, other[:, :width]], axis=0)
+    label = jnp.concatenate([label, other[:, width:]], axis=0).astype(jnp.float32)
+    targets = label[:, :top_count].astype(jnp.int32)
+    probs = label[:, top_count : 2 * top_count]
+    for k in range(2, pieces + 1):
+        probs = probs + label[:, k * top_count : (k + 1) * top_count]
+    return both, targets, probs
 
 
 def shards(
@@ -219,30 +239,21 @@
         return (part[:tokens_here] + other).astype(jnp.bfloat16)
 
     arriving = passed_along(fwd_act[0], "section", 1)
-    targets = jnp.concatenate(
-        [
-            slot_targets(fwd_routes[0], experts, capacity),
-            slot_targets(bwd_routes[0], experts, capacity),
-        ],
-        axis=1,
-    )
-    targets = with_other_core(targets)
-    probs = with_other_core(jnp.concatenate([fwd_probs[0], bwd_probs[0]], axis=1))
     top_count = fwd_routes.shape[2]
-    table_fwd, shares_fwd = chip_tables(
-        targets[:, :top_count], probs[:, :top_count], rows, capacity
-    )
-    table_bwd, shares_bwd = chip_tables(
-        targets[:, top_count:], probs[:, top_count:], rows, capacity
-    )
-    slot_probs = jnp.sum(shares_bwd, axis=0)[:, None]
+    label_fwd = labels(slot_targets(fwd_routes[0], experts, capacity), fwd_probs[0], 2)
+    tokens_fwd, targets_fwd, probs_fwd = with_other_core(arriving, label_fwd, top_count, 2)
+    table_fwd, shares_fwd = chip_tables(targets_fwd, probs_fwd, rows, capacity)
     pick_fwd = jnp.concatenate(halves(shares_fwd), axis=0)
 
-    sent_fwd = contract_first(table_fwd, with_other_core(arriving)).astype(jnp.bfloat16)
+    sent_fwd = contract_first(table_fwd, tokens_fwd).astype(jnp.bfloat16)
     sent_fwd, grad_in = lax.optimization_barrier((sent_fwd, bwd_grad[0]))
     recv_fwd = to_experts(sent_fwd)
 
-    incoming = with_other_core(passed_along(grad_in, "section", -1))
+    label_bwd = labels(slot_targets(bwd_routes[0], experts, capacity), bwd_probs[0], 3)
+    incoming = passed_along(grad_in, "section", -1)
+    incoming, targets_bwd, probs_bwd = with_other_core(incoming, label_bwd, top_count, 3)
+    table_bwd, shares_bwd = chip_tables(targets_bwd, probs_bwd, rows, capacity)
+    slot_probs = jnp.sum(shares_bwd, axis=0)[:, None]
     sent_bwd = (slot_probs * contract_first(table_bwd, incoming)).astype(jnp.bfloat16)
     stash_own = turned_own(act_stash[0, 0])
     slope_own = silu_slope(stash_own.astype(jnp.float32))

time: 198 us -> 192 us (0.970)
  waiting for transfers between devices: 46.4 us -> 42.2 us
  starting transfers between devices: 122 us -> 118 us
    ppermute x20 -> x18, waiting for transfers between devices: 23.6 us -> 18.8 us  [passed_along(): return lax.ppermute(block, axis, route)]
    ppermute x20 -> x18, starting transfers between devices: 87.7 us -> 83.5 us  [passed_along(): return lax.ppermute(block, axis, route)]
    convert_element_type x0 -> x6, other arithmetic: none -> 2.11 us  [the longest x2 1.38 us: labels(): fields.append(piece.astype(jnp.bfloat16))]
  transfers between devices with their start and end apart: 24 -> 22, of which waited for: 11 -> 10; matrix products, arithmetic and copies ran while one was open for 2% -> 6% of each run, Pallas kernels for 8% -> 8%
where the time goes in v5:
time: 192 us; the launch traced here: 189 us
  starting transfers between devices  118 us (61%)
  waiting for transfers between devices  42.2 us (22%)
  Pallas kernels  15.2 us (8%)
  other arithmetic  6.1 us (3%)
  matrix products  3.58 us (2%)
  local copies, waits for them, and re-layouts  3.49 us (2%)
    ppermute x18, starting transfers between devices, passed_along(): return lax.ppermute(block, axis, route)  83.5 us
    all_to_all x4, starting transfers between devices, to_experts(): lax.all_to_all(block, 'chip', split_axis=0, concat_axis=0, tiled=True)  34.3 us
    all_to_all x4, waiting for transfers between devices, to_experts(): lax.all_to_all(block, 'chip', split_axis=0, concat_axis=0, tiled=True)  23.4 us
    ppermute x18, waiting for transfers between devices, passed_along(): return lax.ppermute(block, axis, route)  18.8 us
    pallas_call x4, Pallas kernels, streamed(): pl.pallas_call(kernel, out_shape=out_shape, in_specs=[pl.BlockSpec(memory...  15.2 us
  transfers between devices with their start and end apart: 22, of which 10 were waited for; matrix products, arithmetic and copies ran while one was open for 6% of the time, Pallas kernels for 8%

profile of v5, /device:TPU:1, one launch (start us, length us, event | category | flops | bytes accessed | tf_op | source)
XLA Modules:
  0.0 189.4 jit_solution(14290812834859160013)
XLA Ops:
  0.6 11.5 %collective-permute-start = (bf16[16,1792]{1,0:T(8,128)(2,1)}, bf16[16,1792]{1,0:T(8,128)(2,1)S(1)}, u32[]{:S(2)}, u32[]{:S(2)}) collective-permute-start(bf16[16,1792]{1,0:T(8,128)(2,1)} %bitcast.48), channel_id=1, source_target_pairs={{768,0},{0,256},{256,512},{512,768},{769,1},{1,257},{257,513},{513... | collective-permute-start | bytes 172040 | tf_op jit(solution)/shard_map/ppermute | solution.py:16
  12.1 0.7 reduce-precision_convert_fusion.3
  12.8 0.7 reduce-precision_convert_fusion.2
  13.5 0.8 copy.39
  14.3 0.8 copy.43
  16.4 0.7 fusion.72
  17.2 4.1 %collective-permute-done = bf16[16,1792]{1,0:T(8,128)(2,1)S(1)} collective-permute-done((bf16[16,1792]{1,0:T(8,128)(2,1)}, bf16[16,1792]{1,0:T(8,128)(2,1)S(1)}, u32[]{:S(2)}, u32[]{:S(2)}) %collective-permute-start) | collective-permute-done | bytes 57376 | tf_op jit(solution)/shard_map/ppermute | solution.py:16
  21.4 5.5 %collective-permute-start.1 = (bf16[16,1920]{1,0:T(8,128)(2,1)S(1)}, bf16[16,1920]{1,0:T(8,128)(2,1)S(1)}, u32[]{:S(2)}, u32[]{:S(2)}) collective-permute-start(bf16[16,1920]{1,0:T(8,128)(2,1)S(1)} %pad_maximum_fusion), channel_id=1, source_target_pairs={{4,0},{0,4},{5,1},{1,5},{6,2},{2,6},{7,3},{3,7},{12,8},{8,12},{13,... | collective-permute-start | bytes 184328 | tf_op jit(solution)/shard_map/ppermute | solution.py:16
  26.9 0.9 collective-permute-done.1
  28.2 1.5 convolution_convert_fusion
  29.7 7.5 %all-to-all-start = ((bf16[32,8,1792]{2,1,0:T(8,128)(2,1)}), bf16[32,8,1792]{2,1,0:T(8,128)(2,1)S(1)}, u32[]{:S(2)}, u32[]{:S(2)}) async-start(bf16[32,8,1792]{2,1,0:T(8,128)(2,1)} %bitcast.5), calls=%async_computation | async-start | bytes 1835008 | tf_op jit(solution)/shard_map/all_to_all | solution.py:234
  37.3 9.0 %collective-permute-start.5 = (bf16[16,1792]{1,0:T(8,128)(2,1)S(1)}, bf16[16,1792]{1,0:T(8,128)(2,1)S(1)}, u32[]{:S(2)}, u32[]{:S(2)}) collective-permute-start(bf16[16,1792]{1,0:T(8,128)(2,1)S(1)} %bitcast.49), channel_id=1, source_target_pairs={{256,0},{512,256},{768,512},{0,768},{257,1},{513,257},{769,513},{1... | collective-permute-start | bytes 172040 | tf_op jit(solution)/shard_map/ppermute | solution.py:16
  46.4 1.1 collective-permute-done.5
  47.5 3.4 %collective-permute-start.6 = (bf16[16,1920]{1,0:T(8,128)(2,1)S(1)}, bf16[16,1920]{1,0:T(8,128)(2,1)S(1)}, u32[]{:S(2)}, u32[]{:S(2)}) collective-permute-start(bf16[16,1920]{1,0:T(8,128)(2,1)S(1)} %pad_maximum_fusion.1), channel_id=1, source_target_pairs={{4,0},{0,4},{5,1},{1,5},{6,2},{2,6},{7,3},{3,7},{12,8},{8,12},{13,... | collective-permute-start | bytes 184328 | tf_op jit(solution)/shard_map/ppermute | solution.py:16
  50.9 1.0 fusion.9
  52.0 0.3 slice_reduce_fusion.15
  52.4 0.3 slice_reduce_fusion.14
  52.9 1.5 fusion
  54.4 5.1 %all-to-all-done = bf16[32,8,1792]{2,1,0:T(8,128)(2,1)S(1)} async-done(((bf16[32,8,1792]{2,1,0:T(8,128)(2,1)}), bf16[32,8,1792]{2,1,0:T(8,128)(2,1)S(1)}, u32[]{:S(2)}, u32[]{:S(2)}) %all-to-all-start) | async-done | bytes 917536 | tf_op jit(solution)/shard_map/all_to_all | solution.py:234
  59.5 8.2 %all-to-all-start.1 = ((bf16[32,8,1792]{2,1,0:T(8,128)(2,1)}), bf16[32,8,1792]{2,1,0:T(8,128)(2,1)S(1)}, u32[]{:S(2)}, u32[]{:S(2)}) async-start(bf16[32,8,1792]{2,1,0:T(8,128)(2,1)} %bitcast.12), calls=%async_computation.1 | async-start | bytes 1835008 | tf_op jit(solution)/shard_map/all_to_all | solution.py:234
  67.7 3.7 %shard_map.104 = (f32[256,256]{1,0:T(8,128)S(1)}, bf16[256,256]{1,0:T(8,128)(2,1)S(1)}, bf16[256,256]{1,0:T(8,128)(2,1)S(1)}, bf16[256,256]{1,0:T(8,128)(2,1)S(1)}) custom-call(s32[1]{0:T(128)} %bitcast.3.own, bf16[256,1792]{1,0:T(8,128)(2,1)S(1)} %bitcast.42, bf16[1792,1024]{1,0:T(8,128)(2,1)} %bitcast.46), custom_call_target="tpu_custom_call" | custom-call | tf_op jit(solution)/shard_map/pallas_call | solution.py:91
  71.4 4.1 %collective-permute-start.2 = (bf16[256,256]{1,0:T(8,128)(2,1)S(1)}, bf16[256,256]{1,0:T(8,128)(2,1)S(1)}, u32[]{:S(2)}, u32[]{:S(2)}) collective-permute-start(bf16[256,256]{1,0:T(8,128)(2,1)S(1)} %get-tuple-element.23), channel_id=1, source_target_pairs={{3,0},{0,1},{1,2},{2,3},{7,4},{4,5},{5,6},{6,7},{11,8},{8,9},{9,10... | collective-permute-start | bytes 393224 | tf_op jit(solution)/shard_map/ppermute | solution.py:16
  75.5 6.2 %collective-permute-start.3 = (bf16[256,256]{1,0:T(8,128)(2,1)S(1)}, bf16[256,256]{1,0:T(8,128)(2,1)S(1)}, u32[]{:S(2)}, u32[]{:S(2)}) collective-permute-start(bf16[256,256]{1,0:T(8,128)(2,1)S(1)} %get-tuple-element.24), channel_id=1, source_target_pairs={{2,0},{3,1},{0,2},{1,3},{6,4},{7,5},{4,6},{5,7},{10,8},{11,9},{8,1... | collective-permute-start | bytes 393224 | tf_op jit(solution)/shard_map/ppermute | solution.py:16
  81.7 2.0 %collective-permute-start.4 = (bf16[256,256]{1,0:T(8,128)(2,1)S(1)}, bf16[256,256]{1,0:T(8,128)(2,1)S(1)}, u32[]{:S(2)}, u32[]{:S(2)}) collective-permute-start(bf16[256,256]{1,0:T(8,128)(2,1)S(1)} %get-tuple-element.25), channel_id=1, source_target_pairs={{1,0},{2,1},{3,2},{0,3},{5,4},{6,5},{7,6},{4,7},{9,8},{10,9},{11,1... | collective-permute-start | bytes 393224 | tf_op jit(solution)/shard_map/ppermute | solution.py:16
  83.7 5.6 %collective-permute-done.3 = bf16[256,256]{1,0:T(8,128)(2,1)S(1)} collective-permute-done((bf16[256,256]{1,0:T(8,128)(2,1)S(1)}, bf16[256,256]{1,0:T(8,128)(2,1)S(1)}, u32[]{:S(2)}, u32[]{:S(2)}) %collective-permute-start.3) | collective-permute-done | bytes 131104 | tf_op jit(solution)/shard_map/ppermute | solution.py:16
  89.3 1.8 collective-permute-done.4
  91.3 3.2 %collective-permute-start.9 = (bf16[256,256]{1,0:T(8,128)(2,1)S(1)}, bf16[256,256]{1,0:T(8,128)(2,1)S(1)}, u32[]{:S(2)}, u32[]{:S(2)}) collective-permute-start(bf16[256,256]{1,0:T(8,128)(2,1)S(1)} %multiply_convert_fusion.1.refs_0_), channel_id=1, source_target_pairs={{3,0},{0,1},{1,2},{2,3},{7,4},{4,5},{5,6},{6,7},{11,8},{8,9},{9,10... | collective-permute-start | bytes 393224 | tf_op jit(solution)/shard_map/ppermute | solution.py:16
  94.5 5.5 %collective-permute-start.8 = (bf16[256,256]{1,0:T(8,128)(2,1)S(1)}, bf16[256,256]{1,0:T(8,128)(2,1)S(1)}, u32[]{:S(2)}, u32[]{:S(2)}) collective-permute-start(bf16[256,256]{1,0:T(8,128)(2,1)S(1)} %multiply_convert_fusion.1.refs_0_), channel_id=1, source_target_pairs={{2,0},{3,1},{0,2},{1,3},{6,4},{7,5},{4,6},{5,7},{10,8},{11,9},{8,1... | collective-permute-start | bytes 393224 | tf_op jit(solution)/shard_map/ppermute | solution.py:16
  100.0 2.0 %collective-permute-start.7 = (bf16[256,256]{1,0:T(8,128)(2,1)S(1)}, bf16[256,256]{1,0:T(8,128)(2,1)S(1)}, u32[]{:S(2)}, u32[]{:S(2)}) collective-permute-start(bf16[256,256]{1,0:T(8,128)(2,1)S(1)} %multiply_convert_fusion.1.refs_0_), channel_id=1, source_target_pairs={{1,0},{2,1},{3,2},{0,3},{5,4},{6,5},{7,6},{4,7},{9,8},{10,9},{11,1... | collective-permute-start | bytes 393224 | tf_op jit(solution)/shard_map/ppermute | solution.py:16
  101.9 3.8 %shard_map.106 = (f32[256,256]{1,0:T(8,128)S(1)}, bf16[256,256]{1,0:T(8,128)(2,1)S(1)}, bf16[256,256]{1,0:T(8,128)(2,1)S(1)}, bf16[256,256]{1,0:T(8,128)(2,1)S(1)}) custom-call(s32[1]{0:T(128)} %bitcast.3.own, bf16[256,1792]{1,0:T(8,128)(2,1)S(1)} %bitcast.43, bf16[1024,1792]{1,0:T(8,128)(2,1)} %bitcast.44), custom_call_target="tpu_custom_call" | custom-call | tf_op jit(solution)/shard_map/pallas_call | solution.py:91
  105.8 3.3 %collective-permute-start.10 = (bf16[256,256]{1,0:T(8,128)(2,1)S(1)}, bf16[256,256]{1,0:T(8,128)(2,1)S(1)}, u32[]{:S(2)}, u32[]{:S(2)}) collective-permute-start(bf16[256,256]{1,0:T(8,128)(2,1)S(1)} %get-tuple-element.31), channel_id=1, source_target_pairs={{3,0},{0,1},{1,2},{2,3},{7,4},{4,5},{5,6},{6,7},{11,8},{8,9},{9,10... | collective-permute-start | bytes 393224 | tf_op jit(solution)/shard_map/ppermute | solution.py:16
  109.1 1.9 %collective-permute-start.11 = (bf16[256,256]{1,0:T(8,128)(2,1)S(1)}, bf16[256,256]{1,0:T(8,128)(2,1)S(1)}, u32[]{:S(2)}, u32[]{:S(2)}) collective-permute-start(bf16[256,256]{1,0:T(8,128)(2,1)S(1)} %get-tuple-element.32), channel_id=1, source_target_pairs={{2,0},{3,1},{0,2},{1,3},{6,4},{7,5},{4,6},{5,7},{10,8},{11,9},{8,1... | collective-permute-start | bytes 393224 | tf_op jit(solution)/shard_map/ppermute | solution.py:16
  111.0 4.0 %collective-permute-start.12 = (bf16[256,256]{1,0:T(8,128)(2,1)S(1)}, bf16[256,256]{1,0:T(8,128)(2,1)S(1)}, u32[]{:S(2)}, u32[]{:S(2)}) collective-permute-start(bf16[256,256]{1,0:T(8,128)(2,1)S(1)} %get-tuple-element.33), channel_id=1, source_target_pairs={{1,0},{2,1},{3,2},{0,3},{5,4},{6,5},{7,6},{4,7},{9,8},{10,9},{11,1... | collective-permute-start | bytes 393224 | tf_op jit(solution)/shard_map/ppermute | solution.py:16
  115.1 3.8 %shard_map.105 = bf16[256,1792]{1,0:T(8,128)(2,1)} custom-call(s32[1]{0:T(128)} %bitcast.3.own, bf16[256,256]{1,0:T(8,128)(2,1)S(1)} %multiply_convert_fusion.1.refs_0_, bf16[256,256]{1,0:T(8,128)(2,1)S(1)} %collective-permute-done.7.refs_1_, bf16[256,256]{1,0:T(8,128)(2,1)S(1)} %collective-permute-done.8.refs_2_, ...), custom_call_target="tpu_custom_call" | custom-call | tf_op jit(solution)/shard_map/pallas_call | solution.py:91
  118.9 10.5 %all-to-all-start.2 = ((bf16[32,8,1792]{2,1,0:T(8,128)(2,1)}), bf16[32,8,1792]{2,1,0:T(8,128)(2,1)S(1)}, u32[]{:S(2)}, u32[]{:S(2)}) async-start(bf16[32,8,1792]{2,1,0:T(8,128)(2,1)} %bitcast.15), calls=%async_computation.2 | async-start | bytes 1835008 | tf_op jit(solution)/shard_map/all_to_all | solution.py:234
  129.5 5.0 %collective-permute-start.16 = (bf16[256,256]{1,0:T(8,128)(2,1)S(1)}, bf16[256,256]{1,0:T(8,128)(2,1)S(1)}, u32[]{:S(2)}, u32[]{:S(2)}) collective-permute-start(bf16[256,256]{1,0:T(8,128)(2,1)S(1)} %multiply_convert_fusion.refs_0_), channel_id=1, source_target_pairs={{3,0},{0,1},{1,2},{2,3},{7,4},{4,5},{5,6},{6,7},{11,8},{8,9},{9,10... | collective-permute-start | bytes 393224 | tf_op jit(solution)/shard_map/ppermute | solution.py:16
  134.5 1.9 %collective-permute-start.15 = (bf16[256,256]{1,0:T(8,128)(2,1)S(1)}, bf16[256,256]{1,0:T(8,128)(2,1)S(1)}, u32[]{:S(2)}, u32[]{:S(2)}) collective-permute-start(bf16[256,256]{1,0:T(8,128)(2,1)S(1)} %multiply_convert_fusion.refs_0_), channel_id=1, source_target_pairs={{2,0},{3,1},{0,2},{1,3},{6,4},{7,5},{4,6},{5,7},{10,8},{11,9},{8,1... | collective-permute-start | bytes 393224 | tf_op jit(solution)/shard_map/ppermute | solution.py:16
  136.4 4.0 %collective-permute-start.14 = (bf16[256,256]{1,0:T(8,128)(2,1)S(1)}, bf16[256,256]{1,0:T(8,128)(2,1)S(1)}, u32[]{:S(2)}, u32[]{:S(2)}) collective-permute-start(bf16[256,256]{1,0:T(8,128)(2,1)S(1)} %multiply_convert_fusion.refs_0_), channel_id=1, source_target_pairs={{1,0},{2,1},{3,2},{0,3},{5,4},{6,5},{7,6},{4,7},{9,8},{10,9},{11,1... | collective-permute-start | bytes 393224 | tf_op jit(solution)/shard_map/ppermute | solution.py:16
  140.4 4.9 %collective-permute-done.15.refs_2_ = bf16[256,256]{1,0:T(8,128)(2,1)S(1)} collective-permute-done((bf16[256,256]{1,0:T(8,128)(2,1)S(1)}, bf16[256,256]{1,0:T(8,128)(2,1)S(1)}, u32[]{:S(2)}, u32[]{:S(2)}) %collective-permute-start.15) | collective-permute-done | bytes 131104 | tf_op jit(solution)/shard_map/ppermute | solution.py:16
  145.3 3.9 %shard_map.107 = bf16[256,1792]{1,0:T(8,128)(2,1)} custom-call(s32[1]{0:T(128)} %bitcast.3.own, bf16[256,256]{1,0:T(8,128)(2,1)S(1)} %multiply_convert_fusion.refs_0_, bf16[256,256]{1,0:T(8,128)(2,1)S(1)} %collective-permute-done.14.refs_1_, bf16[256,256]{1,0:T(8,128)(2,1)S(1)} %collective-permute-done.15.refs_2_, ...), custom_call_target="tpu_custom_call" | custom-call | tf_op jit(solution)/shard_map/pallas_call | solution.py:91
  149.2 1.7 all-to-all-done.2
  150.9 8.1 %all-to-all-start.3 = ((bf16[32,8,1792]{2,1,0:T(8,128)(2,1)}), bf16[32,8,1792]{2,1,0:T(8,128)(2,1)S(1)}, u32[]{:S(2)}, u32[]{:S(2)}) async-start(bf16[32,8,1792]{2,1,0:T(8,128)(2,1)} %bitcast.18), calls=%async_computation.3 | async-start | bytes 1835008 | tf_op jit(solution)/shard_map/all_to_all | solution.py:234
  159.1 0.3 slice_reduce_fusion.30
  159.9 4.1 %collective-permute-start.13 = (f32[16,1792]{1,0:T(8,128)S(1)}, f32[16,1792]{1,0:T(8,128)S(1)}, u32[]{:S(2)}, u32[]{:S(2)}) collective-permute-start(f32[16,1792]{1,0:T(8,128)S(1)} %slice.242), channel_id=1, source_target_pairs={{4,0},{0,4},{5,1},{1,5},{6,2},{2,6},{7,3},{3,7},{12,8},{8,12},{13,... | collective-permute-start | bytes 344072 | tf_op jit(solution)/shard_map/ppermute | solution.py:16
  164.1 16.6 %all-to-all-done.3 = bf16[32,8,1792]{2,1,0:T(8,128)(2,1)S(1)} async-done(((bf16[32,8,1792]{2,1,0:T(8,128)(2,1)}), bf16[32,8,1792]{2,1,0:T(8,128)(2,1)S(1)}, u32[]{:S(2)}, u32[]{:S(2)}) %all-to-all-start.3) | async-done | bytes 917536 | tf_op jit(solution)/shard_map/all_to_all | solution.py:234
  180.9 6.9 %collective-permute-start.17 = (f32[16,1792]{1,0:T(8,128)S(1)}, f32[16,1792]{1,0:T(8,128)S(1)}, u32[]{:S(2)}, u32[]{:S(2)}) collective-permute-start(f32[16,1792]{1,0:T(8,128)S(1)} %slice.244), channel_id=1, source_target_pairs={{4,0},{0,4},{5,1},{1,5},{6,2},{2,6},{7,3},{3,7},{12,8},{8,12},{13,... | collective-permute-start | bytes 344072 | tf_op jit(solution)/shard_map/ppermute | solution.py:16
  187.9 0.6 fusion.20
  188.8 0.6 fusion.21
  (59 shorter events, 3.7 us)
Async XLA Ops:
  0.6 20.7 %collective-permute-start = (bf16[16,1792]{1,0:T(8,128)(2,1)}, bf16[16,1792]{1,0:T(8,128)(2,1)S(1)}, u32[]{:S(2)}, u32[]{:S(2)}) collective-permute-start(bf16[16,1792]{1,0:T(8,128)(2,1)} %bitcast.48), channel_id=1, source_target_pairs={{768,0},{0,256},{256,512},{512,768},{769,1},{1,257},{257,513},{513... | collective-permute-start | bytes 172040 | tf_op jit(solution)/shard_map/ppermute | solution.py:16
  15.8 21.4 %copy-start = (s32[1,16,8]{1,2,0:T(8,128)S(1)}, s32[1,16,8]{1,2,0:T(8,128)}, u32[]{:S(2)}) copy-start(s32[1,16,8]{1,2,0:T(8,128)} %param.13) | copy-start | bytes 1540
  15.8 21.5 %copy-start.1 = (bf16[1,16,1792]{2,1,0:T(8,128)(2,1)S(1)}, bf16[1,16,1792]{2,1,0:T(8,128)(2,1)}, u32[]{:S(2)}) copy-start(bf16[1,16,1792]{2,1,0:T(8,128)(2,1)} %param.12) | copy-start | bytes 172036
  21.4 6.4 %collective-permute-start.1 = (bf16[16,1920]{1,0:T(8,128)(2,1)S(1)}, bf16[16,1920]{1,0:T(8,128)(2,1)S(1)}, u32[]{:S(2)}, u32[]{:S(2)}) collective-permute-start(bf16[16,1920]{1,0:T(8,128)(2,1)S(1)} %pad_maximum_fusion), channel_id=1, source_target_pairs={{4,0},{0,4},{5,1},{1,5},{6,2},{2,6},{7,3},{3,7},{12,8},{8,12},{13,... | collective-permute-start | bytes 184328 | tf_op jit(solution)/shard_map/ppermute | solution.py:16
  29.7 29.8 %all-to-all-start = ((bf16[32,8,1792]{2,1,0:T(8,128)(2,1)}), bf16[32,8,1792]{2,1,0:T(8,128)(2,1)S(1)}, u32[]{:S(2)}, u32[]{:S(2)}) async-start(bf16[32,8,1792]{2,1,0:T(8,128)(2,1)} %bitcast.5), calls=%async_computation | async-start | bytes 1835008 | tf_op jit(solution)/shard_map/all_to_all | solution.py:234
  37.3 10.2 %collective-permute-start.5 = (bf16[16,1792]{1,0:T(8,128)(2,1)S(1)}, bf16[16,1792]{1,0:T(8,128)(2,1)S(1)}, u32[]{:S(2)}, u32[]{:S(2)}) collective-permute-start(bf16[16,1792]{1,0:T(8,128)(2,1)S(1)} %bitcast.49), channel_id=1, source_target_pairs={{256,0},{512,256},{768,512},{0,768},{257,1},{513,257},{769,513},{1... | collective-permute-start | bytes 172040 | tf_op jit(solution)/shard_map/ppermute | solution.py:16
  47.5 4.4 %collective-permute-start.6 = (bf16[16,1920]{1,0:T(8,128)(2,1)S(1)}, bf16[16,1920]{1,0:T(8,128)(2,1)S(1)}, u32[]{:S(2)}, u32[]{:S(2)}) collective-permute-start(bf16[16,1920]{1,0:T(8,128)(2,1)S(1)} %pad_maximum_fusion.1), channel_id=1, source_target_pairs={{4,0},{0,4},{5,1},{1,5},{6,2},{2,6},{7,3},{3,7},{12,8},{8,12},{13,... | collective-permute-start | bytes 184328 | tf_op jit(solution)/shard_map/ppermute | solution.py:16
  59.5 31.8 %all-to-all-start.1 = ((bf16[32,8,1792]{2,1,0:T(8,128)(2,1)}), bf16[32,8,1792]{2,1,0:T(8,128)(2,1)S(1)}, u32[]{:S(2)}, u32[]{:S(2)}) async-start(bf16[32,8,1792]{2,1,0:T(8,128)(2,1)} %bitcast.12), calls=%async_computation.1 | async-start | bytes 1835008 | tf_op jit(solution)/shard_map/all_to_all | solution.py:234
  71.4 12.3 %collective-permute-start.2 = (bf16[256,256]{1,0:T(8,128)(2,1)S(1)}, bf16[256,256]{1,0:T(8,128)(2,1)S(1)}, u32[]{:S(2)}, u32[]{:S(2)}) collective-permute-start(bf16[256,256]{1,0:T(8,128)(2,1)S(1)} %get-tuple-element.23), channel_id=1, source_target_pairs={{3,0},{0,1},{1,2},{2,3},{7,4},{4,5},{5,6},{6,7},{11,8},{8,9},{9,10... | collective-permute-start | bytes 393224 | tf_op jit(solution)/shard_map/ppermute | solution.py:16
  75.5 13.9 %collective-permute-start.3 = (bf16[256,256]{1,0:T(8,128)(2,1)S(1)}, bf16[256,256]{1,0:T(8,128)(2,1)S(1)}, u32[]{:S(2)}, u32[]{:S(2)}) collective-permute-start(bf16[256,256]{1,0:T(8,128)(2,1)S(1)} %get-tuple-element.24), channel_id=1, source_target_pairs={{2,0},{3,1},{0,2},{1,3},{6,4},{7,5},{4,6},{5,7},{10,8},{11,9},{8,1... | collective-permute-start | bytes 393224 | tf_op jit(solution)/shard_map/ppermute | solution.py:16
  81.7 9.4 %collective-permute-start.4 = (bf16[256,256]{1,0:T(8,128)(2,1)S(1)}, bf16[256,256]{1,0:T(8,128)(2,1)S(1)}, u32[]{:S(2)}, u32[]{:S(2)}) collective-permute-start(bf16[256,256]{1,0:T(8,128)(2,1)S(1)} %get-tuple-element.25), channel_id=1, source_target_pairs={{1,0},{2,1},{3,2},{0,3},{5,4},{6,5},{7,6},{4,7},{9,8},{10,9},{11,1... | collective-permute-start | bytes 393224 | tf_op jit(solution)/shard_map/ppermute | solution.py:16
  91.3 19.8 %collective-permute-start.9 = (bf16[256,256]{1,0:T(8,128)(2,1)S(1)}, bf16[256,256]{1,0:T(8,128)(2,1)S(1)}, u32[]{:S(2)}, u32[]{:S(2)}) collective-permute-start(bf16[256,256]{1,0:T(8,128)(2,1)S(1)} %multiply_convert_fusion.1.refs_0_), channel_id=1, source_target_pairs={{3,0},{0,1},{1,2},{2,3},{7,4},{4,5},{5,6},{6,7},{11,8},{8,9},{9,10... | collective-permute-start | bytes 393224 | tf_op jit(solution)/shard_map/ppermute | solution.py:16
  94.5 20.6 %collective-permute-start.8 = (bf16[256,256]{1,0:T(8,128)(2,1)S(1)}, bf16[256,256]{1,0:T(8,128)(2,1)S(1)}, u32[]{:S(2)}, u32[]{:S(2)}) collective-permute-start(bf16[256,256]{1,0:T(8,128)(2,1)S(1)} %multiply_convert_fusion.1.refs_0_), channel_id=1, source_target_pairs={{2,0},{3,1},{0,2},{1,3},{6,4},{7,5},{4,6},{5,7},{10,8},{11,9},{8,1... | collective-permute-start | bytes 393224 | tf_op jit(solution)/shard_map/ppermute | solution.py:16
  100.0 15.1 %collective-permute-start.7 = (bf16[256,256]{1,0:T(8,128)(2,1)S(1)}, bf16[256,256]{1,0:T(8,128)(2,1)S(1)}, u32[]{:S(2)}, u32[]{:S(2)}) collective-permute-start(bf16[256,256]{1,0:T(8,128)(2,1)S(1)} %multiply_convert_fusion.1.refs_0_), channel_id=1, source_target_pairs={{1,0},{2,1},{3,2},{0,3},{5,4},{6,5},{7,6},{4,7},{9,8},{10,9},{11,1... | collective-permute-start | bytes 393224 | tf_op jit(solution)/shard_map/ppermute | solution.py:16
  105.8 13.1 %collective-permute-start.10 = (bf16[256,256]{1,0:T(8,128)(2,1)S(1)}, bf16[256,256]{1,0:T(8,128)(2,1)S(1)}, u32[]{:S(2)}, u32[]{:S(2)}) collective-permute-start(bf16[256,256]{1,0:T(8,128)(2,1)S(1)} %get-tuple-element.31), channel_id=1, source_target_pairs={{3,0},{0,1},{1,2},{2,3},{7,4},{4,5},{5,6},{6,7},{11,8},{8,9},{9,10... | collective-permute-start | bytes 393224 | tf_op jit(solution)/shard_map/ppermute | solution.py:16
  109.1 9.7 %collective-permute-start.11 = (bf16[256,256]{1,0:T(8,128)(2,1)S(1)}, bf16[256,256]{1,0:T(8,128)(2,1)S(1)}, u32[]{:S(2)}, u32[]{:S(2)}) collective-permute-start(bf16[256,256]{1,0:T(8,128)(2,1)S(1)} %get-tuple-element.32), channel_id=1, source_target_pairs={{2,0},{3,1},{0,2},{1,3},{6,4},{7,5},{4,6},{5,7},{10,8},{11,9},{8,1... | collective-permute-start | bytes 393224 | tf_op jit(solution)/shard_map/ppermute | solution.py:16
  111.0 7.8 %collective-permute-start.12 = (bf16[256,256]{1,0:T(8,128)(2,1)S(1)}, bf16[256,256]{1,0:T(8,128)(2,1)S(1)}, u32[]{:S(2)}, u32[]{:S(2)}) collective-permute-start(bf16[256,256]{1,0:T(8,128)(2,1)S(1)} %get-tuple-element.33), channel_id=1, source_target_pairs={{1,0},{2,1},{3,2},{0,3},{5,4},{6,5},{7,6},{4,7},{9,8},{10,9},{11,1... | collective-permute-start | bytes 393224 | tf_op jit(solution)/shard_map/ppermute | solution.py:16
  118.9 32.1 %all-to-all-start.2 = ((bf16[32,8,1792]{2,1,0:T(8,128)(2,1)}), bf16[32,8,1792]{2,1,0:T(8,128)(2,1)S(1)}, u32[]{:S(2)}, u32[]{:S(2)}) async-start(bf16[32,8,1792]{2,1,0:T(8,128)(2,1)} %bitcast.15), calls=%async_computation.2 | async-start | bytes 1835008 | tf_op jit(solution)/shard_map/all_to_all | solution.py:234
  129.5 10.9 %collective-permute-start.16 = (bf16[256,256]{1,0:T(8,128)(2,1)S(1)}, bf16[256,256]{1,0:T(8,128)(2,1)S(1)}, u32[]{:S(2)}, u32[]{:S(2)}) collective-permute-start(bf16[256,256]{1,0:T(8,128)(2,1)S(1)} %multiply_convert_fusion.refs_0_), channel_id=1, source_target_pairs={{3,0},{0,1},{1,2},{2,3},{7,4},{4,5},{5,6},{6,7},{11,8},{8,9},{9,10... | collective-permute-start | bytes 393224 | tf_op jit(solution)/shard_map/ppermute | solution.py:16
  134.5 10.8 %collective-permute-start.15 = (bf16[256,256]{1,0:T(8,128)(2,1)S(1)}, bf16[256,256]{1,0:T(8,128)(2,1)S(1)}, u32[]{:S(2)}, u32[]{:S(2)}) collective-permute-start(bf16[256,256]{1,0:T(8,128)(2,1)S(1)} %multiply_convert_fusion.refs_0_), channel_id=1, source_target_pairs={{2,0},{3,1},{0,2},{1,3},{6,4},{7,5},{4,6},{5,7},{10,8},{11,9},{8,1... | collective-permute-start | bytes 393224 | tf_op jit(solution)/shard_map/ppermute | solution.py:16
  136.4 8.9 %collective-permute-start.14 = (bf16[256,256]{1,0:T(8,128)(2,1)S(1)}, bf16[256,256]{1,0:T(8,128)(2,1)S(1)}, u32[]{:S(2)}, u32[]{:S(2)}) collective-permute-start(bf16[256,256]{1,0:T(8,128)(2,1)S(1)} %multiply_convert_fusion.refs_0_), channel_id=1, source_target_pairs={{1,0},{2,1},{3,2},{0,3},{5,4},{6,5},{7,6},{4,7},{9,8},{10,9},{11,1... | collective-permute-start | bytes 393224 | tf_op jit(solution)/shard_map/ppermute | solution.py:16
  150.9 29.7 %all-to-all-start.3 = ((bf16[32,8,1792]{2,1,0:T(8,128)(2,1)}), bf16[32,8,1792]{2,1,0:T(8,128)(2,1)S(1)}, u32[]{:S(2)}, u32[]{:S(2)}) async-start(bf16[32,8,1792]{2,1,0:T(8,128)(2,1)} %bitcast.18), calls=%async_computation.3 | async-start | bytes 1835008 | tf_op jit(solution)/shard_map/all_to_all | solution.py:234
  159.9 27.9 %collective-permute-start.13 = (f32[16,1792]{1,0:T(8,128)S(1)}, f32[16,1792]{1,0:T(8,128)S(1)}, u32[]{:S(2)}, u32[]{:S(2)}) collective-permute-start(f32[16,1792]{1,0:T(8,128)S(1)} %slice.242), channel_id=1, source_target_pairs={{4,0},{0,4},{5,1},{1,5},{6,2},{2,6},{7,3},{3,7},{12,8},{8,12},{13,... | collective-permute-start | bytes 344072 | tf_op jit(solution)/shard_map/ppermute | solution.py:16
  180.9 7.8 %collective-permute-start.17 = (f32[16,1792]{1,0:T(8,128)S(1)}, f32[16,1792]{1,0:T(8,128)S(1)}, u32[]{:S(2)}, u32[]{:S(2)}) collective-permute-start(f32[16,1792]{1,0:T(8,128)S(1)} %slice.244), channel_id=1, source_target_pairs={{4,0},{0,4},{5,1},{1,5},{6,2},{2,6},{7,3},{3,7},{12,8},{8,12},{13,... | collective-permute-start | bytes 344072 | tf_op jit(solution)/shard_map/ppermute | solution.py:16

commit v6 on v5

--- a/solution.py
+++ b/solution.py
@@ -264,12 +264,12 @@
     pre_parts = hidden_blocks(recv_fwd, up_weight, 1)
     pre_own = added([pre_parts[0]] + to_others(pre_parts))
     hidden_own = jax.nn.silu(pre_own).astype(jnp.bfloat16)
-    hidden_own, recv_bwd = lax.optimization_barrier((hidden_own, recv_bwd))
     hidden_parts = [hidden_own] + from_others(hidden_own)
+    hidden_parts[2], recv_bwd = lax.optimization_barrier((hidden_parts[2], recv_bwd))
     back_parts = hidden_blocks(recv_bwd, down_weight, 0)
     back_parts = [back_parts[0]] + to_others(back_parts)
     out_rows = model_rows(hidden_parts, down_weight, 0)
-    out_rows, back_parts = lax.optimization_barrier((out_rows, back_parts))
+    out_rows, back_parts[1:3] = lax.optimization_barrier((out_rows, back_parts[1:3]))
     back_own = added(back_parts)
     back_fwd = to_experts(out_rows)
     grad_own = (back_own * slope_own).astype(jnp.bfloat16)
@@ -279,6 +279,7 @@
     both = matmul(pick_fwd, back_fwd)
     half = both.shape[0] // 2
     fwd_out = to_tokens(both[:half] + both[half:])
+    fwd_out, back_bwd = lax.optimization_barrier((fwd_out, back_bwd))
     bwd_out = to_tokens(matmul(table_bwd, back_bwd))
     return (fwd_out[None], bwd_out[None])
 

time: 192 us -> 195 us (1.016)
  waiting for transfers between devices: 42.2 us -> 46.7 us
    ppermute x18, waiting for transfers between devices: 18.8 us -> 32 us  [passed_along(): return lax.ppermute(block, axis, route)]
    all_to_all x4, waiting for transfers between devices: 23.4 us -> 14.7 us  [to_experts(): lax.all_to_all(block, 'chip', split_axis=0, concat_axis=0, tiled=True)]
  transfers between devices with their start and end apart: 22 -> 22, of which waited for: 10 -> 13; matrix products, arithmetic and copies ran while one was open for 6% -> 5% of each run, Pallas kernels for 8% -> 8%
where the time goes in v6:
time: 195 us; the launch traced here: 194 us
  starting transfers between devices  117 us (60%)
  waiting for transfers between devices  46.7 us (24%)
  Pallas kernels  15.2 us (8%)
  other arithmetic  6.08 us (3%)
  matrix products  3.57 us (2%)
  local copies, waits for them, and re-layouts  3.47 us (2%)
    ppermute x18, starting transfers between devices, passed_along(): return lax.ppermute(block, axis, route)  83.9 us
    all_to_all x4, starting transfers between devices, to_experts(): lax.all_to_all(block, 'chip', split_axis=0, concat_axis=0, tiled=True)  33.6 us
    ppermute x18, waiting for transfers between devices, passed_along(): return lax.ppermute(block, axis, route)  32 us
    pallas_call x4, Pallas kernels, streamed(): pl.pallas_call(kernel, out_shape=out_shape, in_specs=[pl.BlockSpec(memory...  15.2 us
    all_to_all x4, waiting for transfers between devices, to_experts(): lax.all_to_all(block, 'chip', split_axis=0, concat_axis=0, tiled=True)  14.7 us
  transfers between devices with their start and end apart: 22, of which 13 were waited for; matrix products, arithmetic and copies ran while one was open for 5% of the time, Pallas kernels for 8%

profile of v6, /device:TPU:1, one launch (start us, length us, event | category | flops | bytes accessed | tf_op | source)
XLA Modules:
  0.0 193.6 jit_solution(13189779668636007555)
XLA Ops:
  0.6 11.5 %collective-permute-start = (bf16[16,1792]{1,0:T(8,128)(2,1)}, bf16[16,1792]{1,0:T(8,128)(2,1)S(1)}, u32[]{:S(2)}, u32[]{:S(2)}) collective-permute-start(bf16[16,1792]{1,0:T(8,128)(2,1)} %bitcast.48), channel_id=1, source_target_pairs={{768,0},{0,256},{256,512},{512,768},{769,1},{1,257},{257,513},{513... | collective-permute-start | bytes 172040 | tf_op jit(solution)/shard_map/ppermute | solution.py:16
  12.1 0.7 reduce-precision_convert_fusion.3
  12.8 0.8 copy.39
  14.3 0.7 fusion.69
  15.0 0.7 reduce-precision_convert_fusion.2
  15.7 0.8 copy.43
  17.2 4.1 %collective-permute-done = bf16[16,1792]{1,0:T(8,128)(2,1)S(1)} collective-permute-done((bf16[16,1792]{1,0:T(8,128)(2,1)}, bf16[16,1792]{1,0:T(8,128)(2,1)S(1)}, u32[]{:S(2)}, u32[]{:S(2)}) %collective-permute-start) | collective-permute-done | bytes 57376 | tf_op jit(solution)/shard_map/ppermute | solution.py:16
  21.4 5.5 %collective-permute-start.1 = (bf16[16,1920]{1,0:T(8,128)(2,1)S(1)}, bf16[16,1920]{1,0:T(8,128)(2,1)S(1)}, u32[]{:S(2)}, u32[]{:S(2)}) collective-permute-start(bf16[16,1920]{1,0:T(8,128)(2,1)S(1)} %pad_maximum_fusion), channel_id=1, source_target_pairs={{4,0},{0,4},{5,1},{1,5},{6,2},{2,6},{7,3},{3,7},{12,8},{8,12},{13,... | collective-permute-start | bytes 184328 | tf_op jit(solution)/shard_map/ppermute | solution.py:16
  26.9 0.9 collective-permute-done.1
  28.2 1.5 convolution_convert_fusion
  29.7 7.6 %all-to-all-start = ((bf16[32,8,1792]{2,1,0:T(8,128)(2,1)}), bf16[32,8,1792]{2,1,0:T(8,128)(2,1)S(1)}, u32[]{:S(2)}, u32[]{:S(2)}) async-start(bf16[32,8,1792]{2,1,0:T(8,128)(2,1)} %bitcast.5), calls=%async_computation | async-start | bytes 1835008 | tf_op jit(solution)/shard_map/all_to_all | solution.py:234
  37.3 9.0 %collective-permute-start.7 = (bf16[16,1792]{1,0:T(8,128)(2,1)S(1)}, bf16[16,1792]{1,0:T(8,128)(2,1)S(1)}, u32[]{:S(2)}, u32[]{:S(2)}) collective-permute-start(bf16[16,1792]{1,0:T(8,128)(2,1)S(1)} %bitcast.49), channel_id=1, source_target_pairs={{256,0},{512,256},{768,512},{0,768},{257,1},{513,257},{769,513},{1... | collective-permute-start | bytes 172040 | tf_op jit(solution)/shard_map/ppermute | solution.py:16
  46.4 1.1 collective-permute-done.7
  47.5 3.4 %collective-permute-start.8 = (bf16[16,1920]{1,0:T(8,128)(2,1)S(1)}, bf16[16,1920]{1,0:T(8,128)(2,1)S(1)}, u32[]{:S(2)}, u32[]{:S(2)}) collective-permute-start(bf16[16,1920]{1,0:T(8,128)(2,1)S(1)} %pad_maximum_fusion.1), channel_id=1, source_target_pairs={{4,0},{0,4},{5,1},{1,5},{6,2},{2,6},{7,3},{3,7},{12,8},{8,12},{13,... | collective-permute-start | bytes 184328 | tf_op jit(solution)/shard_map/ppermute | solution.py:16
  50.9 1.0 fusion.7
  52.9 1.5 fusion
  54.4 5.1 %all-to-all-done = bf16[32,8,1792]{2,1,0:T(8,128)(2,1)S(1)} async-done(((bf16[32,8,1792]{2,1,0:T(8,128)(2,1)}), bf16[32,8,1792]{2,1,0:T(8,128)(2,1)S(1)}, u32[]{:S(2)}, u32[]{:S(2)}) %all-to-all-start) | async-done | bytes 917536 | tf_op jit(solution)/shard_map/all_to_all | solution.py:234
  59.5 8.2 %all-to-all-start.1 = ((bf16[32,8,1792]{2,1,0:T(8,128)(2,1)}), bf16[32,8,1792]{2,1,0:T(8,128)(2,1)S(1)}, u32[]{:S(2)}, u32[]{:S(2)}) async-start(bf16[32,8,1792]{2,1,0:T(8,128)(2,1)} %bitcast.12), calls=%async_computation.1 | async-start | bytes 1835008 | tf_op jit(solution)/shard_map/all_to_all | solution.py:234
  67.7 3.7 %shard_map.104 = (f32[256,256]{1,0:T(8,128)S(1)}, bf16[256,256]{1,0:T(8,128)(2,1)S(1)}, bf16[256,256]{1,0:T(8,128)(2,1)S(1)}, bf16[256,256]{1,0:T(8,128)(2,1)S(1)}) custom-call(s32[1]{0:T(128)} %bitcast.3.own, bf16[256,1792]{1,0:T(8,128)(2,1)S(1)} %bitcast.40, bf16[1792,1024]{1,0:T(8,128)(2,1)} %bitcast.44), custom_call_target="tpu_custom_call" | custom-call | tf_op jit(solution)/shard_map/pallas_call | solution.py:91
  71.4 8.1 %collective-permute-start.4 = (bf16[256,256]{1,0:T(8,128)(2,1)S(1)}, bf16[256,256]{1,0:T(8,128)(2,1)S(1)}, u32[]{:S(2)}, u32[]{:S(2)}) collective-permute-start(bf16[256,256]{1,0:T(8,128)(2,1)S(1)} %get-tuple-element.25), channel_id=1, source_target_pairs={{1,0},{2,1},{3,2},{0,3},{5,4},{6,5},{7,6},{4,7},{9,8},{10,9},{11,1... | collective-permute-start | bytes 393224 | tf_op jit(solution)/shard_map/ppermute | solution.py:16
  79.5 1.9 collective-permute-start.3
  81.5 2.2 %collective-permute-start.2 = (bf16[256,256]{1,0:T(8,128)(2,1)S(1)}, bf16[256,256]{1,0:T(8,128)(2,1)S(1)}, u32[]{:S(2)}, u32[]{:S(2)}) collective-permute-start(bf16[256,256]{1,0:T(8,128)(2,1)S(1)} %get-tuple-element.23), channel_id=1, source_target_pairs={{3,0},{0,1},{1,2},{2,3},{7,4},{4,5},{5,6},{6,7},{11,8},{8,9},{9,10... | collective-permute-start | bytes 393224 | tf_op jit(solution)/shard_map/ppermute | solution.py:16
  83.7 6.5 %collective-permute-done.3 = bf16[256,256]{1,0:T(8,128)(2,1)S(1)} collective-permute-done((bf16[256,256]{1,0:T(8,128)(2,1)S(1)}, bf16[256,256]{1,0:T(8,128)(2,1)S(1)}, u32[]{:S(2)}, u32[]{:S(2)}) %collective-permute-start.3) | collective-permute-done | bytes 131104 | tf_op jit(solution)/shard_map/ppermute | solution.py:16
  90.2 5.5 %collective-permute-start.6 = (bf16[256,256]{1,0:T(8,128)(2,1)S(1)}, bf16[256,256]{1,0:T(8,128)(2,1)S(1)}, u32[]{:S(2)}, u32[]{:S(2)}) collective-permute-start(bf16[256,256]{1,0:T(8,128)(2,1)S(1)} %multiply_convert_fusion.1.refs_0_), channel_id=1, source_target_pairs={{2,0},{3,1},{0,2},{1,3},{6,4},{7,5},{4,6},{5,7},{10,8},{11,9},{8,1... | collective-permute-start | bytes 393224 | tf_op jit(solution)/shard_map/ppermute | solution.py:16
  95.7 2.1 %collective-permute-start.5 = (bf16[256,256]{1,0:T(8,128)(2,1)S(1)}, bf16[256,256]{1,0:T(8,128)(2,1)S(1)}, u32[]{:S(2)}, u32[]{:S(2)}) collective-permute-start(bf16[256,256]{1,0:T(8,128)(2,1)S(1)} %multiply_convert_fusion.1.refs_0_), channel_id=1, source_target_pairs={{1,0},{2,1},{3,2},{0,3},{5,4},{6,5},{7,6},{4,7},{9,8},{10,9},{11,1... | collective-permute-start | bytes 393224 | tf_op jit(solution)/shard_map/ppermute | solution.py:16
  97.8 3.2 %collective-permute-start.9 = (bf16[256,256]{1,0:T(8,128)(2,1)S(1)}, bf16[256,256]{1,0:T(8,128)(2,1)S(1)}, u32[]{:S(2)}, u32[]{:S(2)}) collective-permute-start(bf16[256,256]{1,0:T(8,128)(2,1)S(1)} %multiply_convert_fusion.1.refs_0_), channel_id=1, source_target_pairs={{3,0},{0,1},{1,2},{2,3},{7,4},{4,5},{5,6},{6,7},{11,8},{8,9},{9,10... | collective-permute-start | bytes 393224 | tf_op jit(solution)/shard_map/ppermute | solution.py:16
  101.0 1.3 collective-permute-done.6.refs_2_
  102.4 3.8 %shard_map.106 = (f32[256,256]{1,0:T(8,128)S(1)}, bf16[256,256]{1,0:T(8,128)(2,1)S(1)}, bf16[256,256]{1,0:T(8,128)(2,1)S(1)}, bf16[256,256]{1,0:T(8,128)(2,1)S(1)}) custom-call(s32[1]{0:T(128)} %bitcast.3.own, bf16[256,1792]{1,0:T(8,128)(2,1)S(1)} %bitcast.41, bf16[1024,1792]{1,0:T(8,128)(2,1)} %bitcast.42), custom_call_target="tpu_custom_call" | custom-call | tf_op jit(solution)/shard_map/pallas_call | solution.py:91
  106.2 1.9 collective-permute-start.10
  108.1 2.8 %collective-permute-start.11 = (bf16[256,256]{1,0:T(8,128)(2,1)S(1)}, bf16[256,256]{1,0:T(8,128)(2,1)S(1)}, u32[]{:S(2)}, u32[]{:S(2)}) collective-permute-start(bf16[256,256]{1,0:T(8,128)(2,1)S(1)} %get-tuple-element.31), channel_id=1, source_target_pairs={{2,0},{3,1},{0,2},{1,3},{6,4},{7,5},{4,6},{5,7},{10,8},{11,9},{8,1... | collective-permute-start | bytes 393224 | tf_op jit(solution)/shard_map/ppermute | solution.py:16
  111.0 3.8 %shard_map.105 = bf16[256,1792]{1,0:T(8,128)(2,1)} custom-call(s32[1]{0:T(128)} %bitcast.3.own, bf16[256,256]{1,0:T(8,128)(2,1)S(1)} %multiply_convert_fusion.1.refs_0_, bf16[256,256]{1,0:T(8,128)(2,1)S(1)} %collective-permute-done.5.refs_1_, bf16[256,256]{1,0:T(8,128)(2,1)S(1)} %collective-permute-done.6.refs_2_, ...), custom_call_target="tpu_custom_call" | custom-call | tf_op jit(solution)/shard_map/pallas_call | solution.py:91
  114.8 5.5 %collective-permute-done.11 = bf16[256,256]{1,0:T(8,128)(2,1)S(1)} collective-permute-done((bf16[256,256]{1,0:T(8,128)(2,1)S(1)}, bf16[256,256]{1,0:T(8,128)(2,1)S(1)}, u32[]{:S(2)}, u32[]{:S(2)}) %collective-permute-start.11) | collective-permute-done | bytes 131104 | tf_op jit(solution)/shard_map/ppermute | solution.py:16
  120.3 8.8 %all-to-all-start.2 = ((bf16[32,8,1792]{2,1,0:T(8,128)(2,1)}), bf16[32,8,1792]{2,1,0:T(8,128)(2,1)S(1)}, u32[]{:S(2)}, u32[]{:S(2)}) async-start(bf16[32,8,1792]{2,1,0:T(8,128)(2,1)} %bitcast.15), calls=%async_computation.2 | async-start | bytes 1835008 | tf_op jit(solution)/shard_map/all_to_all | solution.py:234
  129.1 1.9 collective-permute-start.13
  131.0 3.8 %collective-permute-done.13 = bf16[256,256]{1,0:T(8,128)(2,1)S(1)} collective-permute-done((bf16[256,256]{1,0:T(8,128)(2,1)S(1)}, bf16[256,256]{1,0:T(8,128)(2,1)S(1)}, u32[]{:S(2)}, u32[]{:S(2)}) %collective-permute-start.13) | collective-permute-done | bytes 131104 | tf_op jit(solution)/shard_map/ppermute | solution.py:16
  134.8 4.0 %collective-permute-start.14 = (bf16[256,256]{1,0:T(8,128)(2,1)S(1)}, bf16[256,256]{1,0:T(8,128)(2,1)S(1)}, u32[]{:S(2)}, u32[]{:S(2)}) collective-permute-start(bf16[256,256]{1,0:T(8,128)(2,1)S(1)} %multiply_convert_fusion.refs_0_), channel_id=1, source_target_pairs={{1,0},{2,1},{3,2},{0,3},{5,4},{6,5},{7,6},{4,7},{9,8},{10,9},{11,1... | collective-permute-start | bytes 393224 | tf_op jit(solution)/shard_map/ppermute | solution.py:16
  138.9 1.9 collective-permute-start.15
  140.8 2.2 %collective-permute-start.16 = (bf16[256,256]{1,0:T(8,128)(2,1)S(1)}, bf16[256,256]{1,0:T(8,128)(2,1)S(1)}, u32[]{:S(2)}, u32[]{:S(2)}) collective-permute-start(bf16[256,256]{1,0:T(8,128)(2,1)S(1)} %multiply_convert_fusion.refs_0_), channel_id=1, source_target_pairs={{3,0},{0,1},{1,2},{2,3},{7,4},{4,5},{5,6},{6,7},{11,8},{8,9},{9,10... | collective-permute-start | bytes 393224 | tf_op jit(solution)/shard_map/ppermute | solution.py:16
  143.0 3.8 %collective-permute-done.15.refs_2_ = bf16[256,256]{1,0:T(8,128)(2,1)S(1)} collective-permute-done((bf16[256,256]{1,0:T(8,128)(2,1)S(1)}, bf16[256,256]{1,0:T(8,128)(2,1)S(1)}, u32[]{:S(2)}, u32[]{:S(2)}) %collective-permute-start.15) | collective-permute-done | bytes 131104 | tf_op jit(solution)/shard_map/ppermute | solution.py:16
  146.8 3.2 %collective-permute-done.16.refs_3_ = bf16[256,256]{1,0:T(8,128)(2,1)S(1)} collective-permute-done((bf16[256,256]{1,0:T(8,128)(2,1)S(1)}, bf16[256,256]{1,0:T(8,128)(2,1)S(1)}, u32[]{:S(2)}, u32[]{:S(2)}) %collective-permute-start.16) | collective-permute-done | bytes 131104 | tf_op jit(solution)/shard_map/ppermute | solution.py:16
  149.9 3.9 %shard_map.107 = bf16[256,1792]{1,0:T(8,128)(2,1)} custom-call(s32[1]{0:T(128)} %bitcast.3.own, bf16[256,256]{1,0:T(8,128)(2,1)S(1)} %multiply_convert_fusion.refs_0_, bf16[256,256]{1,0:T(8,128)(2,1)S(1)} %collective-permute-done.14.refs_1_, bf16[256,256]{1,0:T(8,128)(2,1)S(1)} %collective-permute-done.15.refs_2_, ...), custom_call_target="tpu_custom_call" | custom-call | tf_op jit(solution)/shard_map/pallas_call | solution.py:91
  153.9 9.1 %all-to-all-start.3 = ((bf16[32,8,1792]{2,1,0:T(8,128)(2,1)}), bf16[32,8,1792]{2,1,0:T(8,128)(2,1)S(1)}, u32[]{:S(2)}, u32[]{:S(2)}) async-start(bf16[32,8,1792]{2,1,0:T(8,128)(2,1)} %bitcast.17), calls=%async_computation.3 | async-start | bytes 1835008 | tf_op jit(solution)/shard_map/all_to_all | solution.py:234
  163.8 6.0 %collective-permute-start.12 = (f32[16,1792]{1,0:T(8,128)S(1)}, f32[16,1792]{1,0:T(8,128)S(1)}, u32[]{:S(2)}, u32[]{:S(2)}) collective-permute-start(f32[16,1792]{1,0:T(8,128)S(1)} %slice.242), channel_id=1, source_target_pairs={{4,0},{0,4},{5,1},{1,5},{6,2},{2,6},{7,3},{3,7},{12,8},{8,12},{13,... | collective-permute-start | bytes 344072 | tf_op jit(solution)/shard_map/ppermute | solution.py:16
  169.8 0.9 collective-permute-done.12
  170.7 0.6 fusion.9
  171.4 9.6 %all-to-all-done.3 = bf16[32,8,1792]{2,1,0:T(8,128)(2,1)S(1)} async-done(((bf16[32,8,1792]{2,1,0:T(8,128)(2,1)}), bf16[32,8,1792]{2,1,0:T(8,128)(2,1)S(1)}, u32[]{:S(2)}, u32[]{:S(2)}) %all-to-all-start.3) | async-done | bytes 917536 | tf_op jit(solution)/shard_map/all_to_all | solution.py:234
  181.3 10.7 %collective-permute-start.17 = (f32[16,1792]{1,0:T(8,128)S(1)}, f32[16,1792]{1,0:T(8,128)S(1)}, u32[]{:S(2)}, u32[]{:S(2)}) collective-permute-start(f32[16,1792]{1,0:T(8,128)S(1)} %slice.244), channel_id=1, source_target_pairs={{4,0},{0,4},{5,1},{1,5},{6,2},{2,6},{7,3},{3,7},{12,8},{8,12},{13,... | collective-permute-start | bytes 344072 | tf_op jit(solution)/shard_map/ppermute | solution.py:16
  192.0 0.9 collective-permute-done.17
  (59 shorter events, 4.9 us)
Async XLA Ops:
  0.6 20.7 %collective-permute-start = (bf16[16,1792]{1,0:T(8,128)(2,1)}, bf16[16,1792]{1,0:T(8,128)(2,1)S(1)}, u32[]{:S(2)}, u32[]{:S(2)}) collective-permute-start(bf16[16,1792]{1,0:T(8,128)(2,1)} %bitcast.48), channel_id=1, source_target_pairs={{768,0},{0,256},{256,512},{512,768},{769,1},{1,257},{257,513},{513... | collective-permute-start | bytes 172040 | tf_op jit(solution)/shard_map/ppermute | solution.py:16
  16.4 20.8 %copy-start = (s32[1,16,8]{1,2,0:T(8,128)S(1)}, s32[1,16,8]{1,2,0:T(8,128)}, u32[]{:S(2)}) copy-start(s32[1,16,8]{1,2,0:T(8,128)} %param.13) | copy-start | bytes 1540
  16.5 20.8 %copy-start.1 = (bf16[1,16,1792]{2,1,0:T(8,128)(2,1)S(1)}, bf16[1,16,1792]{2,1,0:T(8,128)(2,1)}, u32[]{:S(2)}) copy-start(bf16[1,16,1792]{2,1,0:T(8,128)(2,1)} %param.12) | copy-start | bytes 172036
  21.4 6.4 %collective-permute-start.1 = (bf16[16,1920]{1,0:T(8,128)(2,1)S(1)}, bf16[16,1920]{1,0:T(8,128)(2,1)S(1)}, u32[]{:S(2)}, u32[]{:S(2)}) collective-permute-start(bf16[16,1920]{1,0:T(8,128)(2,1)S(1)} %pad_maximum_fusion), channel_id=1, source_target_pairs={{4,0},{0,4},{5,1},{1,5},{6,2},{2,6},{7,3},{3,7},{12,8},{8,12},{13,... | collective-permute-start | bytes 184328 | tf_op jit(solution)/shard_map/ppermute | solution.py:16
  29.7 29.8 %all-to-all-start = ((bf16[32,8,1792]{2,1,0:T(8,128)(2,1)}), bf16[32,8,1792]{2,1,0:T(8,128)(2,1)S(1)}, u32[]{:S(2)}, u32[]{:S(2)}) async-start(bf16[32,8,1792]{2,1,0:T(8,128)(2,1)} %bitcast.5), calls=%async_computation | async-start | bytes 1835008 | tf_op jit(solution)/shard_map/all_to_all | solution.py:234
  37.3 10.2 %collective-permute-start.7 = (bf16[16,1792]{1,0:T(8,128)(2,1)S(1)}, bf16[16,1792]{1,0:T(8,128)(2,1)S(1)}, u32[]{:S(2)}, u32[]{:S(2)}) collective-permute-start(bf16[16,1792]{1,0:T(8,128)(2,1)S(1)} %bitcast.49), channel_id=1, source_target_pairs={{256,0},{512,256},{768,512},{0,768},{257,1},{513,257},{769,513},{1... | collective-permute-start | bytes 172040 | tf_op jit(solution)/shard_map/ppermute | solution.py:16
  47.5 4.4 %collective-permute-start.8 = (bf16[16,1920]{1,0:T(8,128)(2,1)S(1)}, bf16[16,1920]{1,0:T(8,128)(2,1)S(1)}, u32[]{:S(2)}, u32[]{:S(2)}) collective-permute-start(bf16[16,1920]{1,0:T(8,128)(2,1)S(1)} %pad_maximum_fusion.1), channel_id=1, source_target_pairs={{4,0},{0,4},{5,1},{1,5},{6,2},{2,6},{7,3},{3,7},{12,8},{8,12},{13,... | collective-permute-start | bytes 184328 | tf_op jit(solution)/shard_map/ppermute | solution.py:16
  59.5 41.5 %all-to-all-start.1 = ((bf16[32,8,1792]{2,1,0:T(8,128)(2,1)}), bf16[32,8,1792]{2,1,0:T(8,128)(2,1)S(1)}, u32[]{:S(2)}, u32[]{:S(2)}) async-start(bf16[32,8,1792]{2,1,0:T(8,128)(2,1)} %bitcast.12), calls=%async_computation.1 | async-start | bytes 1835008 | tf_op jit(solution)/shard_map/all_to_all | solution.py:234
  71.4 12.3 %collective-permute-start.4 = (bf16[256,256]{1,0:T(8,128)(2,1)S(1)}, bf16[256,256]{1,0:T(8,128)(2,1)S(1)}, u32[]{:S(2)}, u32[]{:S(2)}) collective-permute-start(bf16[256,256]{1,0:T(8,128)(2,1)S(1)} %get-tuple-element.25), channel_id=1, source_target_pairs={{1,0},{2,1},{3,2},{0,3},{5,4},{6,5},{7,6},{4,7},{9,8},{10,9},{11,1... | collective-permute-start | bytes 393224 | tf_op jit(solution)/shard_map/ppermute | solution.py:16
  79.5 10.6 %collective-permute-start.3 = (bf16[256,256]{1,0:T(8,128)(2,1)S(1)}, bf16[256,256]{1,0:T(8,128)(2,1)S(1)}, u32[]{:S(2)}, u32[]{:S(2)}) collective-permute-start(bf16[256,256]{1,0:T(8,128)(2,1)S(1)} %get-tuple-element.24), channel_id=1, source_target_pairs={{2,0},{3,1},{0,2},{1,3},{6,4},{7,5},{4,6},{5,7},{10,8},{11,9},{8,1... | collective-permute-start | bytes 393224 | tf_op jit(solution)/shard_map/ppermute | solution.py:16
  81.5 8.7 %collective-permute-start.2 = (bf16[256,256]{1,0:T(8,128)(2,1)S(1)}, bf16[256,256]{1,0:T(8,128)(2,1)S(1)}, u32[]{:S(2)}, u32[]{:S(2)}) collective-permute-start(bf16[256,256]{1,0:T(8,128)(2,1)S(1)} %get-tuple-element.23), channel_id=1, source_target_pairs={{3,0},{0,1},{1,2},{2,3},{7,4},{4,5},{5,6},{6,7},{11,8},{8,9},{9,10... | collective-permute-start | bytes 393224 | tf_op jit(solution)/shard_map/ppermute | solution.py:16
  90.2 12.1 %collective-permute-start.6 = (bf16[256,256]{1,0:T(8,128)(2,1)S(1)}, bf16[256,256]{1,0:T(8,128)(2,1)S(1)}, u32[]{:S(2)}, u32[]{:S(2)}) collective-permute-start(bf16[256,256]{1,0:T(8,128)(2,1)S(1)} %multiply_convert_fusion.1.refs_0_), channel_id=1, source_target_pairs={{2,0},{3,1},{0,2},{1,3},{6,4},{7,5},{4,6},{5,7},{10,8},{11,9},{8,1... | collective-permute-start | bytes 393224 | tf_op jit(solution)/shard_map/ppermute | solution.py:16
  95.7 15.2 %collective-permute-start.5 = (bf16[256,256]{1,0:T(8,128)(2,1)S(1)}, bf16[256,256]{1,0:T(8,128)(2,1)S(1)}, u32[]{:S(2)}, u32[]{:S(2)}) collective-permute-start(bf16[256,256]{1,0:T(8,128)(2,1)S(1)} %multiply_convert_fusion.1.refs_0_), channel_id=1, source_target_pairs={{1,0},{2,1},{3,2},{0,3},{5,4},{6,5},{7,6},{4,7},{9,8},{10,9},{11,1... | collective-permute-start | bytes 393224 | tf_op jit(solution)/shard_map/ppermute | solution.py:16
  97.8 13.2 %collective-permute-start.9 = (bf16[256,256]{1,0:T(8,128)(2,1)S(1)}, bf16[256,256]{1,0:T(8,128)(2,1)S(1)}, u32[]{:S(2)}, u32[]{:S(2)}) collective-permute-start(bf16[256,256]{1,0:T(8,128)(2,1)S(1)} %multiply_convert_fusion.1.refs_0_), channel_id=1, source_target_pairs={{3,0},{0,1},{1,2},{2,3},{7,4},{4,5},{5,6},{6,7},{11,8},{8,9},{9,10... | collective-permute-start | bytes 393224 | tf_op jit(solution)/shard_map/ppermute | solution.py:16
  106.2 8.6 %collective-permute-start.10 = (bf16[256,256]{1,0:T(8,128)(2,1)S(1)}, bf16[256,256]{1,0:T(8,128)(2,1)S(1)}, u32[]{:S(2)}, u32[]{:S(2)}) collective-permute-start(bf16[256,256]{1,0:T(8,128)(2,1)S(1)} %get-tuple-element.30), channel_id=1, source_target_pairs={{3,0},{0,1},{1,2},{2,3},{7,4},{4,5},{5,6},{6,7},{11,8},{8,9},{9,10... | collective-permute-start | bytes 393224 | tf_op jit(solution)/shard_map/ppermute | solution.py:16
  108.1 12.1 %collective-permute-start.11 = (bf16[256,256]{1,0:T(8,128)(2,1)S(1)}, bf16[256,256]{1,0:T(8,128)(2,1)S(1)}, u32[]{:S(2)}, u32[]{:S(2)}) collective-permute-start(bf16[256,256]{1,0:T(8,128)(2,1)S(1)} %get-tuple-element.31), channel_id=1, source_target_pairs={{2,0},{3,1},{0,2},{1,3},{6,4},{7,5},{4,6},{5,7},{10,8},{11,9},{8,1... | collective-permute-start | bytes 393224 | tf_op jit(solution)/shard_map/ppermute | solution.py:16
  120.3 33.6 %all-to-all-start.2 = ((bf16[32,8,1792]{2,1,0:T(8,128)(2,1)}), bf16[32,8,1792]{2,1,0:T(8,128)(2,1)S(1)}, u32[]{:S(2)}, u32[]{:S(2)}) async-start(bf16[32,8,1792]{2,1,0:T(8,128)(2,1)} %bitcast.15), calls=%async_computation.2 | async-start | bytes 1835008 | tf_op jit(solution)/shard_map/all_to_all | solution.py:234
  129.1 5.7 %collective-permute-start.13 = (bf16[256,256]{1,0:T(8,128)(2,1)S(1)}, bf16[256,256]{1,0:T(8,128)(2,1)S(1)}, u32[]{:S(2)}, u32[]{:S(2)}) collective-permute-start(bf16[256,256]{1,0:T(8,128)(2,1)S(1)} %get-tuple-element.36), channel_id=1, source_target_pairs={{1,0},{2,1},{3,2},{0,3},{5,4},{6,5},{7,6},{4,7},{9,8},{10,9},{11,1... | collective-permute-start | bytes 393224 | tf_op jit(solution)/shard_map/ppermute | solution.py:16
  134.8 8.2 %collective-permute-start.14 = (bf16[256,256]{1,0:T(8,128)(2,1)S(1)}, bf16[256,256]{1,0:T(8,128)(2,1)S(1)}, u32[]{:S(2)}, u32[]{:S(2)}) collective-permute-start(bf16[256,256]{1,0:T(8,128)(2,1)S(1)} %multiply_convert_fusion.refs_0_), channel_id=1, source_target_pairs={{1,0},{2,1},{3,2},{0,3},{5,4},{6,5},{7,6},{4,7},{9,8},{10,9},{11,1... | collective-permute-start | bytes 393224 | tf_op jit(solution)/shard_map/ppermute | solution.py:16
  138.9 7.9 %collective-permute-start.15 = (bf16[256,256]{1,0:T(8,128)(2,1)S(1)}, bf16[256,256]{1,0:T(8,128)(2,1)S(1)}, u32[]{:S(2)}, u32[]{:S(2)}) collective-permute-start(bf16[256,256]{1,0:T(8,128)(2,1)S(1)} %multiply_convert_fusion.refs_0_), channel_id=1, source_target_pairs={{2,0},{3,1},{0,2},{1,3},{6,4},{7,5},{4,6},{5,7},{10,8},{11,9},{8,1... | collective-permute-start | bytes 393224 | tf_op jit(solution)/shard_map/ppermute | solution.py:16
  140.8 9.2 %collective-permute-start.16 = (bf16[256,256]{1,0:T(8,128)(2,1)S(1)}, bf16[256,256]{1,0:T(8,128)(2,1)S(1)}, u32[]{:S(2)}, u32[]{:S(2)}) collective-permute-start(bf16[256,256]{1,0:T(8,128)(2,1)S(1)} %multiply_convert_fusion.refs_0_), channel_id=1, source_target_pairs={{3,0},{0,1},{1,2},{2,3},{7,4},{4,5},{5,6},{6,7},{11,8},{8,9},{9,10... | collective-permute-start | bytes 393224 | tf_op jit(solution)/shard_map/ppermute | solution.py:16
  153.9 27.1 %all-to-all-start.3 = ((bf16[32,8,1792]{2,1,0:T(8,128)(2,1)}), bf16[32,8,1792]{2,1,0:T(8,128)(2,1)S(1)}, u32[]{:S(2)}, u32[]{:S(2)}) async-start(bf16[32,8,1792]{2,1,0:T(8,128)(2,1)} %bitcast.17), calls=%async_computation.3 | async-start | bytes 1835008 | tf_op jit(solution)/shard_map/all_to_all | solution.py:234
  163.8 6.9 %collective-permute-start.12 = (f32[16,1792]{1,0:T(8,128)S(1)}, f32[16,1792]{1,0:T(8,128)S(1)}, u32[]{:S(2)}, u32[]{:S(2)}) collective-permute-start(f32[16,1792]{1,0:T(8,128)S(1)} %slice.242), channel_id=1, source_target_pairs={{4,0},{0,4},{5,1},{1,5},{6,2},{2,6},{7,3},{3,7},{12,8},{8,12},{13,... | collective-permute-start | bytes 344072 | tf_op jit(solution)/shard_map/ppermute | solution.py:16
  181.3 11.7 %collective-permute-start.17 = (f32[16,1792]{1,0:T(8,128)S(1)}, f32[16,1792]{1,0:T(8,128)S(1)}, u32[]{:S(2)}, u32[]{:S(2)}) collective-permute-start(f32[16,1792]{1,0:T(8,128)S(1)} %slice.244), channel_id=1, source_target_pairs={{4,0},{0,4},{5,1},{1,5},{6,2},{2,6},{7,3},{3,7},{12,8},{8,12},{13,... | collective-permute-start | bytes 344072 | tf_op jit(solution)/shard_map/ppermute | solution.py:16

commit v7 on v6

--- a/solution.py
+++ b/solution.py
@@ -269,7 +269,7 @@
     back_parts = hidden_blocks(recv_bwd, down_weight, 0)
     back_parts = [back_parts[0]] + to_others(back_parts)
     out_rows = model_rows(hidden_parts, down_weight, 0)
-    out_rows, back_parts[1:3] = lax.optimization_barrier((out_rows, back_parts[1:3]))
+    out_rows, back_parts = lax.optimization_barrier((out_rows, back_parts))
     back_own = added(back_parts)
     back_fwd = to_experts(out_rows)
     grad_own = (back_own * slope_own).astype(jnp.bfloat16)

time: 195 us -> 190 us (0.974)
  waiting for transfers between devices: 46.7 us -> 39.4 us
  starting transfers between devices: 117 us -> 120 us
    ppermute x18, waiting for transfers between devices: 32 us -> 23.9 us  [passed_along(): return lax.ppermute(block, axis, route)]
    ppermute x18, starting transfers between devices: 83.9 us -> 86.5 us  [passed_along(): return lax.ppermute(block, axis, route)]
  transfers between devices with their start and end apart: 22 -> 22, of which waited for: 13 -> 12; matrix products, arithmetic and copies ran while one was open for 5% -> 5% of each run, Pallas kernels for 8% -> 8%
where the time goes in v7:
time: 190 us; the launch traced here: 189 us
  starting transfers between devices  120 us (63%)
  waiting for transfers between devices  39.4 us (21%)
  Pallas kernels  15.2 us (8%)
  other arithmetic  6.09 us (3%)
  matrix products  3.57 us (2%)
  local copies, waits for them, and re-layouts  3.47 us (2%)
    ppermute x18, starting transfers between devices, passed_along(): return lax.ppermute(block, axis, route)  86.5 us
    all_to_all x4, starting transfers between devices, to_experts(): lax.all_to_all(block, 'chip', split_axis=0, concat_axis=0, tiled=True)  33.8 us
    ppermute x18, waiting for transfers between devices, passed_along(): return lax.ppermute(block, axis, route)  23.9 us
    all_to_all x4, waiting for transfers between devices, to_experts(): lax.all_to_all(block, 'chip', split_axis=0, concat_axis=0, tiled=True)  15.4 us
    pallas_call x4, Pallas kernels, streamed(): pl.pallas_call(kernel, out_shape=out_shape, in_specs=[pl.BlockSpec(memory...  15.2 us
  transfers between devices with their start and end apart: 22, of which 12 were waited for; matrix products, arithmetic and copies ran while one was open for 5% of the time, Pallas kernels for 8%

profile of v7, /device:TPU:1, one launch (start us, length us, event | category | flops | bytes accessed | tf_op | source)
XLA Modules:
  0.0 189.1 jit_solution(18375129055753810537)
XLA Ops:
  0.6 11.5 %collective-permute-start = (bf16[16,1792]{1,0:T(8,128)(2,1)}, bf16[16,1792]{1,0:T(8,128)(2,1)S(1)}, u32[]{:S(2)}, u32[]{:S(2)}) collective-permute-start(bf16[16,1792]{1,0:T(8,128)(2,1)} %bitcast.48), channel_id=1, source_target_pairs={{768,0},{0,256},{256,512},{512,768},{769,1},{1,257},{257,513},{513... | collective-permute-start | bytes 172040 | tf_op jit(solution)/shard_map/ppermute | solution.py:16
  12.1 0.7 reduce-precision_convert_fusion.3
  12.8 0.8 copy.39
  14.3 0.7 fusion.69
  15.0 0.7 reduce-precision_convert_fusion.2
  15.7 0.8 copy.43
  17.2 4.1 %collective-permute-done = bf16[16,1792]{1,0:T(8,128)(2,1)S(1)} collective-permute-done((bf16[16,1792]{1,0:T(8,128)(2,1)}, bf16[16,1792]{1,0:T(8,128)(2,1)S(1)}, u32[]{:S(2)}, u32[]{:S(2)}) %collective-permute-start) | collective-permute-done | bytes 57376 | tf_op jit(solution)/shard_map/ppermute | solution.py:16
  21.4 5.5 %collective-permute-start.1 = (bf16[16,1920]{1,0:T(8,128)(2,1)S(1)}, bf16[16,1920]{1,0:T(8,128)(2,1)S(1)}, u32[]{:S(2)}, u32[]{:S(2)}) collective-permute-start(bf16[16,1920]{1,0:T(8,128)(2,1)S(1)} %pad_maximum_fusion), channel_id=1, source_target_pairs={{4,0},{0,4},{5,1},{1,5},{6,2},{2,6},{7,3},{3,7},{12,8},{8,12},{13,... | collective-permute-start | bytes 184328 | tf_op jit(solution)/shard_map/ppermute | solution.py:16
  26.9 0.9 collective-permute-done.1
  28.2 1.5 convolution_convert_fusion
  29.7 7.6 %all-to-all-start = ((bf16[32,8,1792]{2,1,0:T(8,128)(2,1)}), bf16[32,8,1792]{2,1,0:T(8,128)(2,1)S(1)}, u32[]{:S(2)}, u32[]{:S(2)}) async-start(bf16[32,8,1792]{2,1,0:T(8,128)(2,1)} %bitcast.5), calls=%async_computation | async-start | bytes 1835008 | tf_op jit(solution)/shard_map/all_to_all | solution.py:234
  37.3 9.0 %collective-permute-start.7 = (bf16[16,1792]{1,0:T(8,128)(2,1)S(1)}, bf16[16,1792]{1,0:T(8,128)(2,1)S(1)}, u32[]{:S(2)}, u32[]{:S(2)}) collective-permute-start(bf16[16,1792]{1,0:T(8,128)(2,1)S(1)} %bitcast.49), channel_id=1, source_target_pairs={{256,0},{512,256},{768,512},{0,768},{257,1},{513,257},{769,513},{1... | collective-permute-start | bytes 172040 | tf_op jit(solution)/shard_map/ppermute | solution.py:16
  46.4 1.1 collective-permute-done.7
  47.5 3.4 %collective-permute-start.8 = (bf16[16,1920]{1,0:T(8,128)(2,1)S(1)}, bf16[16,1920]{1,0:T(8,128)(2,1)S(1)}, u32[]{:S(2)}, u32[]{:S(2)}) collective-permute-start(bf16[16,1920]{1,0:T(8,128)(2,1)S(1)} %pad_maximum_fusion.1), channel_id=1, source_target_pairs={{4,0},{0,4},{5,1},{1,5},{6,2},{2,6},{7,3},{3,7},{12,8},{8,12},{13,... | collective-permute-start | bytes 184328 | tf_op jit(solution)/shard_map/ppermute | solution.py:16
  50.9 1.0 fusion.7
  52.9 1.5 fusion
  54.4 5.1 %all-to-all-done = bf16[32,8,1792]{2,1,0:T(8,128)(2,1)S(1)} async-done(((bf16[32,8,1792]{2,1,0:T(8,128)(2,1)}), bf16[32,8,1792]{2,1,0:T(8,128)(2,1)S(1)}, u32[]{:S(2)}, u32[]{:S(2)}) %all-to-all-start) | async-done | bytes 917536 | tf_op jit(solution)/shard_map/all_to_all | solution.py:234
  59.5 8.2 %all-to-all-start.1 = ((bf16[32,8,1792]{2,1,0:T(8,128)(2,1)}), bf16[32,8,1792]{2,1,0:T(8,128)(2,1)S(1)}, u32[]{:S(2)}, u32[]{:S(2)}) async-start(bf16[32,8,1792]{2,1,0:T(8,128)(2,1)} %bitcast.12), calls=%async_computation.1 | async-start | bytes 1835008 | tf_op jit(solution)/shard_map/all_to_all | solution.py:234
  67.7 3.7 %shard_map.104 = (f32[256,256]{1,0:T(8,128)S(1)}, bf16[256,256]{1,0:T(8,128)(2,1)S(1)}, bf16[256,256]{1,0:T(8,128)(2,1)S(1)}, bf16[256,256]{1,0:T(8,128)(2,1)S(1)}) custom-call(s32[1]{0:T(128)} %bitcast.3.own, bf16[256,1792]{1,0:T(8,128)(2,1)S(1)} %bitcast.40, bf16[1792,1024]{1,0:T(8,128)(2,1)} %bitcast.44), custom_call_target="tpu_custom_call" | custom-call | tf_op jit(solution)/shard_map/pallas_call | solution.py:91
  71.4 8.1 %collective-permute-start.4 = (bf16[256,256]{1,0:T(8,128)(2,1)S(1)}, bf16[256,256]{1,0:T(8,128)(2,1)S(1)}, u32[]{:S(2)}, u32[]{:S(2)}) collective-permute-start(bf16[256,256]{1,0:T(8,128)(2,1)S(1)} %get-tuple-element.27), channel_id=1, source_target_pairs={{1,0},{2,1},{3,2},{0,3},{5,4},{6,5},{7,6},{4,7},{9,8},{10,9},{11,1... | collective-permute-start | bytes 393224 | tf_op jit(solution)/shard_map/ppermute | solution.py:16
  79.5 1.9 %collective-permute-start.3 = (bf16[256,256]{1,0:T(8,128)(2,1)S(1)}, bf16[256,256]{1,0:T(8,128)(2,1)S(1)}, u32[]{:S(2)}, u32[]{:S(2)}) collective-permute-start(bf16[256,256]{1,0:T(8,128)(2,1)S(1)} %get-tuple-element.26), channel_id=1, source_target_pairs={{2,0},{3,1},{0,2},{1,3},{6,4},{7,5},{4,6},{5,7},{10,8},{11,9},{8,1... | collective-permute-start | bytes 393224 | tf_op jit(solution)/shard_map/ppermute | solution.py:16
  81.5 2.2 %collective-permute-start.2 = (bf16[256,256]{1,0:T(8,128)(2,1)S(1)}, bf16[256,256]{1,0:T(8,128)(2,1)S(1)}, u32[]{:S(2)}, u32[]{:S(2)}) collective-permute-start(bf16[256,256]{1,0:T(8,128)(2,1)S(1)} %get-tuple-element.25), channel_id=1, source_target_pairs={{3,0},{0,1},{1,2},{2,3},{7,4},{4,5},{5,6},{6,7},{11,8},{8,9},{9,10... | collective-permute-start | bytes 393224 | tf_op jit(solution)/shard_map/ppermute | solution.py:16
  83.7 6.5 %collective-permute-done.3 = bf16[256,256]{1,0:T(8,128)(2,1)S(1)} collective-permute-done((bf16[256,256]{1,0:T(8,128)(2,1)S(1)}, bf16[256,256]{1,0:T(8,128)(2,1)S(1)}, u32[]{:S(2)}, u32[]{:S(2)}) %collective-permute-start.3) | collective-permute-done | bytes 131104 | tf_op jit(solution)/shard_map/ppermute | solution.py:16
  90.2 5.5 %collective-permute-start.6 = (bf16[256,256]{1,0:T(8,128)(2,1)S(1)}, bf16[256,256]{1,0:T(8,128)(2,1)S(1)}, u32[]{:S(2)}, u32[]{:S(2)}) collective-permute-start(bf16[256,256]{1,0:T(8,128)(2,1)S(1)} %multiply_convert_fusion.1.refs_0_), channel_id=1, source_target_pairs={{2,0},{3,1},{0,2},{1,3},{6,4},{7,5},{4,6},{5,7},{10,8},{11,9},{8,1... | collective-permute-start | bytes 393224 | tf_op jit(solution)/shard_map/ppermute | solution.py:16
  95.7 2.1 %collective-permute-start.5 = (bf16[256,256]{1,0:T(8,128)(2,1)S(1)}, bf16[256,256]{1,0:T(8,128)(2,1)S(1)}, u32[]{:S(2)}, u32[]{:S(2)}) collective-permute-start(bf16[256,256]{1,0:T(8,128)(2,1)S(1)} %multiply_convert_fusion.1.refs_0_), channel_id=1, source_target_pairs={{1,0},{2,1},{3,2},{0,3},{5,4},{6,5},{7,6},{4,7},{9,8},{10,9},{11,1... | collective-permute-start | bytes 393224 | tf_op jit(solution)/shard_map/ppermute | solution.py:16
  97.8 3.2 %collective-permute-start.9 = (bf16[256,256]{1,0:T(8,128)(2,1)S(1)}, bf16[256,256]{1,0:T(8,128)(2,1)S(1)}, u32[]{:S(2)}, u32[]{:S(2)}) collective-permute-start(bf16[256,256]{1,0:T(8,128)(2,1)S(1)} %multiply_convert_fusion.1.refs_0_), channel_id=1, source_target_pairs={{3,0},{0,1},{1,2},{2,3},{7,4},{4,5},{5,6},{6,7},{11,8},{8,9},{9,10... | collective-permute-start | bytes 393224 | tf_op jit(solution)/shard_map/ppermute | solution.py:16
  101.0 1.3 collective-permute-done.6.refs_2_
  102.4 3.8 %shard_map.106 = (f32[256,256]{1,0:T(8,128)S(1)}, bf16[256,256]{1,0:T(8,128)(2,1)S(1)}, bf16[256,256]{1,0:T(8,128)(2,1)S(1)}, bf16[256,256]{1,0:T(8,128)(2,1)S(1)}) custom-call(s32[1]{0:T(128)} %bitcast.3.own, bf16[256,1792]{1,0:T(8,128)(2,1)S(1)} %bitcast.41, bf16[1024,1792]{1,0:T(8,128)(2,1)} %bitcast.42), custom_call_target="tpu_custom_call" | custom-call | tf_op jit(solution)/shard_map/pallas_call | solution.py:91
  106.2 1.9 %collective-permute-start.10 = (bf16[256,256]{1,0:T(8,128)(2,1)S(1)}, bf16[256,256]{1,0:T(8,128)(2,1)S(1)}, u32[]{:S(2)}, u32[]{:S(2)}) collective-permute-start(bf16[256,256]{1,0:T(8,128)(2,1)S(1)} %get-tuple-element.33), channel_id=1, source_target_pairs={{3,0},{0,1},{1,2},{2,3},{7,4},{4,5},{5,6},{6,7},{11,8},{8,9},{9,10... | collective-permute-start | bytes 393224 | tf_op jit(solution)/shard_map/ppermute | solution.py:16
  108.1 2.8 %collective-permute-start.11 = (bf16[256,256]{1,0:T(8,128)(2,1)S(1)}, bf16[256,256]{1,0:T(8,128)(2,1)S(1)}, u32[]{:S(2)}, u32[]{:S(2)}) collective-permute-start(bf16[256,256]{1,0:T(8,128)(2,1)S(1)} %get-tuple-element.34), channel_id=1, source_target_pairs={{2,0},{3,1},{0,2},{1,3},{6,4},{7,5},{4,6},{5,7},{10,8},{11,9},{8,1... | collective-permute-start | bytes 393224 | tf_op jit(solution)/shard_map/ppermute | solution.py:16
  111.0 4.2 %collective-permute-start.12 = (bf16[256,256]{1,0:T(8,128)(2,1)S(1)}, bf16[256,256]{1,0:T(8,128)(2,1)S(1)}, u32[]{:S(2)}, u32[]{:S(2)}) collective-permute-start(bf16[256,256]{1,0:T(8,128)(2,1)S(1)} %get-tuple-element.35), channel_id=1, source_target_pairs={{1,0},{2,1},{3,2},{0,3},{5,4},{6,5},{7,6},{4,7},{9,8},{10,9},{11,1... | collective-permute-start | bytes 393224 | tf_op jit(solution)/shard_map/ppermute | solution.py:16
  115.2 3.8 %shard_map.105 = bf16[256,1792]{1,0:T(8,128)(2,1)} custom-call(s32[1]{0:T(128)} %bitcast.3.own, bf16[256,256]{1,0:T(8,128)(2,1)S(1)} %multiply_convert_fusion.1.refs_0_, bf16[256,256]{1,0:T(8,128)(2,1)S(1)} %collective-permute-done.5.refs_1_, bf16[256,256]{1,0:T(8,128)(2,1)S(1)} %collective-permute-done.6.refs_2_, ...), custom_call_target="tpu_custom_call" | custom-call | tf_op jit(solution)/shard_map/pallas_call | solution.py:91
  119.0 0.9 collective-permute-done.12
  120.0 9.0 %all-to-all-start.2 = ((bf16[32,8,1792]{2,1,0:T(8,128)(2,1)}), bf16[32,8,1792]{2,1,0:T(8,128)(2,1)S(1)}, u32[]{:S(2)}, u32[]{:S(2)}) async-start(bf16[32,8,1792]{2,1,0:T(8,128)(2,1)} %bitcast.15), calls=%async_computation.2 | async-start | bytes 1835008 | tf_op jit(solution)/shard_map/all_to_all | solution.py:234
  129.1 3.0 %collective-permute-start.14 = (bf16[256,256]{1,0:T(8,128)(2,1)S(1)}, bf16[256,256]{1,0:T(8,128)(2,1)S(1)}, u32[]{:S(2)}, u32[]{:S(2)}) collective-permute-start(bf16[256,256]{1,0:T(8,128)(2,1)S(1)} %multiply_convert_fusion.refs_0_), channel_id=1, source_target_pairs={{1,0},{2,1},{3,2},{0,3},{5,4},{6,5},{7,6},{4,7},{9,8},{10,9},{11,1... | collective-permute-start | bytes 393224 | tf_op jit(solution)/shard_map/ppermute | solution.py:16
  132.1 4.5 %collective-permute-start.15 = (bf16[256,256]{1,0:T(8,128)(2,1)S(1)}, bf16[256,256]{1,0:T(8,128)(2,1)S(1)}, u32[]{:S(2)}, u32[]{:S(2)}) collective-permute-start(bf16[256,256]{1,0:T(8,128)(2,1)S(1)} %multiply_convert_fusion.refs_0_), channel_id=1, source_target_pairs={{2,0},{3,1},{0,2},{1,3},{6,4},{7,5},{4,6},{5,7},{10,8},{11,9},{8,1... | collective-permute-start | bytes 393224 | tf_op jit(solution)/shard_map/ppermute | solution.py:16
  136.6 1.9 %collective-permute-start.16 = (bf16[256,256]{1,0:T(8,128)(2,1)S(1)}, bf16[256,256]{1,0:T(8,128)(2,1)S(1)}, u32[]{:S(2)}, u32[]{:S(2)}) collective-permute-start(bf16[256,256]{1,0:T(8,128)(2,1)S(1)} %multiply_convert_fusion.refs_0_), channel_id=1, source_target_pairs={{3,0},{0,1},{1,2},{2,3},{7,4},{4,5},{5,6},{6,7},{11,8},{8,9},{9,10... | collective-permute-start | bytes 393224 | tf_op jit(solution)/shard_map/ppermute | solution.py:16
  138.5 1.4 collective-permute-done.15.refs_2_
  139.9 5.8 %collective-permute-done.16.refs_3_ = bf16[256,256]{1,0:T(8,128)(2,1)S(1)} collective-permute-done((bf16[256,256]{1,0:T(8,128)(2,1)S(1)}, bf16[256,256]{1,0:T(8,128)(2,1)S(1)}, u32[]{:S(2)}, u32[]{:S(2)}) %collective-permute-start.16) | collective-permute-done | bytes 131104 | tf_op jit(solution)/shard_map/ppermute | solution.py:16
  145.7 3.9 %shard_map.107 = bf16[256,1792]{1,0:T(8,128)(2,1)} custom-call(s32[1]{0:T(128)} %bitcast.3.own, bf16[256,256]{1,0:T(8,128)(2,1)S(1)} %multiply_convert_fusion.refs_0_, bf16[256,256]{1,0:T(8,128)(2,1)S(1)} %collective-permute-done.14.refs_1_, bf16[256,256]{1,0:T(8,128)(2,1)S(1)} %collective-permute-done.15.refs_2_, ...), custom_call_target="tpu_custom_call" | custom-call | tf_op jit(solution)/shard_map/pallas_call | solution.py:91
  149.6 9.0 %all-to-all-start.3 = ((bf16[32,8,1792]{2,1,0:T(8,128)(2,1)}), bf16[32,8,1792]{2,1,0:T(8,128)(2,1)S(1)}, u32[]{:S(2)}, u32[]{:S(2)}) async-start(bf16[32,8,1792]{2,1,0:T(8,128)(2,1)} %bitcast.17), calls=%async_computation.3 | async-start | bytes 1835008 | tf_op jit(solution)/shard_map/all_to_all | solution.py:234
  159.6 5.7 %collective-permute-start.13 = (f32[16,1792]{1,0:T(8,128)S(1)}, f32[16,1792]{1,0:T(8,128)S(1)}, u32[]{:S(2)}, u32[]{:S(2)}) collective-permute-start(f32[16,1792]{1,0:T(8,128)S(1)} %slice.242), channel_id=1, source_target_pairs={{4,0},{0,4},{5,1},{1,5},{6,2},{2,6},{7,3},{3,7},{12,8},{8,12},{13,... | collective-permute-start | bytes 344072 | tf_op jit(solution)/shard_map/ppermute | solution.py:16
  165.2 0.9 collective-permute-done.13
  166.2 0.6 fusion.9
  166.8 10.3 %all-to-all-done.3 = bf16[32,8,1792]{2,1,0:T(8,128)(2,1)S(1)} async-done(((bf16[32,8,1792]{2,1,0:T(8,128)(2,1)}), bf16[32,8,1792]{2,1,0:T(8,128)(2,1)S(1)}, u32[]{:S(2)}, u32[]{:S(2)}) %all-to-all-start.3) | async-done | bytes 917536 | tf_op jit(solution)/shard_map/all_to_all | solution.py:234
  177.5 10.1 %collective-permute-start.17 = (f32[16,1792]{1,0:T(8,128)S(1)}, f32[16,1792]{1,0:T(8,128)S(1)}, u32[]{:S(2)}, u32[]{:S(2)}) collective-permute-start(f32[16,1792]{1,0:T(8,128)S(1)} %slice.244), channel_id=1, source_target_pairs={{4,0},{0,4},{5,1},{1,5},{6,2},{2,6},{7,3},{3,7},{12,8},{8,12},{13,... | collective-permute-start | bytes 344072 | tf_op jit(solution)/shard_map/ppermute | solution.py:16
  187.6 0.9 collective-permute-done.17
  188.5 0.6 fusion.18
  (59 shorter events, 4.3 us)
Async XLA Ops:
  0.6 20.7 %collective-permute-start = (bf16[16,1792]{1,0:T(8,128)(2,1)}, bf16[16,1792]{1,0:T(8,128)(2,1)S(1)}, u32[]{:S(2)}, u32[]{:S(2)}) collective-permute-start(bf16[16,1792]{1,0:T(8,128)(2,1)} %bitcast.48), channel_id=1, source_target_pairs={{768,0},{0,256},{256,512},{512,768},{769,1},{1,257},{257,513},{513... | collective-permute-start | bytes 172040 | tf_op jit(solution)/shard_map/ppermute | solution.py:16
  16.4 20.8 %copy-start = (s32[1,16,8]{1,2,0:T(8,128)S(1)}, s32[1,16,8]{1,2,0:T(8,128)}, u32[]{:S(2)}) copy-start(s32[1,16,8]{1,2,0:T(8,128)} %param.13) | copy-start | bytes 1540
  16.5 20.8 %copy-start.1 = (bf16[1,16,1792]{2,1,0:T(8,128)(2,1)S(1)}, bf16[1,16,1792]{2,1,0:T(8,128)(2,1)}, u32[]{:S(2)}) copy-start(bf16[1,16,1792]{2,1,0:T(8,128)(2,1)} %param.12) | copy-start | bytes 172036
  21.4 6.4 %collective-permute-start.1 = (bf16[16,1920]{1,0:T(8,128)(2,1)S(1)}, bf16[16,1920]{1,0:T(8,128)(2,1)S(1)}, u32[]{:S(2)}, u32[]{:S(2)}) collective-permute-start(bf16[16,1920]{1,0:T(8,128)(2,1)S(1)} %pad_maximum_fusion), channel_id=1, source_target_pairs={{4,0},{0,4},{5,1},{1,5},{6,2},{2,6},{7,3},{3,7},{12,8},{8,12},{13,... | collective-permute-start | bytes 184328 | tf_op jit(solution)/shard_map/ppermute | solution.py:16
  29.7 29.8 %all-to-all-start = ((bf16[32,8,1792]{2,1,0:T(8,128)(2,1)}), bf16[32,8,1792]{2,1,0:T(8,128)(2,1)S(1)}, u32[]{:S(2)}, u32[]{:S(2)}) async-start(bf16[32,8,1792]{2,1,0:T(8,128)(2,1)} %bitcast.5), calls=%async_computation | async-start | bytes 1835008 | tf_op jit(solution)/shard_map/all_to_all | solution.py:234
  37.3 10.2 %collective-permute-start.7 = (bf16[16,1792]{1,0:T(8,128)(2,1)S(1)}, bf16[16,1792]{1,0:T(8,128)(2,1)S(1)}, u32[]{:S(2)}, u32[]{:S(2)}) collective-permute-start(bf16[16,1792]{1,0:T(8,128)(2,1)S(1)} %bitcast.49), channel_id=1, source_target_pairs={{256,0},{512,256},{768,512},{0,768},{257,1},{513,257},{769,513},{1... | collective-permute-start | bytes 172040 | tf_op jit(solution)/shard_map/ppermute | solution.py:16
  47.5 4.4 %collective-permute-start.8 = (bf16[16,1920]{1,0:T(8,128)(2,1)S(1)}, bf16[16,1920]{1,0:T(8,128)(2,1)S(1)}, u32[]{:S(2)}, u32[]{:S(2)}) collective-permute-start(bf16[16,1920]{1,0:T(8,128)(2,1)S(1)} %pad_maximum_fusion.1), channel_id=1, source_target_pairs={{4,0},{0,4},{5,1},{1,5},{6,2},{2,6},{7,3},{3,7},{12,8},{8,12},{13,... | collective-permute-start | bytes 184328 | tf_op jit(solution)/shard_map/ppermute | solution.py:16
  59.5 41.5 %all-to-all-start.1 = ((bf16[32,8,1792]{2,1,0:T(8,128)(2,1)}), bf16[32,8,1792]{2,1,0:T(8,128)(2,1)S(1)}, u32[]{:S(2)}, u32[]{:S(2)}) async-start(bf16[32,8,1792]{2,1,0:T(8,128)(2,1)} %bitcast.12), calls=%async_computation.1 | async-start | bytes 1835008 | tf_op jit(solution)/shard_map/all_to_all | solution.py:234
  71.4 12.3 %collective-permute-start.4 = (bf16[256,256]{1,0:T(8,128)(2,1)S(1)}, bf16[256,256]{1,0:T(8,128)(2,1)S(1)}, u32[]{:S(2)}, u32[]{:S(2)}) collective-permute-start(bf16[256,256]{1,0:T(8,128)(2,1)S(1)} %get-tuple-element.27), channel_id=1, source_target_pairs={{1,0},{2,1},{3,2},{0,3},{5,4},{6,5},{7,6},{4,7},{9,8},{10,9},{11,1... | collective-permute-start | bytes 393224 | tf_op jit(solution)/shard_map/ppermute | solution.py:16
  79.5 10.6 %collective-permute-start.3 = (bf16[256,256]{1,0:T(8,128)(2,1)S(1)}, bf16[256,256]{1,0:T(8,128)(2,1)S(1)}, u32[]{:S(2)}, u32[]{:S(2)}) collective-permute-start(bf16[256,256]{1,0:T(8,128)(2,1)S(1)} %get-tuple-element.26), channel_id=1, source_target_pairs={{2,0},{3,1},{0,2},{1,3},{6,4},{7,5},{4,6},{5,7},{10,8},{11,9},{8,1... | collective-permute-start | bytes 393224 | tf_op jit(solution)/shard_map/ppermute | solution.py:16
  81.5 8.7 %collective-permute-start.2 = (bf16[256,256]{1,0:T(8,128)(2,1)S(1)}, bf16[256,256]{1,0:T(8,128)(2,1)S(1)}, u32[]{:S(2)}, u32[]{:S(2)}) collective-permute-start(bf16[256,256]{1,0:T(8,128)(2,1)S(1)} %get-tuple-element.25), channel_id=1, source_target_pairs={{3,0},{0,1},{1,2},{2,3},{7,4},{4,5},{5,6},{6,7},{11,8},{8,9},{9,10... | collective-permute-start | bytes 393224 | tf_op jit(solution)/shard_map/ppermute | solution.py:16
  90.2 12.1 %collective-permute-start.6 = (bf16[256,256]{1,0:T(8,128)(2,1)S(1)}, bf16[256,256]{1,0:T(8,128)(2,1)S(1)}, u32[]{:S(2)}, u32[]{:S(2)}) collective-permute-start(bf16[256,256]{1,0:T(8,128)(2,1)S(1)} %multiply_convert_fusion.1.refs_0_), channel_id=1, source_target_pairs={{2,0},{3,1},{0,2},{1,3},{6,4},{7,5},{4,6},{5,7},{10,8},{11,9},{8,1... | collective-permute-start | bytes 393224 | tf_op jit(solution)/shard_map/ppermute | solution.py:16
  95.7 19.5 %collective-permute-start.5 = (bf16[256,256]{1,0:T(8,128)(2,1)S(1)}, bf16[256,256]{1,0:T(8,128)(2,1)S(1)}, u32[]{:S(2)}, u32[]{:S(2)}) collective-permute-start(bf16[256,256]{1,0:T(8,128)(2,1)S(1)} %multiply_convert_fusion.1.refs_0_), channel_id=1, source_target_pairs={{1,0},{2,1},{3,2},{0,3},{5,4},{6,5},{7,6},{4,7},{9,8},{10,9},{11,1... | collective-permute-start | bytes 393224 | tf_op jit(solution)/shard_map/ppermute | solution.py:16
  97.8 17.4 %collective-permute-start.9 = (bf16[256,256]{1,0:T(8,128)(2,1)S(1)}, bf16[256,256]{1,0:T(8,128)(2,1)S(1)}, u32[]{:S(2)}, u32[]{:S(2)}) collective-permute-start(bf16[256,256]{1,0:T(8,128)(2,1)S(1)} %multiply_convert_fusion.1.refs_0_), channel_id=1, source_target_pairs={{3,0},{0,1},{1,2},{2,3},{7,4},{4,5},{5,6},{6,7},{11,8},{8,9},{9,10... | collective-permute-start | bytes 393224 | tf_op jit(solution)/shard_map/ppermute | solution.py:16
  106.2 12.8 %collective-permute-start.10 = (bf16[256,256]{1,0:T(8,128)(2,1)S(1)}, bf16[256,256]{1,0:T(8,128)(2,1)S(1)}, u32[]{:S(2)}, u32[]{:S(2)}) collective-permute-start(bf16[256,256]{1,0:T(8,128)(2,1)S(1)} %get-tuple-element.33), channel_id=1, source_target_pairs={{3,0},{0,1},{1,2},{2,3},{7,4},{4,5},{5,6},{6,7},{11,8},{8,9},{9,10... | collective-permute-start | bytes 393224 | tf_op jit(solution)/shard_map/ppermute | solution.py:16
  108.1 10.9 %collective-permute-start.11 = (bf16[256,256]{1,0:T(8,128)(2,1)S(1)}, bf16[256,256]{1,0:T(8,128)(2,1)S(1)}, u32[]{:S(2)}, u32[]{:S(2)}) collective-permute-start(bf16[256,256]{1,0:T(8,128)(2,1)S(1)} %get-tuple-element.34), channel_id=1, source_target_pairs={{2,0},{3,1},{0,2},{1,3},{6,4},{7,5},{4,6},{5,7},{10,8},{11,9},{8,1... | collective-permute-start | bytes 393224 | tf_op jit(solution)/shard_map/ppermute | solution.py:16
  111.0 9.0 %collective-permute-start.12 = (bf16[256,256]{1,0:T(8,128)(2,1)S(1)}, bf16[256,256]{1,0:T(8,128)(2,1)S(1)}, u32[]{:S(2)}, u32[]{:S(2)}) collective-permute-start(bf16[256,256]{1,0:T(8,128)(2,1)S(1)} %get-tuple-element.35), channel_id=1, source_target_pairs={{1,0},{2,1},{3,2},{0,3},{5,4},{6,5},{7,6},{4,7},{9,8},{10,9},{11,1... | collective-permute-start | bytes 393224 | tf_op jit(solution)/shard_map/ppermute | solution.py:16
  120.0 29.7 %all-to-all-start.2 = ((bf16[32,8,1792]{2,1,0:T(8,128)(2,1)}), bf16[32,8,1792]{2,1,0:T(8,128)(2,1)S(1)}, u32[]{:S(2)}, u32[]{:S(2)}) async-start(bf16[32,8,1792]{2,1,0:T(8,128)(2,1)} %bitcast.15), calls=%async_computation.2 | async-start | bytes 1835008 | tf_op jit(solution)/shard_map/all_to_all | solution.py:234
  129.1 9.4 %collective-permute-start.14 = (bf16[256,256]{1,0:T(8,128)(2,1)S(1)}, bf16[256,256]{1,0:T(8,128)(2,1)S(1)}, u32[]{:S(2)}, u32[]{:S(2)}) collective-permute-start(bf16[256,256]{1,0:T(8,128)(2,1)S(1)} %multiply_convert_fusion.refs_0_), channel_id=1, source_target_pairs={{1,0},{2,1},{3,2},{0,3},{5,4},{6,5},{7,6},{4,7},{9,8},{10,9},{11,1... | collective-permute-start | bytes 393224 | tf_op jit(solution)/shard_map/ppermute | solution.py:16
  132.1 7.9 %collective-permute-start.15 = (bf16[256,256]{1,0:T(8,128)(2,1)S(1)}, bf16[256,256]{1,0:T(8,128)(2,1)S(1)}, u32[]{:S(2)}, u32[]{:S(2)}) collective-permute-start(bf16[256,256]{1,0:T(8,128)(2,1)S(1)} %multiply_convert_fusion.refs_0_), channel_id=1, source_target_pairs={{2,0},{3,1},{0,2},{1,3},{6,4},{7,5},{4,6},{5,7},{10,8},{11,9},{8,1... | collective-permute-start | bytes 393224 | tf_op jit(solution)/shard_map/ppermute | solution.py:16
  136.6 9.1 %collective-permute-start.16 = (bf16[256,256]{1,0:T(8,128)(2,1)S(1)}, bf16[256,256]{1,0:T(8,128)(2,1)S(1)}, u32[]{:S(2)}, u32[]{:S(2)}) collective-permute-start(bf16[256,256]{1,0:T(8,128)(2,1)S(1)} %multiply_convert_fusion.refs_0_), channel_id=1, source_target_pairs={{3,0},{0,1},{1,2},{2,3},{7,4},{4,5},{5,6},{6,7},{11,8},{8,9},{9,10... | collective-permute-start | bytes 393224 | tf_op jit(solution)/shard_map/ppermute | solution.py:16
  149.6 27.5 %all-to-all-start.3 = ((bf16[32,8,1792]{2,1,0:T(8,128)(2,1)}), bf16[32,8,1792]{2,1,0:T(8,128)(2,1)S(1)}, u32[]{:S(2)}, u32[]{:S(2)}) async-start(bf16[32,8,1792]{2,1,0:T(8,128)(2,1)} %bitcast.17), calls=%async_computation.3 | async-start | bytes 1835008 | tf_op jit(solution)/shard_map/all_to_all | solution.py:234
  159.6 6.6 %collective-permute-start.13 = (f32[16,1792]{1,0:T(8,128)S(1)}, f32[16,1792]{1,0:T(8,128)S(1)}, u32[]{:S(2)}, u32[]{:S(2)}) collective-permute-start(f32[16,1792]{1,0:T(8,128)S(1)} %slice.242), channel_id=1, source_target_pairs={{4,0},{0,4},{5,1},{1,5},{6,2},{2,6},{7,3},{3,7},{12,8},{8,12},{13,... | collective-permute-start | bytes 344072 | tf_op jit(solution)/shard_map/ppermute | solution.py:16
  177.5 11.0 %collective-permute-start.17 = (f32[16,1792]{1,0:T(8,128)S(1)}, f32[16,1792]{1,0:T(8,128)S(1)}, u32[]{:S(2)}, u32[]{:S(2)}) collective-permute-start(f32[16,1792]{1,0:T(8,128)S(1)} %slice.244), channel_id=1, source_target_pairs={{4,0},{0,4},{5,1},{1,5},{6,2},{2,6},{7,3},{3,7},{12,8},{8,12},{13,... | collective-permute-start | bytes 344072 | tf_op jit(solution)/shard_map/ppermute | solution.py:16

commit v8 on v7

--- a/solution.py
+++ b/solution.py
@@ -235,8 +235,8 @@
         return block.reshape(rows, width_part)
 
     def to_tokens(part):
-        other = passed_along(part[tokens_here:], "core", 1)
-        return (part[:tokens_here] + other).astype(jnp.bfloat16)
+        other = passed_along(part[tokens_here:].astype(jnp.bfloat16), "core", 1)
+        return (part[:tokens_here] + other.astype(jnp.float32)).astype(jnp.bfloat16)
 
     arriving = passed_along(fwd_act[0], "section", 1)
     top_count = fwd_routes.shape[2]

time: 190 us -> 190 us (level)
  no operation moved by 1% of the time
where the time goes in v8:
time: 190 us; the launch traced here: 189 us
  starting transfers between devices  120 us (63%)
  waiting for transfers between devices  39.3 us (21%)
  Pallas kernels  15.2 us (8%)
  other arithmetic  6.09 us (3%)
  matrix products  3.57 us (2%)
  local copies, waits for them, and re-layouts  3.47 us (2%)
    ppermute x18, starting transfers between devices, passed_along(): return lax.ppermute(block, axis, route)  86.5 us
    all_to_all x4, starting transfers between devices, to_experts(): lax.all_to_all(block, 'chip', split_axis=0, concat_axis=0, tiled=True)  33.8 us
    ppermute x18, waiting for transfers between devices, passed_along(): return lax.ppermute(block, axis, route)  23.8 us
    all_to_all x4, waiting for transfers between devices, to_experts(): lax.all_to_all(block, 'chip', split_axis=0, concat_axis=0, tiled=True)  15.5 us
    pallas_call x4, Pallas kernels, streamed(): pl.pallas_call(kernel, out_shape=out_shape, in_specs=[pl.BlockSpec(memory...  15.2 us
  transfers between devices with their start and end apart: 22, of which 12 were waited for; matrix products, arithmetic and copies ran while one was open for 5% of the time, Pallas kernels for 8%

profile of v8, /device:TPU:1, one launch (start us, length us, event | category | flops | bytes accessed | tf_op | source)
XLA Modules:
  0.0 189.1 jit_solution(12723826388812026790)
XLA Ops:
  0.6 11.5 %collective-permute-start = (bf16[16,1792]{1,0:T(8,128)(2,1)}, bf16[16,1792]{1,0:T(8,128)(2,1)S(1)}, u32[]{:S(2)}, u32[]{:S(2)}) collective-permute-start(bf16[16,1792]{1,0:T(8,128)(2,1)} %bitcast.48), channel_id=1, source_target_pairs={{768,0},{0,256},{256,512},{512,768},{769,1},{1,257},{257,513},{513... | collective-permute-start | bytes 172040 | tf_op jit(solution)/shard_map/ppermute | solution.py:16
  12.1 0.7 reduce-precision_convert_fusion.3
  12.8 0.8 copy.39
  14.3 0.7 fusion.69
  15.0 0.7 reduce-precision_convert_fusion.2
  15.7 0.8 copy.43
  17.2 4.1 %collective-permute-done = bf16[16,1792]{1,0:T(8,128)(2,1)S(1)} collective-permute-done((bf16[16,1792]{1,0:T(8,128)(2,1)}, bf16[16,1792]{1,0:T(8,128)(2,1)S(1)}, u32[]{:S(2)}, u32[]{:S(2)}) %collective-permute-start) | collective-permute-done | bytes 57376 | tf_op jit(solution)/shard_map/ppermute | solution.py:16
  21.4 5.5 %collective-permute-start.1 = (bf16[16,1920]{1,0:T(8,128)(2,1)S(1)}, bf16[16,1920]{1,0:T(8,128)(2,1)S(1)}, u32[]{:S(2)}, u32[]{:S(2)}) collective-permute-start(bf16[16,1920]{1,0:T(8,128)(2,1)S(1)} %pad_maximum_fusion), channel_id=1, source_target_pairs={{4,0},{0,4},{5,1},{1,5},{6,2},{2,6},{7,3},{3,7},{12,8},{8,12},{13,... | collective-permute-start | bytes 184328 | tf_op jit(solution)/shard_map/ppermute | solution.py:16
  26.9 0.9 collective-permute-done.1
  28.2 1.5 convolution_convert_fusion
  29.7 7.6 %all-to-all-start = ((bf16[32,8,1792]{2,1,0:T(8,128)(2,1)}), bf16[32,8,1792]{2,1,0:T(8,128)(2,1)S(1)}, u32[]{:S(2)}, u32[]{:S(2)}) async-start(bf16[32,8,1792]{2,1,0:T(8,128)(2,1)} %bitcast.5), calls=%async_computation | async-start | bytes 1835008 | tf_op jit(solution)/shard_map/all_to_all | solution.py:234
  37.3 9.0 %collective-permute-start.7 = (bf16[16,1792]{1,0:T(8,128)(2,1)S(1)}, bf16[16,1792]{1,0:T(8,128)(2,1)S(1)}, u32[]{:S(2)}, u32[]{:S(2)}) collective-permute-start(bf16[16,1792]{1,0:T(8,128)(2,1)S(1)} %bitcast.49), channel_id=1, source_target_pairs={{256,0},{512,256},{768,512},{0,768},{257,1},{513,257},{769,513},{1... | collective-permute-start | bytes 172040 | tf_op jit(solution)/shard_map/ppermute | solution.py:16
  46.4 1.1 collective-permute-done.7
  47.5 3.4 %collective-permute-start.8 = (bf16[16,1920]{1,0:T(8,128)(2,1)S(1)}, bf16[16,1920]{1,0:T(8,128)(2,1)S(1)}, u32[]{:S(2)}, u32[]{:S(2)}) collective-permute-start(bf16[16,1920]{1,0:T(8,128)(2,1)S(1)} %pad_maximum_fusion.1), channel_id=1, source_target_pairs={{4,0},{0,4},{5,1},{1,5},{6,2},{2,6},{7,3},{3,7},{12,8},{8,12},{13,... | collective-permute-start | bytes 184328 | tf_op jit(solution)/shard_map/ppermute | solution.py:16
  50.9 1.0 fusion.7
  52.9 1.5 fusion
  54.4 5.1 %all-to-all-done = bf16[32,8,1792]{2,1,0:T(8,128)(2,1)S(1)} async-done(((bf16[32,8,1792]{2,1,0:T(8,128)(2,1)}), bf16[32,8,1792]{2,1,0:T(8,128)(2,1)S(1)}, u32[]{:S(2)}, u32[]{:S(2)}) %all-to-all-start) | async-done | bytes 917536 | tf_op jit(solution)/shard_map/all_to_all | solution.py:234
  59.5 8.2 %all-to-all-start.1 = ((bf16[32,8,1792]{2,1,0:T(8,128)(2,1)}), bf16[32,8,1792]{2,1,0:T(8,128)(2,1)S(1)}, u32[]{:S(2)}, u32[]{:S(2)}) async-start(bf16[32,8,1792]{2,1,0:T(8,128)(2,1)} %bitcast.12), calls=%async_computation.1 | async-start | bytes 1835008 | tf_op jit(solution)/shard_map/all_to_all | solution.py:234
  67.7 3.7 %shard_map.104 = (f32[256,256]{1,0:T(8,128)S(1)}, bf16[256,256]{1,0:T(8,128)(2,1)S(1)}, bf16[256,256]{1,0:T(8,128)(2,1)S(1)}, bf16[256,256]{1,0:T(8,128)(2,1)S(1)}) custom-call(s32[1]{0:T(128)} %bitcast.3.own, bf16[256,1792]{1,0:T(8,128)(2,1)S(1)} %bitcast.40, bf16[1792,1024]{1,0:T(8,128)(2,1)} %bitcast.44), custom_call_target="tpu_custom_call" | custom-call | tf_op jit(solution)/shard_map/pallas_call | solution.py:91
  71.4 8.1 %collective-permute-start.4 = (bf16[256,256]{1,0:T(8,128)(2,1)S(1)}, bf16[256,256]{1,0:T(8,128)(2,1)S(1)}, u32[]{:S(2)}, u32[]{:S(2)}) collective-permute-start(bf16[256,256]{1,0:T(8,128)(2,1)S(1)} %get-tuple-element.27), channel_id=1, source_target_pairs={{1,0},{2,1},{3,2},{0,3},{5,4},{6,5},{7,6},{4,7},{9,8},{10,9},{11,1... | collective-permute-start | bytes 393224 | tf_op jit(solution)/shard_map/ppermute | solution.py:16
  79.5 1.9 %collective-permute-start.3 = (bf16[256,256]{1,0:T(8,128)(2,1)S(1)}, bf16[256,256]{1,0:T(8,128)(2,1)S(1)}, u32[]{:S(2)}, u32[]{:S(2)}) collective-permute-start(bf16[256,256]{1,0:T(8,128)(2,1)S(1)} %get-tuple-element.26), channel_id=1, source_target_pairs={{2,0},{3,1},{0,2},{1,3},{6,4},{7,5},{4,6},{5,7},{10,8},{11,9},{8,1... | collective-permute-start | bytes 393224 | tf_op jit(solution)/shard_map/ppermute | solution.py:16
  81.5 2.2 %collective-permute-start.2 = (bf16[256,256]{1,0:T(8,128)(2,1)S(1)}, bf16[256,256]{1,0:T(8,128)(2,1)S(1)}, u32[]{:S(2)}, u32[]{:S(2)}) collective-permute-start(bf16[256,256]{1,0:T(8,128)(2,1)S(1)} %get-tuple-element.25), channel_id=1, source_target_pairs={{3,0},{0,1},{1,2},{2,3},{7,4},{4,5},{5,6},{6,7},{11,8},{8,9},{9,10... | collective-permute-start | bytes 393224 | tf_op jit(solution)/shard_map/ppermute | solution.py:16
  83.7 6.5 %collective-permute-done.3 = bf16[256,256]{1,0:T(8,128)(2,1)S(1)} collective-permute-done((bf16[256,256]{1,0:T(8,128)(2,1)S(1)}, bf16[256,256]{1,0:T(8,128)(2,1)S(1)}, u32[]{:S(2)}, u32[]{:S(2)}) %collective-permute-start.3) | collective-permute-done | bytes 131104 | tf_op jit(solution)/shard_map/ppermute | solution.py:16
  90.2 5.5 %collective-permute-start.6 = (bf16[256,256]{1,0:T(8,128)(2,1)S(1)}, bf16[256,256]{1,0:T(8,128)(2,1)S(1)}, u32[]{:S(2)}, u32[]{:S(2)}) collective-permute-start(bf16[256,256]{1,0:T(8,128)(2,1)S(1)} %multiply_convert_fusion.1.refs_0_), channel_id=1, source_target_pairs={{2,0},{3,1},{0,2},{1,3},{6,4},{7,5},{4,6},{5,7},{10,8},{11,9},{8,1... | collective-permute-start | bytes 393224 | tf_op jit(solution)/shard_map/ppermute | solution.py:16
  95.7 2.1 %collective-permute-start.5 = (bf16[256,256]{1,0:T(8,128)(2,1)S(1)}, bf16[256,256]{1,0:T(8,128)(2,1)S(1)}, u32[]{:S(2)}, u32[]{:S(2)}) collective-permute-start(bf16[256,256]{1,0:T(8,128)(2,1)S(1)} %multiply_convert_fusion.1.refs_0_), channel_id=1, source_target_pairs={{1,0},{2,1},{3,2},{0,3},{5,4},{6,5},{7,6},{4,7},{9,8},{10,9},{11,1... | collective-permute-start | bytes 393224 | tf_op jit(solution)/shard_map/ppermute | solution.py:16
  97.8 3.2 %collective-permute-start.9 = (bf16[256,256]{1,0:T(8,128)(2,1)S(1)}, bf16[256,256]{1,0:T(8,128)(2,1)S(1)}, u32[]{:S(2)}, u32[]{:S(2)}) collective-permute-start(bf16[256,256]{1,0:T(8,128)(2,1)S(1)} %multiply_convert_fusion.1.refs_0_), channel_id=1, source_target_pairs={{3,0},{0,1},{1,2},{2,3},{7,4},{4,5},{5,6},{6,7},{11,8},{8,9},{9,10... | collective-permute-start | bytes 393224 | tf_op jit(solution)/shard_map/ppermute | solution.py:16
  101.0 1.3 collective-permute-done.6.refs_2_
  102.4 3.8 %shard_map.106 = (f32[256,256]{1,0:T(8,128)S(1)}, bf16[256,256]{1,0:T(8,128)(2,1)S(1)}, bf16[256,256]{1,0:T(8,128)(2,1)S(1)}, bf16[256,256]{1,0:T(8,128)(2,1)S(1)}) custom-call(s32[1]{0:T(128)} %bitcast.3.own, bf16[256,1792]{1,0:T(8,128)(2,1)S(1)} %bitcast.41, bf16[1024,1792]{1,0:T(8,128)(2,1)} %bitcast.42), custom_call_target="tpu_custom_call" | custom-call | tf_op jit(solution)/shard_map/pallas_call | solution.py:91
  106.2 1.9 %collective-permute-start.10 = (bf16[256,256]{1,0:T(8,128)(2,1)S(1)}, bf16[256,256]{1,0:T(8,128)(2,1)S(1)}, u32[]{:S(2)}, u32[]{:S(2)}) collective-permute-start(bf16[256,256]{1,0:T(8,128)(2,1)S(1)} %get-tuple-element.33), channel_id=1, source_target_pairs={{3,0},{0,1},{1,2},{2,3},{7,4},{4,5},{5,6},{6,7},{11,8},{8,9},{9,10... | collective-permute-start | bytes 393224 | tf_op jit(solution)/shard_map/ppermute | solution.py:16
  108.1 2.8 %collective-permute-start.11 = (bf16[256,256]{1,0:T(8,128)(2,1)S(1)}, bf16[256,256]{1,0:T(8,128)(2,1)S(1)}, u32[]{:S(2)}, u32[]{:S(2)}) collective-permute-start(bf16[256,256]{1,0:T(8,128)(2,1)S(1)} %get-tuple-element.34), channel_id=1, source_target_pairs={{2,0},{3,1},{0,2},{1,3},{6,4},{7,5},{4,6},{5,7},{10,8},{11,9},{8,1... | collective-permute-start | bytes 393224 | tf_op jit(solution)/shard_map/ppermute | solution.py:16
  111.0 4.2 %collective-permute-start.12 = (bf16[256,256]{1,0:T(8,128)(2,1)S(1)}, bf16[256,256]{1,0:T(8,128)(2,1)S(1)}, u32[]{:S(2)}, u32[]{:S(2)}) collective-permute-start(bf16[256,256]{1,0:T(8,128)(2,1)S(1)} %get-tuple-element.35), channel_id=1, source_target_pairs={{1,0},{2,1},{3,2},{0,3},{5,4},{6,5},{7,6},{4,7},{9,8},{10,9},{11,1... | collective-permute-start | bytes 393224 | tf_op jit(solution)/shard_map/ppermute | solution.py:16
  115.2 3.8 %shard_map.105 = bf16[256,1792]{1,0:T(8,128)(2,1)} custom-call(s32[1]{0:T(128)} %bitcast.3.own, bf16[256,256]{1,0:T(8,128)(2,1)S(1)} %multiply_convert_fusion.1.refs_0_, bf16[256,256]{1,0:T(8,128)(2,1)S(1)} %collective-permute-done.5.refs_1_, bf16[256,256]{1,0:T(8,128)(2,1)S(1)} %collective-permute-done.6.refs_2_, ...), custom_call_target="tpu_custom_call" | custom-call | tf_op jit(solution)/shard_map/pallas_call | solution.py:91
  119.0 0.9 collective-permute-done.12
  120.0 9.0 %all-to-all-start.2 = ((bf16[32,8,1792]{2,1,0:T(8,128)(2,1)}), bf16[32,8,1792]{2,1,0:T(8,128)(2,1)S(1)}, u32[]{:S(2)}, u32[]{:S(2)}) async-start(bf16[32,8,1792]{2,1,0:T(8,128)(2,1)} %bitcast.15), calls=%async_computation.2 | async-start | bytes 1835008 | tf_op jit(solution)/shard_map/all_to_all | solution.py:234
  129.1 3.0 %collective-permute-start.14 = (bf16[256,256]{1,0:T(8,128)(2,1)S(1)}, bf16[256,256]{1,0:T(8,128)(2,1)S(1)}, u32[]{:S(2)}, u32[]{:S(2)}) collective-permute-start(bf16[256,256]{1,0:T(8,128)(2,1)S(1)} %multiply_convert_fusion.refs_0_), channel_id=1, source_target_pairs={{1,0},{2,1},{3,2},{0,3},{5,4},{6,5},{7,6},{4,7},{9,8},{10,9},{11,1... | collective-permute-start | bytes 393224 | tf_op jit(solution)/shard_map/ppermute | solution.py:16
  132.1 4.5 %collective-permute-start.15 = (bf16[256,256]{1,0:T(8,128)(2,1)S(1)}, bf16[256,256]{1,0:T(8,128)(2,1)S(1)}, u32[]{:S(2)}, u32[]{:S(2)}) collective-permute-start(bf16[256,256]{1,0:T(8,128)(2,1)S(1)} %multiply_convert_fusion.refs_0_), channel_id=1, source_target_pairs={{2,0},{3,1},{0,2},{1,3},{6,4},{7,5},{4,6},{5,7},{10,8},{11,9},{8,1... | collective-permute-start | bytes 393224 | tf_op jit(solution)/shard_map/ppermute | solution.py:16
  136.6 1.9 %collective-permute-start.16 = (bf16[256,256]{1,0:T(8,128)(2,1)S(1)}, bf16[256,256]{1,0:T(8,128)(2,1)S(1)}, u32[]{:S(2)}, u32[]{:S(2)}) collective-permute-start(bf16[256,256]{1,0:T(8,128)(2,1)S(1)} %multiply_convert_fusion.refs_0_), channel_id=1, source_target_pairs={{3,0},{0,1},{1,2},{2,3},{7,4},{4,5},{5,6},{6,7},{11,8},{8,9},{9,10... | collective-permute-start | bytes 393224 | tf_op jit(solution)/shard_map/ppermute | solution.py:16
  138.5 1.4 collective-permute-done.15.refs_2_
  139.9 5.8 %collective-permute-done.16.refs_3_ = bf16[256,256]{1,0:T(8,128)(2,1)S(1)} collective-permute-done((bf16[256,256]{1,0:T(8,128)(2,1)S(1)}, bf16[256,256]{1,0:T(8,128)(2,1)S(1)}, u32[]{:S(2)}, u32[]{:S(2)}) %collective-permute-start.16) | collective-permute-done | bytes 131104 | tf_op jit(solution)/shard_map/ppermute | solution.py:16
  145.7 3.9 %shard_map.107 = bf16[256,1792]{1,0:T(8,128)(2,1)} custom-call(s32[1]{0:T(128)} %bitcast.3.own, bf16[256,256]{1,0:T(8,128)(2,1)S(1)} %multiply_convert_fusion.refs_0_, bf16[256,256]{1,0:T(8,128)(2,1)S(1)} %collective-permute-done.14.refs_1_, bf16[256,256]{1,0:T(8,128)(2,1)S(1)} %collective-permute-done.15.refs_2_, ...), custom_call_target="tpu_custom_call" | custom-call | tf_op jit(solution)/shard_map/pallas_call | solution.py:91
  149.6 9.0 %all-to-all-start.3 = ((bf16[32,8,1792]{2,1,0:T(8,128)(2,1)}), bf16[32,8,1792]{2,1,0:T(8,128)(2,1)S(1)}, u32[]{:S(2)}, u32[]{:S(2)}) async-start(bf16[32,8,1792]{2,1,0:T(8,128)(2,1)} %bitcast.17), calls=%async_computation.3 | async-start | bytes 1835008 | tf_op jit(solution)/shard_map/all_to_all | solution.py:234
  159.6 5.7 %collective-permute-start.13 = (bf16[16,1792]{1,0:T(8,128)(2,1)S(1)}, bf16[16,1792]{1,0:T(8,128)(2,1)S(1)}, u32[]{:S(2)}, u32[]{:S(2)}) collective-permute-start(bf16[16,1792]{1,0:T(8,128)(2,1)S(1)} %slice.305), channel_id=1, source_target_pairs={{4,0},{0,4},{5,1},{1,5},{6,2},{2,6},{7,3},{3,7},{12,8},{8,12},{13,... | collective-permute-start | bytes 172040 | tf_op jit(solution)/shard_map/ppermute | solution.py:16
  165.2 0.9 collective-permute-done.13
  166.1 0.6 fusion.9
  166.7 10.4 %all-to-all-done.3 = bf16[32,8,1792]{2,1,0:T(8,128)(2,1)S(1)} async-done(((bf16[32,8,1792]{2,1,0:T(8,128)(2,1)}), bf16[32,8,1792]{2,1,0:T(8,128)(2,1)S(1)}, u32[]{:S(2)}, u32[]{:S(2)}) %all-to-all-start.3) | async-done | bytes 917536 | tf_op jit(solution)/shard_map/all_to_all | solution.py:234
  177.5 10.1 %collective-permute-start.17 = (bf16[16,1792]{1,0:T(8,128)(2,1)S(1)}, bf16[16,1792]{1,0:T(8,128)(2,1)S(1)}, u32[]{:S(2)}, u32[]{:S(2)}) collective-permute-start(bf16[16,1792]{1,0:T(8,128)(2,1)S(1)} %slice.304), channel_id=1, source_target_pairs={{4,0},{0,4},{5,1},{1,5},{6,2},{2,6},{7,3},{3,7},{12,8},{8,12},{13,... | collective-permute-start | bytes 172040 | tf_op jit(solution)/shard_map/ppermute | solution.py:16
  187.6 0.9 collective-permute-done.17
  188.4 0.6 fusion.18
  (59 shorter events, 4.3 us)
Async XLA Ops:
  0.6 20.7 %collective-permute-start = (bf16[16,1792]{1,0:T(8,128)(2,1)}, bf16[16,1792]{1,0:T(8,128)(2,1)S(1)}, u32[]{:S(2)}, u32[]{:S(2)}) collective-permute-start(bf16[16,1792]{1,0:T(8,128)(2,1)} %bitcast.48), channel_id=1, source_target_pairs={{768,0},{0,256},{256,512},{512,768},{769,1},{1,257},{257,513},{513... | collective-permute-start | bytes 172040 | tf_op jit(solution)/shard_map/ppermute | solution.py:16
  16.4 20.8 %copy-start = (s32[1,16,8]{1,2,0:T(8,128)S(1)}, s32[1,16,8]{1,2,0:T(8,128)}, u32[]{:S(2)}) copy-start(s32[1,16,8]{1,2,0:T(8,128)} %param.13) | copy-start | bytes 1540
  16.5 20.8 %copy-start.1 = (bf16[1,16,1792]{2,1,0:T(8,128)(2,1)S(1)}, bf16[1,16,1792]{2,1,0:T(8,128)(2,1)}, u32[]{:S(2)}) copy-start(bf16[1,16,1792]{2,1,0:T(8,128)(2,1)} %param.12) | copy-start | bytes 172036
  21.4 6.4 %collective-permute-start.1 = (bf16[16,1920]{1,0:T(8,128)(2,1)S(1)}, bf16[16,1920]{1,0:T(8,128)(2,1)S(1)}, u32[]{:S(2)}, u32[]{:S(2)}) collective-permute-start(bf16[16,1920]{1,0:T(8,128)(2,1)S(1)} %pad_maximum_fusion), channel_id=1, source_target_pairs={{4,0},{0,4},{5,1},{1,5},{6,2},{2,6},{7,3},{3,7},{12,8},{8,12},{13,... | collective-permute-start | bytes 184328 | tf_op jit(solution)/shard_map/ppermute | solution.py:16
  29.7 29.8 %all-to-all-start = ((bf16[32,8,1792]{2,1,0:T(8,128)(2,1)}), bf16[32,8,1792]{2,1,0:T(8,128)(2,1)S(1)}, u32[]{:S(2)}, u32[]{:S(2)}) async-start(bf16[32,8,1792]{2,1,0:T(8,128)(2,1)} %bitcast.5), calls=%async_computation | async-start | bytes 1835008 | tf_op jit(solution)/shard_map/all_to_all | solution.py:234
  37.3 10.2 %collective-permute-start.7 = (bf16[16,1792]{1,0:T(8,128)(2,1)S(1)}, bf16[16,1792]{1,0:T(8,128)(2,1)S(1)}, u32[]{:S(2)}, u32[]{:S(2)}) collective-permute-start(bf16[16,1792]{1,0:T(8,128)(2,1)S(1)} %bitcast.49), channel_id=1, source_target_pairs={{256,0},{512,256},{768,512},{0,768},{257,1},{513,257},{769,513},{1... | collective-permute-start | bytes 172040 | tf_op jit(solution)/shard_map/ppermute | solution.py:16
  47.5 4.4 %collective-permute-start.8 = (bf16[16,1920]{1,0:T(8,128)(2,1)S(1)}, bf16[16,1920]{1,0:T(8,128)(2,1)S(1)}, u32[]{:S(2)}, u32[]{:S(2)}) collective-permute-start(bf16[16,1920]{1,0:T(8,128)(2,1)S(1)} %pad_maximum_fusion.1), channel_id=1, source_target_pairs={{4,0},{0,4},{5,1},{1,5},{6,2},{2,6},{7,3},{3,7},{12,8},{8,12},{13,... | collective-permute-start | bytes 184328 | tf_op jit(solution)/shard_map/ppermute | solution.py:16
  59.5 41.5 %all-to-all-start.1 = ((bf16[32,8,1792]{2,1,0:T(8,128)(2,1)}), bf16[32,8,1792]{2,1,0:T(8,128)(2,1)S(1)}, u32[]{:S(2)}, u32[]{:S(2)}) async-start(bf16[32,8,1792]{2,1,0:T(8,128)(2,1)} %bitcast.12), calls=%async_computation.1 | async-start | bytes 1835008 | tf_op jit(solution)/shard_map/all_to_all | solution.py:234
  71.4 12.3 %collective-permute-start.4 = (bf16[256,256]{1,0:T(8,128)(2,1)S(1)}, bf16[256,256]{1,0:T(8,128)(2,1)S(1)}, u32[]{:S(2)}, u32[]{:S(2)}) collective-permute-start(bf16[256,256]{1,0:T(8,128)(2,1)S(1)} %get-tuple-element.27), channel_id=1, source_target_pairs={{1,0},{2,1},{3,2},{0,3},{5,4},{6,5},{7,6},{4,7},{9,8},{10,9},{11,1... | collective-permute-start | bytes 393224 | tf_op jit(solution)/shard_map/ppermute | solution.py:16
  79.5 10.6 %collective-permute-start.3 = (bf16[256,256]{1,0:T(8,128)(2,1)S(1)}, bf16[256,256]{1,0:T(8,128)(2,1)S(1)}, u32[]{:S(2)}, u32[]{:S(2)}) collective-permute-start(bf16[256,256]{1,0:T(8,128)(2,1)S(1)} %get-tuple-element.26), channel_id=1, source_target_pairs={{2,0},{3,1},{0,2},{1,3},{6,4},{7,5},{4,6},{5,7},{10,8},{11,9},{8,1... | collective-permute-start | bytes 393224 | tf_op jit(solution)/shard_map/ppermute | solution.py:16
  81.5 8.7 %collective-permute-start.2 = (bf16[256,256]{1,0:T(8,128)(2,1)S(1)}, bf16[256,256]{1,0:T(8,128)(2,1)S(1)}, u32[]{:S(2)}, u32[]{:S(2)}) collective-permute-start(bf16[256,256]{1,0:T(8,128)(2,1)S(1)} %get-tuple-element.25), channel_id=1, source_target_pairs={{3,0},{0,1},{1,2},{2,3},{7,4},{4,5},{5,6},{6,7},{11,8},{8,9},{9,10... | collective-permute-start | bytes 393224 | tf_op jit(solution)/shard_map/ppermute | solution.py:16
  90.2 12.1 %collective-permute-start.6 = (bf16[256,256]{1,0:T(8,128)(2,1)S(1)}, bf16[256,256]{1,0:T(8,128)(2,1)S(1)}, u32[]{:S(2)}, u32[]{:S(2)}) collective-permute-start(bf16[256,256]{1,0:T(8,128)(2,1)S(1)} %multiply_convert_fusion.1.refs_0_), channel_id=1, source_target_pairs={{2,0},{3,1},{0,2},{1,3},{6,4},{7,5},{4,6},{5,7},{10,8},{11,9},{8,1... | collective-permute-start | bytes 393224 | tf_op jit(solution)/shard_map/ppermute | solution.py:16
  95.7 19.5 %collective-permute-start.5 = (bf16[256,256]{1,0:T(8,128)(2,1)S(1)}, bf16[256,256]{1,0:T(8,128)(2,1)S(1)}, u32[]{:S(2)}, u32[]{:S(2)}) collective-permute-start(bf16[256,256]{1,0:T(8,128)(2,1)S(1)} %multiply_convert_fusion.1.refs_0_), channel_id=1, source_target_pairs={{1,0},{2,1},{3,2},{0,3},{5,4},{6,5},{7,6},{4,7},{9,8},{10,9},{11,1... | collective-permute-start | bytes 393224 | tf_op jit(solution)/shard_map/ppermute | solution.py:16
  97.8 17.4 %collective-permute-start.9 = (bf16[256,256]{1,0:T(8,128)(2,1)S(1)}, bf16[256,256]{1,0:T(8,128)(2,1)S(1)}, u32[]{:S(2)}, u32[]{:S(2)}) collective-permute-start(bf16[256,256]{1,0:T(8,128)(2,1)S(1)} %multiply_convert_fusion.1.refs_0_), channel_id=1, source_target_pairs={{3,0},{0,1},{1,2},{2,3},{7,4},{4,5},{5,6},{6,7},{11,8},{8,9},{9,10... | collective-permute-start | bytes 393224 | tf_op jit(solution)/shard_map/ppermute | solution.py:16
  106.2 12.8 %collective-permute-start.10 = (bf16[256,256]{1,0:T(8,128)(2,1)S(1)}, bf16[256,256]{1,0:T(8,128)(2,1)S(1)}, u32[]{:S(2)}, u32[]{:S(2)}) collective-permute-start(bf16[256,256]{1,0:T(8,128)(2,1)S(1)} %get-tuple-element.33), channel_id=1, source_target_pairs={{3,0},{0,1},{1,2},{2,3},{7,4},{4,5},{5,6},{6,7},{11,8},{8,9},{9,10... | collective-permute-start | bytes 393224 | tf_op jit(solution)/shard_map/ppermute | solution.py:16
  108.1 10.9 %collective-permute-start.11 = (bf16[256,256]{1,0:T(8,128)(2,1)S(1)}, bf16[256,256]{1,0:T(8,128)(2,1)S(1)}, u32[]{:S(2)}, u32[]{:S(2)}) collective-permute-start(bf16[256,256]{1,0:T(8,128)(2,1)S(1)} %get-tuple-element.34), channel_id=1, source_target_pairs={{2,0},{3,1},{0,2},{1,3},{6,4},{7,5},{4,6},{5,7},{10,8},{11,9},{8,1... | collective-permute-start | bytes 393224 | tf_op jit(solution)/shard_map/ppermute | solution.py:16
  111.0 9.0 %collective-permute-start.12 = (bf16[256,256]{1,0:T(8,128)(2,1)S(1)}, bf16[256,256]{1,0:T(8,128)(2,1)S(1)}, u32[]{:S(2)}, u32[]{:S(2)}) collective-permute-start(bf16[256,256]{1,0:T(8,128)(2,1)S(1)} %get-tuple-element.35), channel_id=1, source_target_pairs={{1,0},{2,1},{3,2},{0,3},{5,4},{6,5},{7,6},{4,7},{9,8},{10,9},{11,1... | collective-permute-start | bytes 393224 | tf_op jit(solution)/shard_map/ppermute | solution.py:16
  120.0 29.7 %all-to-all-start.2 = ((bf16[32,8,1792]{2,1,0:T(8,128)(2,1)}), bf16[32,8,1792]{2,1,0:T(8,128)(2,1)S(1)}, u32[]{:S(2)}, u32[]{:S(2)}) async-start(bf16[32,8,1792]{2,1,0:T(8,128)(2,1)} %bitcast.15), calls=%async_computation.2 | async-start | bytes 1835008 | tf_op jit(solution)/shard_map/all_to_all | solution.py:234
  129.1 9.4 %collective-permute-start.14 = (bf16[256,256]{1,0:T(8,128)(2,1)S(1)}, bf16[256,256]{1,0:T(8,128)(2,1)S(1)}, u32[]{:S(2)}, u32[]{:S(2)}) collective-permute-start(bf16[256,256]{1,0:T(8,128)(2,1)S(1)} %multiply_convert_fusion.refs_0_), channel_id=1, source_target_pairs={{1,0},{2,1},{3,2},{0,3},{5,4},{6,5},{7,6},{4,7},{9,8},{10,9},{11,1... | collective-permute-start | bytes 393224 | tf_op jit(solution)/shard_map/ppermute | solution.py:16
  132.1 7.9 %collective-permute-start.15 = (bf16[256,256]{1,0:T(8,128)(2,1)S(1)}, bf16[256,256]{1,0:T(8,128)(2,1)S(1)}, u32[]{:S(2)}, u32[]{:S(2)}) collective-permute-start(bf16[256,256]{1,0:T(8,128)(2,1)S(1)} %multiply_convert_fusion.refs_0_), channel_id=1, source_target_pairs={{2,0},{3,1},{0,2},{1,3},{6,4},{7,5},{4,6},{5,7},{10,8},{11,9},{8,1... | collective-permute-start | bytes 393224 | tf_op jit(solution)/shard_map/ppermute | solution.py:16
  136.6 9.1 %collective-permute-start.16 = (bf16[256,256]{1,0:T(8,128)(2,1)S(1)}, bf16[256,256]{1,0:T(8,128)(2,1)S(1)}, u32[]{:S(2)}, u32[]{:S(2)}) collective-permute-start(bf16[256,256]{1,0:T(8,128)(2,1)S(1)} %multiply_convert_fusion.refs_0_), channel_id=1, source_target_pairs={{3,0},{0,1},{1,2},{2,3},{7,4},{4,5},{5,6},{6,7},{11,8},{8,9},{9,10... | collective-permute-start | bytes 393224 | tf_op jit(solution)/shard_map/ppermute | solution.py:16
  149.6 27.5 %all-to-all-start.3 = ((bf16[32,8,1792]{2,1,0:T(8,128)(2,1)}), bf16[32,8,1792]{2,1,0:T(8,128)(2,1)S(1)}, u32[]{:S(2)}, u32[]{:S(2)}) async-start(bf16[32,8,1792]{2,1,0:T(8,128)(2,1)} %bitcast.17), calls=%async_computation.3 | async-start | bytes 1835008 | tf_op jit(solution)/shard_map/all_to_all | solution.py:234
  159.6 6.5 %collective-permute-start.13 = (bf16[16,1792]{1,0:T(8,128)(2,1)S(1)}, bf16[16,1792]{1,0:T(8,128)(2,1)S(1)}, u32[]{:S(2)}, u32[]{:S(2)}) collective-permute-start(bf16[16,1792]{1,0:T(8,128)(2,1)S(1)} %slice.305), channel_id=1, source_target_pairs={{4,0},{0,4},{5,1},{1,5},{6,2},{2,6},{7,3},{3,7},{12,8},{8,12},{13,... | collective-permute-start | bytes 172040 | tf_op jit(solution)/shard_map/ppermute | solution.py:16
  177.5 10.9 %collective-permute-start.17 = (bf16[16,1792]{1,0:T(8,128)(2,1)S(1)}, bf16[16,1792]{1,0:T(8,128)(2,1)S(1)}, u32[]{:S(2)}, u32[]{:S(2)}) collective-permute-start(bf16[16,1792]{1,0:T(8,128)(2,1)S(1)} %slice.304), channel_id=1, source_target_pairs={{4,0},{0,4},{5,1},{1,5},{6,2},{2,6},{7,3},{3,7},{12,8},{8,12},{13,... | collective-permute-start | bytes 172040 | tf_op jit(solution)/shard_map/ppermute | solution.py:16
